TPU v7x, 1024 devices: a whole 4x4x32 slice. The times are simulated.
1024 devices in a mesh: section: 32 (over y, z_lo), fsdp: 32 (over z_hi, x, core).
Axes of the slice: x: 4, y: 4, z: 32 (z_hi: 4, z_lo: 8; z = z_hi * 8 + z_lo), core: 2. Of those that a mesh axis runs over, the one named last changes fastest.
Arguments:
- tokens: bfloat16 [256, 8192], P('section', 'fsdp'), may hold values from -6 to 6
- gate_weight: bfloat16 [8192, 28672], P('fsdp', 'section'), may hold values from -0.0625 to 0.0625
- up_weight: bfloat16 [8192, 28672], P('fsdp', 'section'), may hold values from -0.0625 to 0.0625
- down_weight: bfloat16 [28672, 8192], P('section', 'fsdp'), may hold values from -0.03125 to 0.03125
- out_grad: bfloat16 [256, 8192], P('section', 'fsdp'), may hold values from -6 to 6
Outputs:
- output: bfloat16 [256, 8192], P('section', 'fsdp')
- token_grads: bfloat16 [256, 8192], P('section', 'fsdp')
- gate_grads: bfloat16 [8192, 28672], P('fsdp', 'section')
- up_grads: bfloat16 [8192, 28672], P('fsdp', 'section')
- down_grads: bfloat16 [28672, 8192], P('section', 'fsdp')
All inputs are finite; a program needn't handle non-finite values.
Results may differ from a plain program's by a relative error of at most 0.0065.
Values may be sent and summed in bfloat16 or wider, within the bound.
No kernel may reach another device: no remote copies, remote signals or barrier semaphores. Data moves between devices by JAX's collectives and lax.ppermute only.
A program may use at most 32 MiB of HBM per device.

v0:
```python
import jax
import jax.numpy as jnp
from jax import lax
from jax.sharding import PartitionSpec as P


def contract_last(left, right):
    return lax.dot_general(
        left, right, (((1,), (1,)), ((), ())), preferred_element_type=jnp.float32
    )


def contract_first(left, right):
    return lax.dot_general(
        left, right, (((0,), (0,)), ((), ())), preferred_element_type=jnp.float32
    )


def shards(tokens, gate_weight, up_weight, down_weight, out_grad):
    model_width = tokens.shape[1]
    whole_tokens, whole_grad = (
        lax.all_gather(tokens, "section", axis=0, tiled=True),
        lax.all_gather(out_grad, "section", axis=0, tiled=True),
    )
    total_rows = whole_tokens.shape[0]
    share_rows = total_rows // lax.axis_size("fsdp")
    share_start = lax.axis_index("fsdp") * share_rows
    gate_part = jnp.dot(whole_tokens, gate_weight, preferred_element_type=jnp.float32)
    up_part = jnp.dot(whole_tokens, up_weight, preferred_element_type=jnp.float32)
    gate_sum, up_sum = lax.psum((gate_part, up_part), "fsdp")
    gate_sigmoid = jax.nn.sigmoid(gate_sum)
    hidden = (gate_sum * gate_sigmoid * up_sum).astype(jnp.bfloat16)
    gate_share = lax.dynamic_slice_in_dim(gate_sum, share_start, share_rows, 0)
    up_share = lax.dynamic_slice_in_dim(up_sum, share_start, share_rows, 0)
    sigmoid_share = lax.dynamic_slice_in_dim(gate_sigmoid, share_start, share_rows, 0)
    hidden_delta = lax.psum_scatter(
        contract_last(whole_grad, down_weight), "fsdp", scatter_dimension=0, tiled=True
    )
    gate_delta = (
        hidden_delta * up_share * sigmoid_share * (1.0 + gate_share * (1.0 - sigmoid_share))
    ).astype(jnp.bfloat16)
    up_delta = (hidden_delta * gate_share * sigmoid_share).astype(jnp.bfloat16)
    gate_delta, up_delta = (
        lax.all_gather(gate_delta, "fsdp", axis=0, tiled=True),
        lax.all_gather(up_delta, "fsdp", axis=0, tiled=True),
    )
    forward_part = jnp.dot(hidden, down_weight, preferred_element_type=jnp.float32)
    backward_part = contract_last(gate_delta, gate_weight) + contract_last(up_delta, up_weight)
    section_summed = lax.psum_scatter(
        jnp.concatenate([forward_part, backward_part], axis=1),
        "section",
        scatter_dimension=0,
        tiled=True,
    )
    output = section_summed[:, :model_width].astype(jnp.bfloat16)
    token_grads = section_summed[:, model_width:].astype(jnp.bfloat16)
    gate_grads = contract_first(whole_tokens, gate_delta).astype(jnp.bfloat16)
    up_grads = contract_first(whole_tokens, up_delta).astype(jnp.bfloat16)
    down_grads = contract_first(hidden, whole_grad).astype(jnp.bfloat16)
    return (output, token_grads, gate_grads, up_grads, down_grads)


def solution(mesh):
    return jax.shard_map(
        shards,
        mesh=mesh,
        in_specs=(
            P("section", "fsdp"),
            P("fsdp", "section"),
            P("fsdp", "section"),
            P("section", "fsdp"),
            P("section", "fsdp"),
        ),
        out_specs=(
            P("section", "fsdp"),
            P("section", "fsdp"),
            P("fsdp", "section"),
            P("fsdp", "section"),
            P("section", "fsdp"),
        ),
        check_vma=False,
    )
```

profile of v0, /device:TPU:2, one launch (start us, length us, event | category | flops | bytes accessed | tf_op | source)
XLA Modules:
  0.0 1194.9 jit_solution(12327404444918882378)
XLA Ops:
  7.2 0.0 copy-start
  7.2 0.0 all-reduce.4.cloned.1.call-start
  7.2 126.3 %all_gather.12 = bf16[256,256]{1,0:T(8,128)(2,1)S(1)} all-gather(bf16[8,256]{1,0:T(8,128)(2,1)} %param.5), channel_id=1, replica_groups=mesh['section'=32,'fsdp'=32] {'section'}, dimensions={0}, use_global_device_ids=true | all-gather | bytes 135168 | tf_op jit(solution)/shard_map/all_gather | solution.py:22
  133.5 0.0 copy-done
  133.5 1.3 fusion.3
  134.8 0.0 copy-done.2
  134.8 1.2 fusion.4
  136.0 112.2 %all_gather.13 = bf16[256,256]{1,0:T(8,128)(2,1)S(1)} all-gather(bf16[8,256]{1,0:T(8,128)(2,1)S(1)} %copy-done.3), channel_id=1, replica_groups=mesh['section'=32,'fsdp'=32] {'section'}, dimensions={0}, use_global_device_ids=true | all-gather | bytes 135168 | tf_op jit(solution)/shard_map/all_gather | solution.py:23
  248.2 0.0 copy-done.1
  248.2 1.3 fusion.6
  249.5 0.0 all-reduce.4.cloned.1.call-update
  249.5 0.0 reduce-scatter.4.cloned.1.call-start
  249.6 1.3 dynamic-slice
  251.5 532.0 %all-reduce.4.cloned.1.call-done = (f32[256,896]{1,0:T(8,128)}, f32[256,896]{1,0:T(8,128)}, f32[256,896]{1,0:T(8,128)}) async-done(((f32[256,896]{1,0:T(8,128)}, f32[256,896]{1,0:T(8,128)}, f32[256,896]{1,0:T(8,128)}), (f32[256,896]{1,0:T(8,128)}, f32[256,896]{1,0:T(8,128)}, f32[256,896]{1,0:T(8,128)})) %all-reduce.4.cloned.1.call-update) | async-done | bytes 2752528 | tf_op jit(solution)/shard_map/psum | solution.py:30
  783.5 1.7 multiply_convert_fusion
  785.2 0.8 multiply_convert_fusion.1
  786.0 81.3 %all_gather.14 = bf16[256,896]{1,0:T(8,128)(2,1)S(1)} all-gather(bf16[8,896]{1,0:T(8,128)(2,1)S(1)} %get-tuple-element.19), channel_id=1, replica_groups=mesh['section'=32,'fsdp'=32] {'fsdp'}, dimensions={0}, use_global_device_ids=true | all-gather | bytes 473088 | tf_op jit(solution)/shard_map/all_gather | solution.py:44
  867.4 0.3 fusion.7
  867.7 68.2 %all_gather.15 = bf16[256,896]{1,0:T(8,128)(2,1)S(1)} all-gather(bf16[8,896]{1,0:T(8,128)(2,1)S(1)} %get-tuple-element.18), channel_id=1, replica_groups=mesh['section'=32,'fsdp'=32] {'fsdp'}, dimensions={0}, use_global_device_ids=true | all-gather | bytes 473088 | tf_op jit(solution)/shard_map/all_gather | solution.py:45
  935.9 0.3 fusion.5
  936.2 0.3 convolution_add_fusion
  936.6 1.0 copy.18
  937.6 0.0 reduce-scatter.4.cloned.1.call-update
  937.7 0.3 fusion
  938.0 1.0 copy.16
  939.0 0.3 fusion.1
  939.3 1.0 copy.17
  940.3 1.1 convolution_convert_fusion
  941.4 244.4 %reduce-scatter.4.cloned.1.call-done = f32[8,512]{1,0:T(8,128)} async-done(((f32[256,512]{1,0:T(8,128)}), f32[8,512]{1,0:T(8,128)}) %reduce-scatter.4.cloned.1.call-update) | async-done | bytes 16400
  1185.8 0.9 copy.19
  1186.7 0.7 copy.14
  1187.4 0.7 copy.15
  (6 shorter events, 0.1 us)
Async XLA Ops:
  7.2 126.3 %copy-start = (bf16[256,896]{1,0:T(8,128)(2,1)S(1)}, bf16[256,896]{1,0:T(8,128)(2,1)}, u32[]{:S(2)}) copy-start(bf16[256,896]{1,0:T(8,128)(2,1)} %param.6) | copy-start | bytes 1376260
  7.2 776.3 %all-reduce.4.cloned.1.call-start = ((), (), s32[]{:S(2)}) async-start(), calls=%async_computation.2 | async-start | bytes 5505024 | tf_op jit(solution)/shard_map/psum | solution.py:30
  133.5 1.3 copy-start.2
  134.8 1.2 copy-start.3
  134.8 113.5 %copy-start.1 = (bf16[896,256]{1,0:T(8,128)(2,1)S(1)}, bf16[896,256]{1,0:T(8,128)(2,1)}, u32[]{:S(2)}) copy-start(bf16[896,256]{1,0:T(8,128)(2,1)} %param.8) | copy-start | bytes 1376260
  249.5 936.3 %reduce-scatter.4.cloned.1.call-start = ((), (), s32[]{:S(2)}) async-start(), calls=%async_computation.1 | async-start | bytes 540672
Sparse Core Ops, SparseCore 0:
  249.6 533.7 all-reduce.3
  937.8 248.0 reduce-scatter.3
where the time goes:
time: 1200 us; the launch traced here: 1190 us
  waiting for transfers between devices  776 us (65%)
  blocking collectives  388 us (32%)
  between operations  14.8 us (1%)
    psum x1, waiting for transfers between devices, shards(): gate_sum, up_sum = lax.psum((gate_part, up_part), 'fsdp')  532 us
    unnamed x3, waiting for transfers between devices  244 us
    all_gather x1, blocking collectives, shards(): lax.all_gather(tokens, 'section', axis=0, tiled=True)  126 us
    all_gather x1, blocking collectives, shards(): lax.all_gather(out_grad, 'section', axis=0, tiled=True)  112 us
    all_gather x1, blocking collectives, shards(): lax.all_gather(gate_delta, 'fsdp', axis=0, tiled=True)  81.3 us
    all_gather x1, blocking collectives, shards(): lax.all_gather(up_delta, 'fsdp', axis=0, tiled=True)  68.2 us
  transfers between devices with their start and end apart: 2, of which 2 were waited for; matrix products, arithmetic and copies ran while one was open for 0% of the time, Pallas kernels for 0%

commit v1 on v0

v1 whole, which is shorter than its diff:
```python
import jax
import jax.numpy as jnp
from jax import lax
from jax.sharding import Mesh, PartitionSpec as P

SECTION = ("y", "zl")
FSDP = ("zh", "x", "core")
BF16 = jnp.bfloat16
F32 = jnp.float32


def contract_last(left, right):
    return lax.dot_general(
        left, right, (((1,), (1,)), ((), ())), preferred_element_type=F32
    )


def contract_first(left, right):
    return lax.dot_general(
        left, right, (((0,), (0,)), ((), ())), preferred_element_type=F32
    )


def swap_core(block):
    return lax.ppermute(block, "core", [(0, 1), (1, 0)])


def sum_over(block, axis):
    ways = lax.axis_size(axis)
    rows, columns = block.shape
    pieces = block.astype(BF16).reshape(ways, rows // ways, columns)
    return lax.all_to_all(pieces, axis, 0, 0).astype(F32).sum(0)


def shards(tokens, gate_weight, up_weight, down_weight, out_grad):
    own, width = tokens.shape
    sections = lax.axis_size(SECTION)
    rows = own * sections
    half = rows // 2
    both = jnp.broadcast_to(
        jnp.stack([tokens, out_grad])[None], (sections, 2, own, width)
    )
    both = lax.all_to_all(both, SECTION, 0, 0)
    both = jnp.swapaxes(both, 0, 1).reshape(2, rows, width)
    shift = lax.axis_index("core") * half
    both = jnp.roll(both, shift, axis=1)
    all_tokens, all_grads = both[0], both[1]
    part = jnp.concatenate(
        [
            jnp.dot(all_tokens, gate_weight, preferred_element_type=F32),
            jnp.dot(all_tokens, up_weight, preferred_element_type=F32),
            contract_last(all_grads, down_weight),
        ],
        axis=1,
    )
    units = gate_weight.shape[1]
    part = part[:half] + swap_core(part[half:].astype(BF16)).astype(F32)
    part = sum_over(part, "x")
    part = sum_over(part, "zh")
    gate_sum, up_sum, hidden_delta = (
        part[:, :units],
        part[:, units : 2 * units],
        part[:, 2 * units :],
    )
    gate_sigmoid = jax.nn.sigmoid(gate_sum)
    hidden = (gate_sum * gate_sigmoid * up_sum).astype(BF16)
    gate_delta = (
        hidden_delta * up_sum * gate_sigmoid * (1.0 + gate_sum * (1.0 - gate_sigmoid))
    ).astype(BF16)
    up_delta = (hidden_delta * gate_sum * gate_sigmoid).astype(BF16)
    whole = jnp.concatenate([hidden, gate_delta, up_delta], axis=1)
    whole = lax.all_gather(whole, "zh", axis=0, tiled=True)
    whole = lax.all_gather(whole, "x", axis=0, tiled=True)
    whole = jnp.concatenate([whole, swap_core(whole)], axis=0)
    hidden, gate_delta, up_delta = (
        whole[:, :units],
        whole[:, units : 2 * units],
        whole[:, 2 * units :],
    )
    forward_part = jnp.dot(hidden, down_weight, preferred_element_type=F32)
    backward_part = contract_last(gate_delta, gate_weight) + contract_last(
        up_delta, up_weight
    )
    ends = jnp.stack([forward_part, backward_part]).astype(BF16)
    ends = jnp.roll(ends, shift, axis=1)
    ends = jnp.swapaxes(ends.reshape(2, sections, own, width), 0, 1)
    ends = lax.all_to_all(ends, SECTION, 0, 0).astype(F32).sum(0).astype(BF16)
    gate_grads = contract_first(all_tokens, gate_delta).astype(BF16)
    up_grads = contract_first(all_tokens, up_delta).astype(BF16)
    down_grads = contract_first(hidden, all_grads).astype(BF16)
    return (ends[0], ends[1], gate_grads, up_grads, down_grads)


def solution(mesh):
    fine = Mesh(
        mesh.devices.reshape(4, 8, 4, 4, 2), ("y", "zl", "zh", "x", "core")
    )
    return jax.shard_map(
        shards,
        mesh=fine,
        in_specs=(
            P(SECTION, FSDP),
            P(FSDP, SECTION),
            P(FSDP, SECTION),
            P(SECTION, FSDP),
            P(SECTION, FSDP),
        ),
        out_specs=(
            P(SECTION, FSDP),
            P(SECTION, FSDP),
            P(FSDP, SECTION),
            P(FSDP, SECTION),
            P(SECTION, FSDP),
        ),
        check_vma=False,
    )
```

time: 1200 us -> 188 us (0.16)
  the two profiles are of different devices: /device:TPU:2 before, /device:TPU:1 now
where the time goes in v1:
time: 188 us; the launch traced here: 187 us
  blocking collectives  97.1 us (52%)
  starting transfers between devices  42.2 us (22%)
  waiting for transfers between devices  37.5 us (20%)
  matrix products  5.18 us (3%)
  local copies, waits for them, and re-layouts  2.27 us (1%)
  other arithmetic  1.96 us (1%)
    all_to_all x2, blocking collectives, sum_over(): return lax.all_to_all(pieces, axis, 0, 0).astype(F32).sum(0)  58.3 us
    all_gather x1, blocking collectives, shards(): whole = lax.all_gather(whole, 'zh', axis=0, tiled=True)  27.4 us
    all_to_all x1, waiting for transfers between devices, shards(): both = lax.all_to_all(both, SECTION, 0, 0)  18.6 us
    all_to_all x1, starting transfers between devices, shards(): both = lax.all_to_all(both, SECTION, 0, 0)  16.1 us
    all_to_all x1, waiting for transfers between devices, shards(): ends = lax.all_to_all(ends, SECTION, 0, 0).astype(F32).sum(0).astype(BF16)  15.5 us
    all_to_all x1, starting transfers between devices, shards(): ends = lax.all_to_all(ends, SECTION, 0, 0).astype(F32).sum(0).astype(BF16)  13.2 us
    ppermute x2, starting transfers between devices, swap_core(): return lax.ppermute(block, 'core', [(0, 1), (1, 0)])  12.9 us
    all_gather x1, blocking collectives, shards(): whole = lax.all_gather(whole, 'x', axis=0, tiled=True)  11.4 us
  transfers between devices with their start and end apart: 4, of which 4 were waited for; matrix products, arithmetic and copies ran while one was open for 2% of the time, Pallas kernels for 0%

profile of v1, /device:TPU:1, one launch (start us, length us, event | category | flops | bytes accessed | tf_op | source)
XLA Modules:
  0.0 187.1 jit_solution(99081960469987986)
XLA Ops:
  0.7 0.8 pad_maximum_fusion.2
  1.4 0.7 broadcast_in_dim.2
  2.2 16.1 %all-to-all-start = ((bf16[32,2,8,256]{3,2,1,0:T(8,128)(2,1)}), bf16[32,2,8,256]{3,2,1,0:T(8,128)(2,1)S(1)}, u32[]{:S(2)}, u32[]{:S(2)}) async-start(bf16[32,2,8,256]{3,2,1,0:T(8,128)(2,1)} %broadcast_in_dim.2), calls=%async_computation | async-start | bytes 524288 | tf_op jit(solution)/shard_map/all_to_all | solution.py:43
  18.3 18.6 %all-to-all-done = bf16[32,2,8,256]{3,2,1,0:T(8,128)(2,1)S(1)} async-done(((bf16[32,2,8,256]{3,2,1,0:T(8,128)(2,1)}), bf16[32,2,8,256]{3,2,1,0:T(8,128)(2,1)S(1)}, u32[]{:S(2)}, u32[]{:S(2)}) %all-to-all-start) | async-done | bytes 262176 | tf_op jit(solution)/shard_map/all_to_all | solution.py:43
  36.9 0.3 fusion.15
  37.2 0.3 fusion.17
  37.6 0.3 fusion.18
  37.9 0.3 fusion.16
  38.2 0.2 pad_maximum_fusion
  38.4 0.1 slice.94
  38.5 3.8 %collective-permute-start = (bf16[128,2688]{1,0:T(8,128)(2,1)S(1)}, bf16[128,2688]{1,0:T(8,128)(2,1)S(1)}, u32[]{:S(2)}, u32[]{:S(2)}) collective-permute-start(bf16[128,2688]{1,0:T(8,128)(2,1)S(1)} %slice.94), channel_id=1, source_target_pairs={{0,1},{1,0},{2,3},{3,2},{4,5},{5,4},{6,7},{7,6},{8,9},{9,8},{10,11... | collective-permute-start | bytes 2064392 | tf_op jit(solution)/shard_map/ppermute | solution.py:25
  42.3 1.7 collective-permute-done
  44.0 0.1 fusion
  44.1 14.5 %all_to_all.20 = bf16[4,32,2688]{2,1,0:T(8,128)(2,1)S(1)} all-to-all(bf16[4,32,2688]{2,1,0:T(8,128)(2,1)S(1)} %bitcast.37), channel_id=1, replica_groups=mesh['y'=4,'zl'=8,'zh'=4,'x'=4,'core'=2] {'x'}, dimensions={0} | all-to-all | bytes 1376256 | tf_op jit(solution)/shard_map/all_to_all | solution.py:32
  58.6 0.1 reduce_sum.33
  58.7 43.8 %all_to_all.21 = bf16[4,8,2688]{2,1,0:T(8,128)(2,1)S(1)} all-to-all(bf16[4,8,2688]{2,1,0:T(8,128)(2,1)S(1)} %bitcast.39), channel_id=1, replica_groups=mesh['y'=4,'zl'=8,'zh'=4,'x'=4,'core'=2] {'zh'}, dimensions={0} | all-to-all | bytes 344064 | tf_op jit(solution)/shard_map/all_to_all | solution.py:32
  102.7 27.4 %all_gather.6 = bf16[32,2688]{1,0:T(8,128)(2,1)S(1)} all-gather(bf16[8,2688]{1,0:T(8,128)(2,1)S(1)} %pad_maximum_fusion.1), channel_id=1, replica_groups=mesh['y'=4,'zl'=8,'zh'=4,'x'=4,'core'=2] {'zh'}, dimensions={0}, use_global_device_ids=true | all-gather | bytes 215040 | tf_op jit(solution)/shard_map/all_gather | solution.py:72
  130.1 11.4 %all_gather.7 = bf16[128,2688]{1,0:T(8,128)(2,1)S(1)} all-gather(bf16[32,2688]{1,0:T(8,128)(2,1)S(1)} %all_gather.6), channel_id=1, replica_groups=mesh['y'=4,'zl'=8,'zh'=4,'x'=4,'core'=2] {'x'}, dimensions={0}, use_global_device_ids=true | all-gather | bytes 860160 | tf_op jit(solution)/shard_map/all_gather | solution.py:73
  141.4 9.1 %collective-permute-start.1 = (bf16[128,2688]{1,0:T(8,128)(2,1)S(1)}, bf16[128,2688]{1,0:T(8,128)(2,1)S(1)}, u32[]{:S(2)}, u32[]{:S(2)}) collective-permute-start(bf16[128,2688]{1,0:T(8,128)(2,1)S(1)} %all_gather.7), channel_id=1, source_target_pairs={{0,1},{1,0},{2,3},{3,2},{4,5},{5,4},{6,7},{7,6},{8,9},{9,8},{10,11... | collective-permute-start | bytes 2064392 | tf_op jit(solution)/shard_map/ppermute | solution.py:25
  150.6 1.7 collective-permute-done.1
  152.3 0.1 constant_dynamic-update-slice_fusion
  152.4 0.3 fusion.2
  152.7 0.3 fusion.5
  153.0 0.3 fusion.3
  153.4 0.3 fusion.13
  153.7 0.7 copy.14
  154.4 13.2 %all-to-all-start.3 = ((bf16[32,2,8,256]{3,2,1,0:T(8,128)(2,1)}), bf16[32,2,8,256]{3,2,1,0:T(8,128)(2,1)S(1)}, u32[]{:S(2)}, u32[]{:S(2)}) async-start(bf16[32,2,8,256]{3,2,1,0:T(8,128)(2,1)} %copy.14), calls=%async_computation.3 | async-start | bytes 524288 | tf_op jit(solution)/shard_map/all_to_all | solution.py:87
  167.7 1.1 convolution_convert_fusion
  168.8 1.1 convolution_convert_fusion.2
  169.8 1.1 convolution_convert_fusion.1
  170.9 15.5 %all-to-all-done.3 = bf16[32,2,8,256]{3,2,1,0:T(8,128)(2,1)S(1)} async-done(((bf16[32,2,8,256]{3,2,1,0:T(8,128)(2,1)}), bf16[32,2,8,256]{3,2,1,0:T(8,128)(2,1)S(1)}, u32[]{:S(2)}, u32[]{:S(2)}) %all-to-all-start.3) | async-done | bytes 262176 | tf_op jit(solution)/shard_map/all_to_all | solution.py:87
  186.5 0.6 slice_bitcast_fusion.8
  (12 shorter events, 0.2 us)
Async XLA Ops:
  0.6 37.2 %copy-start = (bf16[896,256]{1,0:T(8,128)(2,1)S(1)}, bf16[896,256]{1,0:T(8,128)(2,1)}, u32[]{:S(2)}) copy-start(bf16[896,256]{1,0:T(8,128)(2,1)} %param.10) | copy-start | bytes 1376260
  0.6 36.6 %copy-start.2 = (bf16[256,896]{1,0:T(8,128)(2,1)S(1)}, bf16[256,896]{1,0:T(8,128)(2,1)}, u32[]{:S(2)}) copy-start(bf16[256,896]{1,0:T(8,128)(2,1)} %param.9) | copy-start | bytes 1376260
  2.2 34.7 %all-to-all-start = ((bf16[32,2,8,256]{3,2,1,0:T(8,128)(2,1)}), bf16[32,2,8,256]{3,2,1,0:T(8,128)(2,1)S(1)}, u32[]{:S(2)}, u32[]{:S(2)}) async-start(bf16[32,2,8,256]{3,2,1,0:T(8,128)(2,1)} %broadcast_in_dim.2), calls=%async_computation | async-start | bytes 524288 | tf_op jit(solution)/shard_map/all_to_all | solution.py:43
  18.3 19.3 %copy-start.1 = (bf16[256,896]{1,0:T(8,128)(2,1)S(1)}, bf16[256,896]{1,0:T(8,128)(2,1)}, u32[]{:S(2)}) copy-start(bf16[256,896]{1,0:T(8,128)(2,1)} %param.8) | copy-start | bytes 1376260
  38.5 5.5 %collective-permute-start = (bf16[128,2688]{1,0:T(8,128)(2,1)S(1)}, bf16[128,2688]{1,0:T(8,128)(2,1)S(1)}, u32[]{:S(2)}, u32[]{:S(2)}) collective-permute-start(bf16[128,2688]{1,0:T(8,128)(2,1)S(1)} %slice.94), channel_id=1, source_target_pairs={{0,1},{1,0},{2,3},{3,2},{4,5},{5,4},{6,7},{7,6},{8,9},{9,8},{10,11... | collective-permute-start | bytes 2064392 | tf_op jit(solution)/shard_map/ppermute | solution.py:25
  141.4 10.9 %collective-permute-start.1 = (bf16[128,2688]{1,0:T(8,128)(2,1)S(1)}, bf16[128,2688]{1,0:T(8,128)(2,1)S(1)}, u32[]{:S(2)}, u32[]{:S(2)}) collective-permute-start(bf16[128,2688]{1,0:T(8,128)(2,1)S(1)} %all_gather.7), channel_id=1, source_target_pairs={{0,1},{1,0},{2,3},{3,2},{4,5},{5,4},{6,7},{7,6},{8,9},{9,8},{10,11... | collective-permute-start | bytes 2064392 | tf_op jit(solution)/shard_map/ppermute | solution.py:25
  154.4 32.0 %all-to-all-start.3 = ((bf16[32,2,8,256]{3,2,1,0:T(8,128)(2,1)}), bf16[32,2,8,256]{3,2,1,0:T(8,128)(2,1)S(1)}, u32[]{:S(2)}, u32[]{:S(2)}) async-start(bf16[32,2,8,256]{3,2,1,0:T(8,128)(2,1)} %copy.14), calls=%async_computation.3 | async-start | bytes 524288 | tf_op jit(solution)/shard_map/all_to_all | solution.py:87

commit v2 on v1

--- a/solution.py
+++ b/solution.py
@@ -28,8 +28,26 @@
 def sum_over(block, axis):
     ways = lax.axis_size(axis)
     rows, columns = block.shape
-    pieces = block.astype(BF16).reshape(ways, rows // ways, columns)
-    return lax.all_to_all(pieces, axis, 0, 0).astype(F32).sum(0)
+    pieces = block.reshape(ways, rows // ways, columns)
+    me = lax.axis_index(axis)
+    mine = lax.dynamic_index_in_dim(pieces, me, 0, keepdims=False)
+    others = lax.all_to_all(pieces.astype(BF16), axis, 0, 0).astype(F32)
+    foreign = (lax.iota(jnp.int32, ways) != me)[:, None, None]
+    return mine + jnp.where(foreign, others, 0.0).sum(0)
+
+
+def total_over_far(block):
+    def swap(part, flip):
+        pairs = [(i, i ^ flip) for i in range(4)]
+        return lax.ppermute(part.astype(BF16), "zh", pairs).astype(F32)
+
+    half = block.shape[0] // 2
+    top, low = block[:half], block[half:]
+    top = top + swap(top, 1)
+    low = low + swap(low, 3)
+    top = top + swap(top, 3)
+    low = low + swap(low, 1)
+    return jnp.concatenate([top, low], axis=0)
 
 
 def shards(tokens, gate_weight, up_weight, down_weight, out_grad):
@@ -54,9 +72,9 @@
         axis=1,
     )
     units = gate_weight.shape[1]
-    part = part[:half] + swap_core(part[half:].astype(BF16)).astype(F32)
+    part = part[:half] + swap_core(part[half:])
     part = sum_over(part, "x")
-    part = sum_over(part, "zh")
+    part = total_over_far(part)
     gate_sum, up_sum, hidden_delta = (
         part[:, :units],
         part[:, units : 2 * units],
@@ -69,7 +87,6 @@
     ).astype(BF16)
     up_delta = (hidden_delta * gate_sum * gate_sigmoid).astype(BF16)
     whole = jnp.concatenate([hidden, gate_delta, up_delta], axis=1)
-    whole = lax.all_gather(whole, "zh", axis=0, tiled=True)
     whole = lax.all_gather(whole, "x", axis=0, tiled=True)
     whole = jnp.concatenate([whole, swap_core(whole)], axis=0)
     hidden, gate_delta, up_delta = (

time: 188 us -> 176 us (0.936)
  blocking collectives: 97.1 us -> 10.2 us
  starting transfers between devices: 42.2 us -> 85.2 us
  waiting for transfers between devices: 37.5 us -> 68.1 us
    all_to_all x2 -> x0, blocking collectives: 58.3 us -> none  [sum_over(): return lax.all_to_all(pieces, axis, 0, 0).astype(F32).sum(0)]
    ppermute x0 -> x4, starting transfers between devices: none -> 38.6 us  [swap(): return lax.ppermute(part.astype(BF16), 'zh', pairs).astype(F32)]
    all_gather x1 -> x0, blocking collectives: 27.4 us -> none  [shards(): whole = lax.all_gather(whole, 'zh', axis=0, tiled=True)]
    ppermute x0 -> x4, waiting for transfers between devices: none -> 18.9 us  [swap(): return lax.ppermute(part.astype(BF16), 'zh', pairs).astype(F32)]
    all_to_all x0 -> x1, waiting for transfers between devices: none -> 10.7 us  [sum_over(): others = lax.all_to_all(pieces.astype(BF16), axis, 0, 0).astype(F32)]
    all_to_all x0 -> x1, starting transfers between devices: none -> 4.01 us  [sum_over(): others = lax.all_to_all(pieces.astype(BF16), axis, 0, 0).astype(F32)]
    all_to_all x1, starting transfers between devices: 13.2 us -> 16.7 us  [shards(): ends = lax.all_to_all(ends, SECTION, 0, 0).astype(F32).sum(0).astype(BF16)]
    ppermute x2, starting transfers between devices: 12.9 us -> 9.73 us  [swap_core(): return lax.ppermute(block, 'core', [(0, 1), (1, 0)])]
  transfers between devices with their start and end apart: 4 -> 9, of which waited for: 4 -> 8; matrix products, arithmetic and copies ran while one was open for 2% -> 2% of each run, Pallas kernels for 0% -> 0%
where the time goes in v2:
time: 176 us; the launch traced here: 175 us
  starting transfers between devices  85.2 us (48%)
  waiting for transfers between devices  68.1 us (39%)
  blocking collectives  10.2 us (6%)
  matrix products  5.18 us (3%)
  other arithmetic  3.19 us (2%)
  local copies, waits for them, and re-layouts  2.68 us (2%)
    ppermute x4, starting transfers between devices, swap(): return lax.ppermute(part.astype(BF16), 'zh', pairs).astype(F32)  38.6 us
    ppermute x4, waiting for transfers between devices, swap(): return lax.ppermute(part.astype(BF16), 'zh', pairs).astype(F32)  18.9 us
    all_to_all x1, waiting for transfers between devices, shards(): both = lax.all_to_all(both, SECTION, 0, 0)  18.6 us
    all_to_all x1, starting transfers between devices, shards(): ends = lax.all_to_all(ends, SECTION, 0, 0).astype(F32).sum(0).astype(BF16)  16.7 us
    all_to_all x1, starting transfers between devices, shards(): both = lax.all_to_all(both, SECTION, 0, 0)  16.1 us
    all_to_all x1, waiting for transfers between devices, shards(): ends = lax.all_to_all(ends, SECTION, 0, 0).astype(F32).sum(0).astype(BF16)  15.5 us
    all_to_all x1, waiting for transfers between devices, sum_over(): others = lax.all_to_all(pieces.astype(BF16), axis, 0, 0).astype(F32)  10.7 us
    all_gather x1, blocking collectives, shards(): whole = lax.all_gather(whole, 'x', axis=0, tiled=True)  10.2 us
  transfers between devices with their start and end apart: 9, of which 8 were waited for; matrix products, arithmetic and copies ran while one was open for 2% of the time, Pallas kernels for 0%

profile of v2, /device:TPU:1, one launch (start us, length us, event | category | flops | bytes accessed | tf_op | source)
XLA Modules:
  0.0 175.4 jit_solution(11048331886634407053)
XLA Ops:
  0.7 0.8 pad_maximum_fusion.3
  1.4 0.7 broadcast_in_dim.19
  2.2 16.1 %all-to-all-start = ((bf16[32,2,8,256]{3,2,1,0:T(8,128)(2,1)}), bf16[32,2,8,256]{3,2,1,0:T(8,128)(2,1)S(1)}, u32[]{:S(2)}, u32[]{:S(2)}) async-start(bf16[32,2,8,256]{3,2,1,0:T(8,128)(2,1)} %broadcast_in_dim.19), calls=%async_computation | async-start | bytes 524288 | tf_op jit(solution)/shard_map/all_to_all | solution.py:61
  18.3 18.6 %all-to-all-done = bf16[32,2,8,256]{3,2,1,0:T(8,128)(2,1)S(1)} async-done(((bf16[32,2,8,256]{3,2,1,0:T(8,128)(2,1)}), bf16[32,2,8,256]{3,2,1,0:T(8,128)(2,1)S(1)}, u32[]{:S(2)}, u32[]{:S(2)}) %all-to-all-start) | async-done | bytes 262176 | tf_op jit(solution)/shard_map/all_to_all | solution.py:61
  36.9 0.3 fusion.14
  37.3 0.3 fusion.15
  37.9 0.4 copy-done.1
  38.9 3.8 %collective-permute-start = (f32[128,2688]{1,0:T(8,128)S(1)}, f32[128,2688]{1,0:T(8,128)S(1)}, u32[]{:S(2)}, u32[]{:S(2)}) collective-permute-start(f32[128,2688]{1,0:T(8,128)S(1)} %slice.59), channel_id=1, source_target_pairs={{0,1},{1,0},{2,3},{3,2},{4,5},{5,4},{6,7},{7,6},{8,9},{9,8},{10,11... | collective-permute-start | bytes 4128776 | tf_op jit(solution)/shard_map/ppermute | solution.py:25
  42.6 2.7 %collective-permute-done = f32[128,2688]{1,0:T(8,128)S(1)} collective-permute-done((f32[128,2688]{1,0:T(8,128)S(1)}, f32[128,2688]{1,0:T(8,128)S(1)}, u32[]{:S(2)}, u32[]{:S(2)}) %collective-permute-start) | collective-permute-done | bytes 1376288 | tf_op jit(solution)/shard_map/ppermute | solution.py:25
  45.5 0.9 convert_element_type.51
  46.5 4.0 %all-to-all-start.1 = ((bf16[4,32,2688]{2,1,0:T(8,128)(2,1)}), bf16[4,32,2688]{2,1,0:T(8,128)(2,1)S(1)}, u32[]{:S(2)}, u32[]{:S(2)}) async-start(bf16[4,32,2688]{2,1,0:T(8,128)(2,1)} %convert_element_type.51), calls=%async_computation.1 | async-start | bytes 1376256 | tf_op jit(solution)/shard_map/all_to_all | solution.py:34
  50.5 10.7 %all-to-all-done.1 = bf16[4,32,2688]{2,1,0:T(8,128)(2,1)S(1)} async-done(((bf16[4,32,2688]{2,1,0:T(8,128)(2,1)}), bf16[4,32,2688]{2,1,0:T(8,128)(2,1)S(1)}, u32[]{:S(2)}, u32[]{:S(2)}) %all-to-all-start.1) | async-done | bytes 688160 | tf_op jit(solution)/shard_map/all_to_all | solution.py:34
  61.4 15.4 %collective-permute-start.1 = (bf16[16,2688]{1,0:T(8,128)(2,1)S(1)}, bf16[16,2688]{1,0:T(8,128)(2,1)S(1)}, u32[]{:S(2)}, u32[]{:S(2)}) collective-permute-start(bf16[16,2688]{1,0:T(8,128)(2,1)S(1)} %get-tuple-element.13), channel_id=1, source_target_pairs={{0,8},{8,0},{16,24},{24,16},{1,9},{9,1},{17,25},{25,17},{2,10},{10... | collective-permute-start | bytes 258056 | tf_op jit(solution)/shard_map/ppermute | solution.py:42
  76.9 7.9 %collective-permute-start.3 = (bf16[16,2688]{1,0:T(8,128)(2,1)S(1)}, bf16[16,2688]{1,0:T(8,128)(2,1)S(1)}, u32[]{:S(2)}, u32[]{:S(2)}) collective-permute-start(bf16[16,2688]{1,0:T(8,128)(2,1)S(1)} %get-tuple-element.14), channel_id=1, source_target_pairs={{0,24},{8,16},{16,8},{24,0},{1,25},{9,17},{17,9},{25,1},{2,26},{10... | collective-permute-start | bytes 258056 | tf_op jit(solution)/shard_map/ppermute | solution.py:42
  84.8 6.9 %collective-permute-done.1 = bf16[16,2688]{1,0:T(8,128)(2,1)S(1)} collective-permute-done((bf16[16,2688]{1,0:T(8,128)(2,1)S(1)}, bf16[16,2688]{1,0:T(8,128)(2,1)S(1)}, u32[]{:S(2)}, u32[]{:S(2)}) %collective-permute-start.1) | collective-permute-done | bytes 86048 | tf_op jit(solution)/shard_map/ppermute | solution.py:42
  91.7 4.7 %collective-permute-done.3 = bf16[16,2688]{1,0:T(8,128)(2,1)S(1)} collective-permute-done((bf16[16,2688]{1,0:T(8,128)(2,1)S(1)}, bf16[16,2688]{1,0:T(8,128)(2,1)S(1)}, u32[]{:S(2)}, u32[]{:S(2)}) %collective-permute-start.3) | collective-permute-done | bytes 86048 | tf_op jit(solution)/shard_map/ppermute | solution.py:42
  96.5 6.4 %collective-permute-start.2 = (bf16[16,2688]{1,0:T(8,128)(2,1)S(1)}, bf16[16,2688]{1,0:T(8,128)(2,1)S(1)}, u32[]{:S(2)}, u32[]{:S(2)}) collective-permute-start(bf16[16,2688]{1,0:T(8,128)(2,1)S(1)} %get-tuple-element.11), channel_id=1, source_target_pairs={{0,24},{8,16},{16,8},{24,0},{1,25},{9,17},{17,9},{25,1},{2,26},{10... | collective-permute-start | bytes 258056 | tf_op jit(solution)/shard_map/ppermute | solution.py:42
  102.9 8.8 %collective-permute-start.4 = (bf16[16,2688]{1,0:T(8,128)(2,1)S(1)}, bf16[16,2688]{1,0:T(8,128)(2,1)S(1)}, u32[]{:S(2)}, u32[]{:S(2)}) collective-permute-start(bf16[16,2688]{1,0:T(8,128)(2,1)S(1)} %get-tuple-element.12), channel_id=1, source_target_pairs={{0,8},{8,0},{16,24},{24,16},{1,9},{9,1},{17,25},{25,17},{2,10},{10... | collective-permute-start | bytes 258056 | tf_op jit(solution)/shard_map/ppermute | solution.py:42
  111.7 7.3 %collective-permute-done.4 = bf16[16,2688]{1,0:T(8,128)(2,1)S(1)} collective-permute-done((bf16[16,2688]{1,0:T(8,128)(2,1)S(1)}, bf16[16,2688]{1,0:T(8,128)(2,1)S(1)}, u32[]{:S(2)}, u32[]{:S(2)}) %collective-permute-start.4) | collective-permute-done | bytes 86048 | tf_op jit(solution)/shard_map/ppermute | solution.py:42
  119.2 10.2 %all_gather.3 = bf16[128,2688]{1,0:T(8,128)(2,1)S(1)} all-gather(bf16[32,2688]{1,0:T(8,128)(2,1)S(1)} %pad_maximum_fusion.1), channel_id=1, replica_groups=mesh['y'=4,'zl'=8,'zh'=4,'x'=4,'core'=2] {'x'}, dimensions={0}, use_global_device_ids=true | all-gather | bytes 860160 | tf_op jit(solution)/shard_map/all_gather | solution.py:90
  129.4 6.0 %collective-permute-start.5 = (bf16[128,2688]{1,0:T(8,128)(2,1)S(1)}, bf16[128,2688]{1,0:T(8,128)(2,1)S(1)}, u32[]{:S(2)}, u32[]{:S(2)}) collective-permute-start(bf16[128,2688]{1,0:T(8,128)(2,1)S(1)} %all_gather.3), channel_id=1, source_target_pairs={{0,1},{1,0},{2,3},{3,2},{4,5},{5,4},{6,7},{7,6},{8,9},{9,8},{10,11... | collective-permute-start | bytes 2064392 | tf_op jit(solution)/shard_map/ppermute | solution.py:25
  135.5 1.7 collective-permute-done.5
  137.2 0.3 fusion.4
  137.9 0.3 fusion.2
  138.2 0.3 fusion.12
  138.5 0.7 copy.12
  139.3 16.7 %all-to-all-start.2 = ((bf16[32,2,8,256]{3,2,1,0:T(8,128)(2,1)}), bf16[32,2,8,256]{3,2,1,0:T(8,128)(2,1)S(1)}, u32[]{:S(2)}, u32[]{:S(2)}) async-start(bf16[32,2,8,256]{3,2,1,0:T(8,128)(2,1)} %copy.12), calls=%async_computation.2 | async-start | bytes 524288 | tf_op jit(solution)/shard_map/all_to_all | solution.py:104
  156.0 1.1 convolution_convert_fusion
  157.1 1.1 convolution_convert_fusion.1
  158.2 1.1 convolution_convert_fusion.2
  159.3 15.5 %all-to-all-done.2 = bf16[32,2,8,256]{3,2,1,0:T(8,128)(2,1)S(1)} async-done(((bf16[32,2,8,256]{3,2,1,0:T(8,128)(2,1)}), bf16[32,2,8,256]{3,2,1,0:T(8,128)(2,1)S(1)}, u32[]{:S(2)}, u32[]{:S(2)}) %all-to-all-start.2) | async-done | bytes 262176 | tf_op jit(solution)/shard_map/all_to_all | solution.py:104
  174.8 0.6 slice_bitcast_fusion.8
  (26 shorter events, 2.0 us)
Async XLA Ops:
  0.6 37.0 %copy-start = (bf16[256,896]{1,0:T(8,128)(2,1)S(1)}, bf16[256,896]{1,0:T(8,128)(2,1)}, u32[]{:S(2)}) copy-start(bf16[256,896]{1,0:T(8,128)(2,1)} %param.9) | copy-start | bytes 1376260
  0.6 36.6 %copy-start.2 = (bf16[896,256]{1,0:T(8,128)(2,1)S(1)}, bf16[896,256]{1,0:T(8,128)(2,1)}, u32[]{:S(2)}) copy-start(bf16[896,256]{1,0:T(8,128)(2,1)} %param.10) | copy-start | bytes 1376260
  2.2 34.7 %all-to-all-start = ((bf16[32,2,8,256]{3,2,1,0:T(8,128)(2,1)}), bf16[32,2,8,256]{3,2,1,0:T(8,128)(2,1)S(1)}, u32[]{:S(2)}, u32[]{:S(2)}) async-start(bf16[32,2,8,256]{3,2,1,0:T(8,128)(2,1)} %broadcast_in_dim.19), calls=%async_computation | async-start | bytes 524288 | tf_op jit(solution)/shard_map/all_to_all | solution.py:61
  37.2 1.0 copy-start.1
  38.9 6.5 %collective-permute-start = (f32[128,2688]{1,0:T(8,128)S(1)}, f32[128,2688]{1,0:T(8,128)S(1)}, u32[]{:S(2)}, u32[]{:S(2)}) collective-permute-start(f32[128,2688]{1,0:T(8,128)S(1)} %slice.59), channel_id=1, source_target_pairs={{0,1},{1,0},{2,3},{3,2},{4,5},{5,4},{6,7},{7,6},{8,9},{9,8},{10,11... | collective-permute-start | bytes 4128776 | tf_op jit(solution)/shard_map/ppermute | solution.py:25
  46.5 14.7 %all-to-all-start.1 = ((bf16[4,32,2688]{2,1,0:T(8,128)(2,1)}), bf16[4,32,2688]{2,1,0:T(8,128)(2,1)S(1)}, u32[]{:S(2)}, u32[]{:S(2)}) async-start(bf16[4,32,2688]{2,1,0:T(8,128)(2,1)} %convert_element_type.51), calls=%async_computation.1 | async-start | bytes 1376256 | tf_op jit(solution)/shard_map/all_to_all | solution.py:34
  61.4 30.3 %collective-permute-start.1 = (bf16[16,2688]{1,0:T(8,128)(2,1)S(1)}, bf16[16,2688]{1,0:T(8,128)(2,1)S(1)}, u32[]{:S(2)}, u32[]{:S(2)}) collective-permute-start(bf16[16,2688]{1,0:T(8,128)(2,1)S(1)} %get-tuple-element.13), channel_id=1, source_target_pairs={{0,8},{8,0},{16,24},{24,16},{1,9},{9,1},{17,25},{25,17},{2,10},{10... | collective-permute-start | bytes 258056 | tf_op jit(solution)/shard_map/ppermute | solution.py:42
  76.9 19.6 %collective-permute-start.3 = (bf16[16,2688]{1,0:T(8,128)(2,1)S(1)}, bf16[16,2688]{1,0:T(8,128)(2,1)S(1)}, u32[]{:S(2)}, u32[]{:S(2)}) collective-permute-start(bf16[16,2688]{1,0:T(8,128)(2,1)S(1)} %get-tuple-element.14), channel_id=1, source_target_pairs={{0,24},{8,16},{16,8},{24,0},{1,25},{9,17},{17,9},{25,1},{2,26},{10... | collective-permute-start | bytes 258056 | tf_op jit(solution)/shard_map/ppermute | solution.py:42
  96.5 15.2 %collective-permute-start.2 = (bf16[16,2688]{1,0:T(8,128)(2,1)S(1)}, bf16[16,2688]{1,0:T(8,128)(2,1)S(1)}, u32[]{:S(2)}, u32[]{:S(2)}) collective-permute-start(bf16[16,2688]{1,0:T(8,128)(2,1)S(1)} %get-tuple-element.11), channel_id=1, source_target_pairs={{0,24},{8,16},{16,8},{24,0},{1,25},{9,17},{17,9},{25,1},{2,26},{10... | collective-permute-start | bytes 258056 | tf_op jit(solution)/shard_map/ppermute | solution.py:42
  102.9 16.1 %collective-permute-start.4 = (bf16[16,2688]{1,0:T(8,128)(2,1)S(1)}, bf16[16,2688]{1,0:T(8,128)(2,1)S(1)}, u32[]{:S(2)}, u32[]{:S(2)}) collective-permute-start(bf16[16,2688]{1,0:T(8,128)(2,1)S(1)} %get-tuple-element.12), channel_id=1, source_target_pairs={{0,8},{8,0},{16,24},{24,16},{1,9},{9,1},{17,25},{25,17},{2,10},{10... | collective-permute-start | bytes 258056 | tf_op jit(solution)/shard_map/ppermute | solution.py:42
  129.4 7.7 %collective-permute-start.5 = (bf16[128,2688]{1,0:T(8,128)(2,1)S(1)}, bf16[128,2688]{1,0:T(8,128)(2,1)S(1)}, u32[]{:S(2)}, u32[]{:S(2)}) collective-permute-start(bf16[128,2688]{1,0:T(8,128)(2,1)S(1)} %all_gather.3), channel_id=1, source_target_pairs={{0,1},{1,0},{2,3},{3,2},{4,5},{5,4},{6,7},{7,6},{8,9},{9,8},{10,11... | collective-permute-start | bytes 2064392 | tf_op jit(solution)/shard_map/ppermute | solution.py:25
  135.4 2.1 %copy-start.3 = (bf16[896,256]{1,0:T(8,128)(2,1)S(1)}, bf16[896,256]{1,0:T(8,128)(2,1)}, u32[]{:S(2)}) copy-start(bf16[896,256]{1,0:T(8,128)(2,1)} %param.10) | copy-start | bytes 1376260
  139.3 35.5 %all-to-all-start.2 = ((bf16[32,2,8,256]{3,2,1,0:T(8,128)(2,1)}), bf16[32,2,8,256]{3,2,1,0:T(8,128)(2,1)S(1)}, u32[]{:S(2)}, u32[]{:S(2)}) async-start(bf16[32,2,8,256]{3,2,1,0:T(8,128)(2,1)} %copy.12), calls=%async_computation.2 | async-start | bytes 524288 | tf_op jit(solution)/shard_map/all_to_all | solution.py:104

commit v3 on v2

v3 whole, which is shorter than its diff:
```python
import jax
import jax.numpy as jnp
from jax import lax
from jax.sharding import Mesh, PartitionSpec as P

SECTION = ("y", "zl")
FSDP = ("zh", "x", "core")
BF16 = jnp.bfloat16
F32 = jnp.float32


def contract_last(left, right):
    return lax.dot_general(
        left, right, (((1,), (1,)), ((), ())), preferred_element_type=F32
    )


def contract_first(left, right):
    return lax.dot_general(
        left, right, (((0,), (0,)), ((), ())), preferred_element_type=F32
    )


def swap_core(block):
    return lax.ppermute(block, "core", [(0, 1), (1, 0)])


def sum_over_x(block):
    ways = lax.axis_size("x")
    rows, columns = block.shape
    pieces = block.reshape(ways, rows // ways, columns)
    me = lax.axis_index("x")
    mine = lax.dynamic_index_in_dim(pieces, me, 0, keepdims=False)
    others = lax.all_to_all(pieces.astype(BF16), "x", 0, 0).astype(F32)
    foreign = (lax.iota(jnp.int32, ways) != me)[:, None, None]
    return mine + jnp.where(foreign, others, 0.0).sum(0)


def swap_far(part, flips):
    pairs = [
        (2 * z + core, 2 * (z ^ flips[core]) + core)
        for z in range(4)
        for core in range(2)
    ]
    return lax.ppermute(part.astype(BF16), ("zh", "core"), pairs)


def total_over_far(block):
    half = block.shape[0] // 2
    top, low = block[:half], block[half:]
    top_in, low_in = swap_far(top, (1, 3)), swap_far(low, (1, 3))
    top = top + top_in
    low_in, _ = lax.optimization_barrier((low_in, top))
    top_in = swap_far(top, (3, 1))
    low = low + low_in
    low_in = swap_far(low, (3, 1))
    top = top + top_in
    low = low + low_in
    return jnp.concatenate([top, low], axis=0)


def shards(tokens, gate_weight, up_weight, down_weight, out_grad):
    own, width = tokens.shape
    units = gate_weight.shape[1]
    sections = lax.axis_size(SECTION)
    rows = own * sections
    half = rows // 2
    both = jnp.concatenate([tokens, out_grad], axis=1)
    both = jnp.broadcast_to(both[None], (sections, own, 2 * width))
    both = lax.all_to_all(both, SECTION, 0, 0).reshape(rows, 2 * width)

    core = lax.axis_index("core")

    def part_of(which):
        side = lax.dynamic_slice_in_dim(both, which * half, half, 0)
        some_tokens, some_grads = side[:, :width], side[:, width:]
        return jnp.concatenate(
            [
                jnp.dot(some_tokens, gate_weight, preferred_element_type=F32),
                jnp.dot(some_tokens, up_weight, preferred_element_type=F32),
                contract_last(some_grads, down_weight),
            ],
            axis=1,
        )

    received = swap_core(part_of(1 - core))
    part = part_of(core) + received
    part = sum_over_x(part)
    part = total_over_far(part)
    gate_sum, up_sum, hidden_delta = (
        part[:, :units],
        part[:, units : 2 * units],
        part[:, 2 * units :],
    )
    gate_sigmoid = jax.nn.sigmoid(gate_sum)
    hidden = (gate_sum * gate_sigmoid * up_sum).astype(BF16)
    gate_delta = (
        hidden_delta * up_sum * gate_sigmoid * (1.0 + gate_sum * (1.0 - gate_sigmoid))
    ).astype(BF16)
    up_delta = (hidden_delta * gate_sum * gate_sigmoid).astype(BF16)
    mine = jnp.concatenate([hidden, gate_delta, up_delta], axis=1)
    mine = lax.all_gather(mine, "x", axis=0, tiled=True)
    theirs = swap_core(mine)
    first = core == 0
    whole = jnp.concatenate(
        [jnp.where(first, mine, theirs), jnp.where(first, theirs, mine)], axis=0
    )
    hidden, gate_delta, up_delta = (
        whole[:, :units],
        whole[:, units : 2 * units],
        whole[:, 2 * units :],
    )
    forward_part = jnp.dot(hidden, down_weight, preferred_element_type=F32)
    backward_part = contract_last(gate_delta, gate_weight) + contract_last(
        up_delta, up_weight
    )
    ends = jnp.concatenate([forward_part, backward_part], axis=1).astype(BF16)
    ends = ends.reshape(sections, own, 2 * width)
    ends = lax.all_to_all(ends, SECTION, 0, 0)
    ends = lax.optimization_barrier(ends.astype(F32)).sum(0).astype(BF16)
    all_tokens, all_grads = both[:, :width], both[:, width:]
    gate_grads = contract_first(all_tokens, gate_delta).astype(BF16)
    up_grads = contract_first(all_tokens, up_delta).astype(BF16)
    down_grads = contract_first(hidden, all_grads).astype(BF16)
    return (ends[:, :width], ends[:, width:], gate_grads, up_grads, down_grads)


def solution(mesh):
    fine = Mesh(
        mesh.devices.reshape(4, 8, 4, 4, 2), ("y", "zl", "zh", "x", "core")
    )
    return jax.shard_map(
        shards,
        mesh=fine,
        in_specs=(
            P(SECTION, FSDP),
            P(FSDP, SECTION),
            P(FSDP, SECTION),
            P(SECTION, FSDP),
            P(SECTION, FSDP),
        ),
        out_specs=(
            P(SECTION, FSDP),
            P(SECTION, FSDP),
            P(FSDP, SECTION),
            P(FSDP, SECTION),
            P(SECTION, FSDP),
        ),
        check_vma=False,
    )
```

time: 176 us -> 172 us (0.977)
  starting transfers between devices: 85.2 us -> 78.4 us
  other arithmetic: 3.19 us -> 7.18 us
  waiting for transfers between devices: 68.1 us -> 65.1 us
    all_to_all x3, starting transfers between devices: 36.8 us -> 29.8 us  [the longest x1 16.1 us: shards(): both = lax.all_to_all(both, SECTION, 0, 0).reshape(rows, 2 * width)]
    ppermute x2, starting transfers between devices: 9.73 us -> 13.6 us  [swap_core(): return lax.ppermute(block, 'core', [(0, 1), (1, 0)])]
    ppermute x4, starting transfers between devices: 38.6 us -> 35 us  [swap_far(): return lax.ppermute(part.astype(BF16), ('zh', 'core'), pairs)]
    ppermute x4, waiting for transfers between devices: 18.9 us -> 16.2 us  [swap_far(): return lax.ppermute(part.astype(BF16), ('zh', 'core'), pairs)]
where the time goes in v3:
time: 172 us; the launch traced here: 171 us
  starting transfers between devices  78.4 us (46%)
  waiting for transfers between devices  65.1 us (38%)
  blocking collectives  11.1 us (6%)
  other arithmetic  7.18 us (4%)
  matrix products  6.77 us (4%)
    ppermute x4, starting transfers between devices, swap_far(): return lax.ppermute(part.astype(BF16), ('zh', 'core'), pairs)  35 us
    all_to_all x1, waiting for transfers between devices, shards(): both = lax.all_to_all(both, SECTION, 0, 0).reshape(rows, 2 * width)  18.6 us
    ppermute x4, waiting for transfers between devices, swap_far(): return lax.ppermute(part.astype(BF16), ('zh', 'core'), pairs)  16.2 us
    all_to_all x1, starting transfers between devices, shards(): both = lax.all_to_all(both, SECTION, 0, 0).reshape(rows, 2 * width)  16.1 us
    all_to_all x1, waiting for transfers between devices, shards(): ends = lax.all_to_all(ends, SECTION, 0, 0)  15.5 us
    ppermute x2, starting transfers between devices, swap_core(): return lax.ppermute(block, 'core', [(0, 1), (1, 0)])  13.6 us
    all_gather x1, blocking collectives, shards(): mine = lax.all_gather(mine, 'x', axis=0, tiled=True)  11.1 us
    all_to_all x1, waiting for transfers between devices, sum_over_x(): others = lax.all_to_all(pieces.astype(BF16), 'x', 0, 0).astype(F32)  10.9 us
  transfers between devices with their start and end apart: 9, of which 8 were waited for; matrix products, arithmetic and copies ran while one was open for 2% of the time, Pallas kernels for 0%

profile of v3, /device:TPU:1, one launch (start us, length us, event | category | flops | bytes accessed | tf_op | source)
XLA Modules:
  0.0 170.9 jit_solution(15218024791180971343)
XLA Ops:
  0.7 0.8 pad_maximum_fusion.5
  1.4 0.7 broadcast_in_dim.19
  2.2 16.1 %all-to-all-start = ((bf16[32,8,512]{2,1,0:T(8,128)(2,1)}), bf16[32,8,512]{2,1,0:T(8,128)(2,1)S(1)}, u32[]{:S(2)}, u32[]{:S(2)}) async-start(bf16[32,8,512]{2,1,0:T(8,128)(2,1)} %broadcast_in_dim.19), calls=%async_computation | async-start | bytes 524288 | tf_op jit(solution)/shard_map/all_to_all | solution.py:70
  18.3 18.6 %all-to-all-done = bf16[32,8,512]{2,1,0:T(8,128)(2,1)S(1)} async-done(((bf16[32,8,512]{2,1,0:T(8,128)(2,1)}), bf16[32,8,512]{2,1,0:T(8,128)(2,1)S(1)}, u32[]{:S(2)}, u32[]{:S(2)}) %all-to-all-start) | async-done | bytes 262176 | tf_op jit(solution)/shard_map/all_to_all | solution.py:70
  36.9 1.2 fusion.15
  38.8 3.9 %collective-permute-start = (f32[128,2688]{1,0:T(8,128)S(1)}, f32[128,2688]{1,0:T(8,128)}, u32[]{:S(2)}, u32[]{:S(2)}) collective-permute-start(f32[128,2688]{1,0:T(8,128)S(1)} %pad_maximum_fusion), channel_id=1, source_target_pairs={{0,1},{1,0},{2,3},{3,2},{4,5},{5,4},{6,7},{7,6},{8,9},{9,8},{10,11... | collective-permute-start | bytes 4128776 | tf_op jit(solution)/shard_map/ppermute | solution.py:25
  43.5 2.1 %collective-permute-done = f32[128,2688]{1,0:T(8,128)} collective-permute-done((f32[128,2688]{1,0:T(8,128)S(1)}, f32[128,2688]{1,0:T(8,128)}, u32[]{:S(2)}, u32[]{:S(2)}) %collective-permute-start) | collective-permute-done | bytes 1376288 | tf_op jit(solution)/shard_map/ppermute | solution.py:25
  45.6 1.5 maximum_add_fusion
  47.1 0.9 convert_element_type.56
  48.1 4.2 %all-to-all-start.1 = ((bf16[4,32,2688]{2,1,0:T(8,128)(2,1)}), bf16[4,32,2688]{2,1,0:T(8,128)(2,1)}, u32[]{:S(2)}, u32[]{:S(2)}) async-start(bf16[4,32,2688]{2,1,0:T(8,128)(2,1)} %convert_element_type.56), calls=%async_computation.1 | async-start | bytes 1376256 | tf_op jit(solution)/shard_map/all_to_all | solution.py:34
  52.3 10.9 %all-to-all-done.1 = bf16[4,32,2688]{2,1,0:T(8,128)(2,1)} async-done(((bf16[4,32,2688]{2,1,0:T(8,128)(2,1)}), bf16[4,32,2688]{2,1,0:T(8,128)(2,1)}, u32[]{:S(2)}, u32[]{:S(2)}) %all-to-all-start.1) | async-done | bytes 688160 | tf_op jit(solution)/shard_map/all_to_all | solution.py:34
  63.1 1.3 select_reduce_fusion
  64.5 15.2 %collective-permute-start.1 = (bf16[16,2688]{1,0:T(8,128)(2,1)S(1)}, bf16[16,2688]{1,0:T(8,128)(2,1)S(1)}, u32[]{:S(2)}, u32[]{:S(2)}) collective-permute-start(bf16[16,2688]{1,0:T(8,128)(2,1)S(1)} %get-tuple-element.14), channel_id=1, source_target_pairs={{0,8},{1,25},{8,0},{9,17},{16,24},{17,9},{24,16},{25,1},{2,10},{3,... | collective-permute-start | bytes 258056 | tf_op jit(solution)/shard_map/ppermute | solution.py:45
  79.8 1.9 %collective-permute-start.3 = (bf16[16,2688]{1,0:T(8,128)(2,1)S(1)}, bf16[16,2688]{1,0:T(8,128)(2,1)S(1)}, u32[]{:S(2)}, u32[]{:S(2)}) collective-permute-start(bf16[16,2688]{1,0:T(8,128)(2,1)S(1)} %get-tuple-element.15), channel_id=1, source_target_pairs={{0,8},{1,25},{8,0},{9,17},{16,24},{17,9},{24,16},{25,1},{2,10},{3,... | collective-permute-start | bytes 258056 | tf_op jit(solution)/shard_map/ppermute | solution.py:45
  81.7 6.6 %collective-permute-done.1 = bf16[16,2688]{1,0:T(8,128)(2,1)S(1)} collective-permute-done((bf16[16,2688]{1,0:T(8,128)(2,1)S(1)}, bf16[16,2688]{1,0:T(8,128)(2,1)S(1)}, u32[]{:S(2)}, u32[]{:S(2)}) %collective-permute-start.1) | collective-permute-done | bytes 86048 | tf_op jit(solution)/shard_map/ppermute | solution.py:45
  88.3 11.3 %collective-permute-start.2 = (bf16[16,2688]{1,0:T(8,128)(2,1)S(1)}, bf16[16,2688]{1,0:T(8,128)(2,1)S(1)}, u32[]{:S(2)}, u32[]{:S(2)}) collective-permute-start(bf16[16,2688]{1,0:T(8,128)(2,1)S(1)} %get-tuple-element.7), channel_id=1, source_target_pairs={{0,24},{1,9},{8,16},{9,1},{16,8},{17,25},{24,0},{25,17},{2,26},{3,... | collective-permute-start | bytes 258056 | tf_op jit(solution)/shard_map/ppermute | solution.py:45
  99.7 6.6 %collective-permute-start.4 = (bf16[16,2688]{1,0:T(8,128)(2,1)S(1)}, bf16[16,2688]{1,0:T(8,128)(2,1)S(1)}, u32[]{:S(2)}, u32[]{:S(2)}) collective-permute-start(bf16[16,2688]{1,0:T(8,128)(2,1)S(1)} %fusion.10), channel_id=1, source_target_pairs={{0,24},{1,9},{8,16},{9,1},{16,8},{17,25},{24,0},{25,17},{2,26},{3,... | collective-permute-start | bytes 258056 | tf_op jit(solution)/shard_map/ppermute | solution.py:45
  106.2 5.7 %collective-permute-done.2 = bf16[16,2688]{1,0:T(8,128)(2,1)S(1)} collective-permute-done((bf16[16,2688]{1,0:T(8,128)(2,1)S(1)}, bf16[16,2688]{1,0:T(8,128)(2,1)S(1)}, u32[]{:S(2)}, u32[]{:S(2)}) %collective-permute-start.2) | collective-permute-done | bytes 86048 | tf_op jit(solution)/shard_map/ppermute | solution.py:45
  111.9 3.9 %collective-permute-done.4 = bf16[16,2688]{1,0:T(8,128)(2,1)S(1)} collective-permute-done((bf16[16,2688]{1,0:T(8,128)(2,1)S(1)}, bf16[16,2688]{1,0:T(8,128)(2,1)S(1)}, u32[]{:S(2)}, u32[]{:S(2)}) %collective-permute-start.4) | collective-permute-done | bytes 86048 | tf_op jit(solution)/shard_map/ppermute | solution.py:45
  116.0 11.1 %all_gather.3 = bf16[128,2688]{1,0:T(8,128)(2,1)S(1)} all-gather(bf16[32,2688]{1,0:T(8,128)(2,1)S(1)} %pad_maximum_fusion.3), channel_id=1, replica_groups=mesh['y'=4,'zl'=8,'zh'=4,'x'=4,'core'=2] {'x'}, dimensions={0}, use_global_device_ids=true | all-gather | bytes 860160 | tf_op jit(solution)/shard_map/all_gather | solution.py:102
  127.1 9.7 %collective-permute-start.5 = (bf16[128,2688]{1,0:T(8,128)(2,1)S(1)}, bf16[128,2688]{1,0:T(8,128)(2,1)}, u32[]{:S(2)}, u32[]{:S(2)}) collective-permute-start(bf16[128,2688]{1,0:T(8,128)(2,1)S(1)} %all_gather.3), channel_id=1, source_target_pairs={{0,1},{1,0},{2,3},{3,2},{4,5},{5,4},{6,7},{7,6},{8,9},{9,8},{10,11... | collective-permute-start | bytes 2064392 | tf_op jit(solution)/shard_map/ppermute | solution.py:25
  136.8 1.9 %collective-permute-done.5 = bf16[128,2688]{1,0:T(8,128)(2,1)} collective-permute-done((bf16[128,2688]{1,0:T(8,128)(2,1)S(1)}, bf16[128,2688]{1,0:T(8,128)(2,1)}, u32[]{:S(2)}, u32[]{:S(2)}) %collective-permute-start.5) | collective-permute-done | bytes 688160 | tf_op jit(solution)/shard_map/ppermute | solution.py:25
  138.7 1.4 broadcast_select_fusion.1
  140.4 0.3 fusion.27
  140.8 0.3 fusion.2
  141.1 0.7 pad_maximum_fusion.2
  141.8 9.6 %all-to-all-start.2 = ((bf16[32,8,512]{2,1,0:T(8,128)(2,1)}), bf16[32,8,512]{2,1,0:T(8,128)(2,1)S(1)}, u32[]{:S(2)}, u32[]{:S(2)}) async-start(bf16[32,8,512]{2,1,0:T(8,128)(2,1)} %pad_maximum_fusion.2), calls=%async_computation.2 | async-start | bytes 524288 | tf_op jit(solution)/shard_map/all_to_all | solution.py:119
  151.4 1.1 convolution_convert_fusion
  152.5 1.1 convolution_convert_fusion.1
  153.6 1.1 convolution_convert_fusion.2
  154.7 15.5 %all-to-all-done.2 = bf16[32,8,512]{2,1,0:T(8,128)(2,1)S(1)} async-done(((bf16[32,8,512]{2,1,0:T(8,128)(2,1)}), bf16[32,8,512]{2,1,0:T(8,128)(2,1)S(1)}, u32[]{:S(2)}, u32[]{:S(2)}) %all-to-all-start.2) | async-done | bytes 262176 | tf_op jit(solution)/shard_map/all_to_all | solution.py:119
  170.3 0.6 fusion.34
  (27 shorter events, 2.0 us)
Async XLA Ops:
  0.6 37.8 %copy-start = (bf16[896,256]{1,0:T(8,128)(2,1)S(1)}, bf16[896,256]{1,0:T(8,128)(2,1)}, u32[]{:S(2)}) copy-start(bf16[896,256]{1,0:T(8,128)(2,1)} %param.8) | copy-start | bytes 1376260
  0.6 37.5 %copy-start.2 = (bf16[256,896]{1,0:T(8,128)(2,1)S(1)}, bf16[256,896]{1,0:T(8,128)(2,1)}, u32[]{:S(2)}) copy-start(bf16[256,896]{1,0:T(8,128)(2,1)} %param.6) | copy-start | bytes 1376260
  2.2 34.7 %all-to-all-start = ((bf16[32,8,512]{2,1,0:T(8,128)(2,1)}), bf16[32,8,512]{2,1,0:T(8,128)(2,1)S(1)}, u32[]{:S(2)}, u32[]{:S(2)}) async-start(bf16[32,8,512]{2,1,0:T(8,128)(2,1)} %broadcast_in_dim.19), calls=%async_computation | async-start | bytes 524288 | tf_op jit(solution)/shard_map/all_to_all | solution.py:70
  38.7 4.3 %copy-start.1 = (bf16[256,896]{1,0:T(8,128)(2,1)S(1)}, bf16[256,896]{1,0:T(8,128)(2,1)}, u32[]{:S(2)}) copy-start(bf16[256,896]{1,0:T(8,128)(2,1)} %param.7) | copy-start | bytes 1376260
  38.8 6.8 %collective-permute-start = (f32[128,2688]{1,0:T(8,128)S(1)}, f32[128,2688]{1,0:T(8,128)}, u32[]{:S(2)}, u32[]{:S(2)}) collective-permute-start(f32[128,2688]{1,0:T(8,128)S(1)} %pad_maximum_fusion), channel_id=1, source_target_pairs={{0,1},{1,0},{2,3},{3,2},{4,5},{5,4},{6,7},{7,6},{8,9},{9,8},{10,11... | collective-permute-start | bytes 4128776 | tf_op jit(solution)/shard_map/ppermute | solution.py:25
  48.1 15.1 %all-to-all-start.1 = ((bf16[4,32,2688]{2,1,0:T(8,128)(2,1)}), bf16[4,32,2688]{2,1,0:T(8,128)(2,1)}, u32[]{:S(2)}, u32[]{:S(2)}) async-start(bf16[4,32,2688]{2,1,0:T(8,128)(2,1)} %convert_element_type.56), calls=%async_computation.1 | async-start | bytes 1376256 | tf_op jit(solution)/shard_map/all_to_all | solution.py:34
  64.5 23.8 %collective-permute-start.1 = (bf16[16,2688]{1,0:T(8,128)(2,1)S(1)}, bf16[16,2688]{1,0:T(8,128)(2,1)S(1)}, u32[]{:S(2)}, u32[]{:S(2)}) collective-permute-start(bf16[16,2688]{1,0:T(8,128)(2,1)S(1)} %get-tuple-element.14), channel_id=1, source_target_pairs={{0,8},{1,25},{8,0},{9,17},{16,24},{17,9},{24,16},{25,1},{2,10},{3,... | collective-permute-start | bytes 258056 | tf_op jit(solution)/shard_map/ppermute | solution.py:45
  79.8 19.8 %collective-permute-start.3 = (bf16[16,2688]{1,0:T(8,128)(2,1)S(1)}, bf16[16,2688]{1,0:T(8,128)(2,1)S(1)}, u32[]{:S(2)}, u32[]{:S(2)}) collective-permute-start(bf16[16,2688]{1,0:T(8,128)(2,1)S(1)} %get-tuple-element.15), channel_id=1, source_target_pairs={{0,8},{1,25},{8,0},{9,17},{16,24},{17,9},{24,16},{25,1},{2,10},{3,... | collective-permute-start | bytes 258056 | tf_op jit(solution)/shard_map/ppermute | solution.py:45
  88.3 23.6 %collective-permute-start.2 = (bf16[16,2688]{1,0:T(8,128)(2,1)S(1)}, bf16[16,2688]{1,0:T(8,128)(2,1)S(1)}, u32[]{:S(2)}, u32[]{:S(2)}) collective-permute-start(bf16[16,2688]{1,0:T(8,128)(2,1)S(1)} %get-tuple-element.7), channel_id=1, source_target_pairs={{0,24},{1,9},{8,16},{9,1},{16,8},{17,25},{24,0},{25,17},{2,26},{3,... | collective-permute-start | bytes 258056 | tf_op jit(solution)/shard_map/ppermute | solution.py:45
  99.7 16.2 %collective-permute-start.4 = (bf16[16,2688]{1,0:T(8,128)(2,1)S(1)}, bf16[16,2688]{1,0:T(8,128)(2,1)S(1)}, u32[]{:S(2)}, u32[]{:S(2)}) collective-permute-start(bf16[16,2688]{1,0:T(8,128)(2,1)S(1)} %fusion.10), channel_id=1, source_target_pairs={{0,24},{1,9},{8,16},{9,1},{16,8},{17,25},{24,0},{25,17},{2,26},{3,... | collective-permute-start | bytes 258056 | tf_op jit(solution)/shard_map/ppermute | solution.py:45
  127.1 9.7 %copy-start.3 = (bf16[128,2688]{1,0:T(8,128)(2,1)}, bf16[128,2688]{1,0:T(8,128)(2,1)S(1)}, u32[]{:S(2)}) copy-start(bf16[128,2688]{1,0:T(8,128)(2,1)S(1)} %all_gather.3) | copy-start | bytes 2064388
  127.1 11.6 %collective-permute-start.5 = (bf16[128,2688]{1,0:T(8,128)(2,1)S(1)}, bf16[128,2688]{1,0:T(8,128)(2,1)}, u32[]{:S(2)}, u32[]{:S(2)}) collective-permute-start(bf16[128,2688]{1,0:T(8,128)(2,1)S(1)} %all_gather.3), channel_id=1, source_target_pairs={{0,1},{1,0},{2,3},{3,2},{4,5},{5,4},{6,7},{7,6},{8,9},{9,8},{10,11... | collective-permute-start | bytes 2064392 | tf_op jit(solution)/shard_map/ppermute | solution.py:25
  141.8 28.3 %all-to-all-start.2 = ((bf16[32,8,512]{2,1,0:T(8,128)(2,1)}), bf16[32,8,512]{2,1,0:T(8,128)(2,1)S(1)}, u32[]{:S(2)}, u32[]{:S(2)}) async-start(bf16[32,8,512]{2,1,0:T(8,128)(2,1)} %pad_maximum_fusion.2), calls=%async_computation.2 | async-start | bytes 524288 | tf_op jit(solution)/shard_map/all_to_all | solution.py:119

commit v4 on v3

--- a/solution.py
+++ b/solution.py
@@ -28,12 +28,8 @@
 def sum_over_x(block):
     ways = lax.axis_size("x")
     rows, columns = block.shape
-    pieces = block.reshape(ways, rows // ways, columns)
-    me = lax.axis_index("x")
-    mine = lax.dynamic_index_in_dim(pieces, me, 0, keepdims=False)
-    others = lax.all_to_all(pieces.astype(BF16), "x", 0, 0).astype(F32)
-    foreign = (lax.iota(jnp.int32, ways) != me)[:, None, None]
-    return mine + jnp.where(foreign, others, 0.0).sum(0)
+    pieces = block.astype(BF16).reshape(ways, rows // ways, columns)
+    return lax.all_to_all(pieces, "x", 0, 0).astype(F32).sum(0)
 
 
 def swap_far(part, flips):
@@ -45,18 +41,25 @@
     return lax.ppermute(part.astype(BF16), ("zh", "core"), pairs)
 
 
-def total_over_far(block):
-    half = block.shape[0] // 2
-    top, low = block[:half], block[half:]
-    top_in, low_in = swap_far(top, (1, 3)), swap_far(low, (1, 3))
-    top = top + top_in
-    low_in, _ = lax.optimization_barrier((low_in, top))
-    top_in = swap_far(top, (3, 1))
-    low = low + low_in
-    low_in = swap_far(low, (3, 1))
-    top = top + top_in
-    low = low + low_in
-    return jnp.concatenate([top, low], axis=0)
+def deltas_of(part):
+    units = part.shape[1] // 3
+    gate_sum, up_sum, hidden_delta = (
+        part[:, :units],
+        part[:, units : 2 * units],
+        part[:, 2 * units :],
+    )
+    gate_sigmoid = jax.nn.sigmoid(gate_sum)
+    hidden = gate_sum * gate_sigmoid * up_sum
+    gate_delta = (
+        hidden_delta * up_sum * gate_sigmoid * (1.0 + gate_sum * (1.0 - gate_sigmoid))
+    )
+    up_delta = hidden_delta * gate_sum * gate_sigmoid
+    return jnp.concatenate([hidden, gate_delta, up_delta], axis=1).astype(BF16)
+
+
+def gather_over_x(block):
+    mine = lax.all_gather(block, "x", axis=0, tiled=False)
+    return mine, swap_core(mine)
 
 
 def shards(tokens, gate_weight, up_weight, down_weight, out_grad):
@@ -83,28 +86,28 @@
             axis=1,
         )
 
-    received = swap_core(part_of(1 - core))
-    part = part_of(core) + received
-    part = sum_over_x(part)
-    part = total_over_far(part)
-    gate_sum, up_sum, hidden_delta = (
-        part[:, :units],
-        part[:, units : 2 * units],
-        part[:, 2 * units :],
-    )
-    gate_sigmoid = jax.nn.sigmoid(gate_sum)
-    hidden = (gate_sum * gate_sigmoid * up_sum).astype(BF16)
-    gate_delta = (
-        hidden_delta * up_sum * gate_sigmoid * (1.0 + gate_sum * (1.0 - gate_sigmoid))
-    ).astype(BF16)
-    up_delta = (hidden_delta * gate_sum * gate_sigmoid).astype(BF16)
-    mine = jnp.concatenate([hidden, gate_delta, up_delta], axis=1)
-    mine = lax.all_gather(mine, "x", axis=0, tiled=True)
-    theirs = swap_core(mine)
+    received = swap_core(part_of(1 - core).astype(BF16))
+    part = sum_over_x(part_of(core) + received)
+
+    piece = part.shape[0] // 2
+    top, low = part[:piece], part[piece:]
+    top_in, low_in = swap_far(top, (1, 3)), swap_far(low, (1, 3))
+    top = top + top_in
+    low_in, _ = lax.optimization_barrier((low_in, top))
+    top_in = swap_far(top, (3, 1))
+    low = low + low_in
+    low_in = swap_far(low, (3, 1))
+    top = deltas_of(top + top_in)
+    top_mine, top_theirs = gather_over_x(top)
+    low_in, _ = lax.optimization_barrier((low_in, top_theirs))
+    low = deltas_of(low + low_in)
+    low_mine, low_theirs = gather_over_x(low)
+    mine = jnp.concatenate([top_mine, low_mine], axis=1)
+    theirs = jnp.concatenate([top_theirs, low_theirs], axis=1)
     first = core == 0
-    whole = jnp.concatenate(
-        [jnp.where(first, mine, theirs), jnp.where(first, theirs, mine)], axis=0
-    )
+    whole = jnp.stack(
+        [jnp.where(first, mine, theirs), jnp.where(first, theirs, mine)]
+    ).reshape(rows, 3 * units)
     hidden, gate_delta, up_delta = (
         whole[:, :units],
         whole[:, units : 2 * units],
@@ -117,7 +120,7 @@
     ends = jnp.concatenate([forward_part, backward_part], axis=1).astype(BF16)
     ends = ends.reshape(sections, own, 2 * width)
     ends = lax.all_to_all(ends, SECTION, 0, 0)
-    ends = lax.optimization_barrier(ends.astype(F32)).sum(0).astype(BF16)
+    ends = ends.astype(F32).sum(0).astype(BF16)
     all_tokens, all_grads = both[:, :width], both[:, width:]
     gate_grads = contract_first(all_tokens, gate_delta).astype(BF16)
     up_grads = contract_first(all_tokens, up_delta).astype(BF16)

time: 172 us -> 181 us (1.052)
  blocking collectives: 11.1 us -> 35.1 us
  starting transfers between devices: 78.4 us -> 70.4 us
  other arithmetic: 7.18 us -> 2.43 us
  waiting for transfers between devices: 65.1 us -> 63.2 us
    all_to_all x0 -> x1, blocking collectives: none -> 14.5 us  [sum_over_x(): return lax.all_to_all(pieces, 'x', 0, 0).astype(F32).sum(0)]
    all_to_all x1 -> x0, waiting for transfers between devices: 10.9 us -> none  [sum_over_x(): others = lax.all_to_all(pieces.astype(BF16), 'x', 0, 0).astype(F32)]
    ppermute x4, waiting for transfers between devices: 16.2 us -> 26.9 us  [swap_far(): return lax.ppermute(part.astype(BF16), ('zh', 'core'), pairs)]
    all_gather x1 -> x2, blocking collectives: 11.1 us -> 20.6 us  [gather_over_x(): mine = lax.all_gather(block, 'x', axis=0, tiled=False)]
    all_to_all x1 -> x0, starting transfers between devices: 4.19 us -> none  [sum_over_x(): others = lax.all_to_all(pieces.astype(BF16), 'x', 0, 0).astype(F32)]
    all_to_all x1, starting transfers between devices: 9.55 us -> 6.44 us  [shards(): ends = lax.all_to_all(ends, SECTION, 0, 0)]
    ppermute x2 -> x3, waiting for transfers between devices: 3.95 us -> 2.23 us  [swap_core(): return lax.ppermute(block, 'core', [(0, 1), (1, 0)])]
    ppermute x2 -> x3, starting transfers between devices: 13.6 us -> 13.3 us  [swap_core(): return lax.ppermute(block, 'core', [(0, 1), (1, 0)])]
  transfers between devices with their start and end apart: 9 -> 9, of which waited for: 8 -> 7; matrix products, arithmetic and copies ran while one was open for 2% -> 2% of each run, Pallas kernels for 0% -> 0%
where the time goes in v4:
time: 181 us; the launch traced here: 180 us
  starting transfers between devices  70.4 us (39%)
  waiting for transfers between devices  63.2 us (35%)
  blocking collectives  35.1 us (19%)
  matrix products  6.77 us (4%)
  other arithmetic  2.43 us (1%)
    ppermute x4, starting transfers between devices, swap_far(): return lax.ppermute(part.astype(BF16), ('zh', 'core'), pairs)  34.6 us
    ppermute x4, waiting for transfers between devices, swap_far(): return lax.ppermute(part.astype(BF16), ('zh', 'core'), pairs)  26.9 us
    all_gather x2, blocking collectives, gather_over_x(): mine = lax.all_gather(block, 'x', axis=0, tiled=False)  20.6 us
    all_to_all x1, waiting for transfers between devices, shards(): both = lax.all_to_all(both, SECTION, 0, 0).reshape(rows, 2 * width)  18.6 us
    all_to_all x1, starting transfers between devices, shards(): both = lax.all_to_all(both, SECTION, 0, 0).reshape(rows, 2 * width)  16.1 us
    all_to_all x1, waiting for transfers between devices, shards(): ends = lax.all_to_all(ends, SECTION, 0, 0)  15.5 us
    all_to_all x1, blocking collectives, sum_over_x(): return lax.all_to_all(pieces, 'x', 0, 0).astype(F32).sum(0)  14.5 us
    ppermute x3, starting transfers between devices, swap_core(): return lax.ppermute(block, 'core', [(0, 1), (1, 0)])  13.3 us
  transfers between devices with their start and end apart: 9, of which 7 were waited for; matrix products, arithmetic and copies ran while one was open for 2% of the time, Pallas kernels for 0%

profile of v4, /device:TPU:1, one launch (start us, length us, event | category | flops | bytes accessed | tf_op | source)
XLA Modules:
  0.0 180.2 jit_solution(17840694091434632289)
XLA Ops:
  0.7 0.8 pad_maximum_fusion.7
  1.4 0.7 broadcast_in_dim.2
  2.2 16.1 %all-to-all-start = ((bf16[32,8,512]{2,1,0:T(8,128)(2,1)}), bf16[32,8,512]{2,1,0:T(8,128)(2,1)S(1)}, u32[]{:S(2)}, u32[]{:S(2)}) async-start(bf16[32,8,512]{2,1,0:T(8,128)(2,1)} %broadcast_in_dim.2), calls=%async_computation | async-start | bytes 524288 | tf_op jit(solution)/shard_map/all_to_all | solution.py:73
  18.3 18.6 %all-to-all-done = bf16[32,8,512]{2,1,0:T(8,128)(2,1)S(1)} async-done(((bf16[32,8,512]{2,1,0:T(8,128)(2,1)}), bf16[32,8,512]{2,1,0:T(8,128)(2,1)S(1)}, u32[]{:S(2)}, u32[]{:S(2)}) %all-to-all-start) | async-done | bytes 262176 | tf_op jit(solution)/shard_map/all_to_all | solution.py:73
  36.9 1.2 convolution_convert_fusion.4
  38.4 0.3 convolution_convert_fusion.3
  38.8 3.8 %collective-permute-start = (bf16[128,2688]{1,0:T(8,128)(2,1)S(1)}, bf16[128,2688]{1,0:T(8,128)(2,1)S(1)}, u32[]{:S(2)}, u32[]{:S(2)}) collective-permute-start(bf16[128,2688]{1,0:T(8,128)(2,1)S(1)} %pad_maximum_fusion.1), channel_id=1, source_target_pairs={{0,1},{1,0},{2,3},{3,2},{4,5},{5,4},{6,7},{7,6},{8,9},{9,8},{10,11... | collective-permute-start | bytes 2064392 | tf_op jit(solution)/shard_map/ppermute | solution.py:25
  42.6 0.3 fusion.16
  43.3 1.0 collective-permute-done
  44.4 14.5 %all_to_all.15 = bf16[4,32,2688]{2,1,0:T(8,128)(2,1)S(1)} all-to-all(bf16[4,32,2688]{2,1,0:T(8,128)(2,1)S(1)} %bitcast.47), channel_id=1, replica_groups=mesh['y'=4,'zl'=8,'zh'=4,'x'=4,'core'=2] {'x'}, dimensions={0} | all-to-all | bytes 1376256 | tf_op jit(solution)/shard_map/all_to_all | solution.py:32
  59.0 15.2 %collective-permute-start.1 = (bf16[16,2688]{1,0:T(8,128)(2,1)S(1)}, bf16[16,2688]{1,0:T(8,128)(2,1)S(1)}, u32[]{:S(2)}, u32[]{:S(2)}) collective-permute-start(bf16[16,2688]{1,0:T(8,128)(2,1)S(1)} %get-tuple-element.13), channel_id=1, source_target_pairs={{0,8},{1,25},{8,0},{9,17},{16,24},{17,9},{24,16},{25,1},{2,10},{3,... | collective-permute-start | bytes 258056 | tf_op jit(solution)/shard_map/ppermute | solution.py:41
  74.3 1.9 %collective-permute-start.3 = (bf16[16,2688]{1,0:T(8,128)(2,1)S(1)}, bf16[16,2688]{1,0:T(8,128)(2,1)S(1)}, u32[]{:S(2)}, u32[]{:S(2)}) collective-permute-start(bf16[16,2688]{1,0:T(8,128)(2,1)S(1)} %get-tuple-element.14), channel_id=1, source_target_pairs={{0,8},{1,25},{8,0},{9,17},{16,24},{17,9},{24,16},{25,1},{2,10},{3,... | collective-permute-start | bytes 258056 | tf_op jit(solution)/shard_map/ppermute | solution.py:41
  76.2 6.8 %collective-permute-done.1 = bf16[16,2688]{1,0:T(8,128)(2,1)S(1)} collective-permute-done((bf16[16,2688]{1,0:T(8,128)(2,1)S(1)}, bf16[16,2688]{1,0:T(8,128)(2,1)S(1)}, u32[]{:S(2)}, u32[]{:S(2)}) %collective-permute-start.1) | collective-permute-done | bytes 86048 | tf_op jit(solution)/shard_map/ppermute | solution.py:41
  83.0 11.1 %collective-permute-start.2 = (bf16[16,2688]{1,0:T(8,128)(2,1)S(1)}, bf16[16,2688]{1,0:T(8,128)(2,1)S(1)}, u32[]{:S(2)}, u32[]{:S(2)}) collective-permute-start(bf16[16,2688]{1,0:T(8,128)(2,1)S(1)} %get-tuple-element.9), channel_id=1, source_target_pairs={{0,24},{1,9},{8,16},{9,1},{16,8},{17,25},{24,0},{25,17},{2,26},{3,... | collective-permute-start | bytes 258056 | tf_op jit(solution)/shard_map/ppermute | solution.py:41
  94.1 9.8 %collective-permute-done.2 = bf16[16,2688]{1,0:T(8,128)(2,1)S(1)} collective-permute-done((bf16[16,2688]{1,0:T(8,128)(2,1)S(1)}, bf16[16,2688]{1,0:T(8,128)(2,1)S(1)}, u32[]{:S(2)}, u32[]{:S(2)}) %collective-permute-start.2) | collective-permute-done | bytes 86048 | tf_op jit(solution)/shard_map/ppermute | solution.py:41
  104.0 10.0 %all_gather.8 = bf16[4,16,2688]{2,1,0:T(8,128)(2,1)S(1)} all-gather(bf16[1,16,2688]{2,1,0:T(8,128)(2,1)S(1)} %pad_maximum_fusion.5), channel_id=1, replica_groups=mesh['y'=4,'zl'=8,'zh'=4,'x'=4,'core'=2] {'x'}, dimensions={0}, use_global_device_ids=true | all-gather | bytes 430080 | tf_op jit(solution)/shard_map/all_gather | solution.py:61
  113.9 7.0 %collective-permute-start.5 = (bf16[4,16,2688]{2,1,0:T(8,128)(2,1)S(1)}, bf16[4,16,2688]{2,1,0:T(8,128)(2,1)S(1)}, u32[]{:S(2)}, u32[]{:S(2)}) collective-permute-start(bf16[4,16,2688]{2,1,0:T(8,128)(2,1)S(1)} %all_gather.8), channel_id=1, source_target_pairs={{0,1},{1,0},{2,3},{3,2},{4,5},{5,4},{6,7},{7,6},{8,9},{9,8},{10,11... | collective-permute-start | bytes 1032200 | tf_op jit(solution)/shard_map/ppermute | solution.py:25
  121.0 6.4 %collective-permute-start.4 = (bf16[16,2688]{1,0:T(8,128)(2,1)S(1)}, bf16[16,2688]{1,0:T(8,128)(2,1)S(1)}, u32[]{:S(2)}, u32[]{:S(2)}) collective-permute-start(bf16[16,2688]{1,0:T(8,128)(2,1)S(1)} %fusion.14), channel_id=1, source_target_pairs={{0,24},{1,9},{8,16},{9,1},{16,8},{17,25},{24,0},{25,17},{2,26},{3,... | collective-permute-start | bytes 258056 | tf_op jit(solution)/shard_map/ppermute | solution.py:41
  127.4 10.3 %collective-permute-done.4 = bf16[16,2688]{1,0:T(8,128)(2,1)S(1)} collective-permute-done((bf16[16,2688]{1,0:T(8,128)(2,1)S(1)}, bf16[16,2688]{1,0:T(8,128)(2,1)S(1)}, u32[]{:S(2)}, u32[]{:S(2)}) %collective-permute-start.4) | collective-permute-done | bytes 86048 | tf_op jit(solution)/shard_map/ppermute | solution.py:41
  137.8 10.6 %all_gather.9 = bf16[4,16,2688]{2,1,0:T(8,128)(2,1)S(1)} all-gather(bf16[1,16,2688]{2,1,0:T(8,128)(2,1)S(1)} %pad_maximum_fusion.6), channel_id=1, replica_groups=mesh['y'=4,'zl'=8,'zh'=4,'x'=4,'core'=2] {'x'}, dimensions={0}, use_global_device_ids=true | all-gather | bytes 430080 | tf_op jit(solution)/shard_map/all_gather | solution.py:61
  148.5 2.4 %collective-permute-start.6 = (bf16[4,16,2688]{2,1,0:T(8,128)(2,1)S(1)}, bf16[4,16,2688]{2,1,0:T(8,128)(2,1)S(1)}, u32[]{:S(2)}, u32[]{:S(2)}) collective-permute-start(bf16[4,16,2688]{2,1,0:T(8,128)(2,1)S(1)} %all_gather.9), channel_id=1, source_target_pairs={{0,1},{1,0},{2,3},{3,2},{4,5},{5,4},{6,7},{7,6},{8,9},{9,8},{10,11... | collective-permute-start | bytes 1032200 | tf_op jit(solution)/shard_map/ppermute | solution.py:25
  150.9 1.3 collective-permute-done.6
  152.6 0.3 fusion.7
  152.9 0.3 fusion.2
  153.2 0.3 fusion.3
  153.5 0.7 pad_maximum_fusion.4
  154.3 6.4 %all-to-all-start.2 = ((bf16[32,8,512]{2,1,0:T(8,128)(2,1)}), bf16[32,8,512]{2,1,0:T(8,128)(2,1)S(1)}, u32[]{:S(2)}, u32[]{:S(2)}) async-start(bf16[32,8,512]{2,1,0:T(8,128)(2,1)} %pad_maximum_fusion.4), calls=%async_computation.2 | async-start | bytes 524288 | tf_op jit(solution)/shard_map/all_to_all | solution.py:122
  160.7 1.1 convolution_convert_fusion
  161.8 1.1 convolution_convert_fusion.1
  162.9 1.1 convolution_convert_fusion.2
  164.0 15.5 %all-to-all-done.2 = bf16[32,8,512]{2,1,0:T(8,128)(2,1)S(1)} async-done(((bf16[32,8,512]{2,1,0:T(8,128)(2,1)}), bf16[32,8,512]{2,1,0:T(8,128)(2,1)S(1)}, u32[]{:S(2)}, u32[]{:S(2)}) %all-to-all-start.2) | async-done | bytes 262176 | tf_op jit(solution)/shard_map/all_to_all | solution.py:122
  179.6 0.6 fusion.36
  (26 shorter events, 1.7 us)
Async XLA Ops:
  0.6 37.5 %copy-start = (bf16[256,896]{1,0:T(8,128)(2,1)S(1)}, bf16[256,896]{1,0:T(8,128)(2,1)}, u32[]{:S(2)}) copy-start(bf16[256,896]{1,0:T(8,128)(2,1)} %param.6) | copy-start | bytes 1376260
  0.6 37.7 %copy-start.2 = (bf16[896,256]{1,0:T(8,128)(2,1)S(1)}, bf16[896,256]{1,0:T(8,128)(2,1)}, u32[]{:S(2)}) copy-start(bf16[896,256]{1,0:T(8,128)(2,1)} %param.8) | copy-start | bytes 1376260
  2.2 34.7 %all-to-all-start = ((bf16[32,8,512]{2,1,0:T(8,128)(2,1)}), bf16[32,8,512]{2,1,0:T(8,128)(2,1)S(1)}, u32[]{:S(2)}, u32[]{:S(2)}) async-start(bf16[32,8,512]{2,1,0:T(8,128)(2,1)} %broadcast_in_dim.2), calls=%async_computation | async-start | bytes 524288 | tf_op jit(solution)/shard_map/all_to_all | solution.py:73
  38.4 4.5 %copy-start.1 = (bf16[256,896]{1,0:T(8,128)(2,1)S(1)}, bf16[256,896]{1,0:T(8,128)(2,1)}, u32[]{:S(2)}) copy-start(bf16[256,896]{1,0:T(8,128)(2,1)} %param.7) | copy-start | bytes 1376260
  38.8 5.5 %collective-permute-start = (bf16[128,2688]{1,0:T(8,128)(2,1)S(1)}, bf16[128,2688]{1,0:T(8,128)(2,1)S(1)}, u32[]{:S(2)}, u32[]{:S(2)}) collective-permute-start(bf16[128,2688]{1,0:T(8,128)(2,1)S(1)} %pad_maximum_fusion.1), channel_id=1, source_target_pairs={{0,1},{1,0},{2,3},{3,2},{4,5},{5,4},{6,7},{7,6},{8,9},{9,8},{10,11... | collective-permute-start | bytes 2064392 | tf_op jit(solution)/shard_map/ppermute | solution.py:25
  59.0 23.9 %collective-permute-start.1 = (bf16[16,2688]{1,0:T(8,128)(2,1)S(1)}, bf16[16,2688]{1,0:T(8,128)(2,1)S(1)}, u32[]{:S(2)}, u32[]{:S(2)}) collective-permute-start(bf16[16,2688]{1,0:T(8,128)(2,1)S(1)} %get-tuple-element.13), channel_id=1, source_target_pairs={{0,8},{1,25},{8,0},{9,17},{16,24},{17,9},{24,16},{25,1},{2,10},{3,... | collective-permute-start | bytes 258056 | tf_op jit(solution)/shard_map/ppermute | solution.py:41
  74.3 19.8 %collective-permute-start.3 = (bf16[16,2688]{1,0:T(8,128)(2,1)S(1)}, bf16[16,2688]{1,0:T(8,128)(2,1)S(1)}, u32[]{:S(2)}, u32[]{:S(2)}) collective-permute-start(bf16[16,2688]{1,0:T(8,128)(2,1)S(1)} %get-tuple-element.14), channel_id=1, source_target_pairs={{0,8},{1,25},{8,0},{9,17},{16,24},{17,9},{24,16},{25,1},{2,10},{3,... | collective-permute-start | bytes 258056 | tf_op jit(solution)/shard_map/ppermute | solution.py:41
  83.0 20.9 %collective-permute-start.2 = (bf16[16,2688]{1,0:T(8,128)(2,1)S(1)}, bf16[16,2688]{1,0:T(8,128)(2,1)S(1)}, u32[]{:S(2)}, u32[]{:S(2)}) collective-permute-start(bf16[16,2688]{1,0:T(8,128)(2,1)S(1)} %get-tuple-element.9), channel_id=1, source_target_pairs={{0,24},{1,9},{8,16},{9,1},{16,8},{17,25},{24,0},{25,17},{2,26},{3,... | collective-permute-start | bytes 258056 | tf_op jit(solution)/shard_map/ppermute | solution.py:41
  113.9 23.8 %collective-permute-start.5 = (bf16[4,16,2688]{2,1,0:T(8,128)(2,1)S(1)}, bf16[4,16,2688]{2,1,0:T(8,128)(2,1)S(1)}, u32[]{:S(2)}, u32[]{:S(2)}) collective-permute-start(bf16[4,16,2688]{2,1,0:T(8,128)(2,1)S(1)} %all_gather.8), channel_id=1, source_target_pairs={{0,1},{1,0},{2,3},{3,2},{4,5},{5,4},{6,7},{7,6},{8,9},{9,8},{10,11... | collective-permute-start | bytes 1032200 | tf_op jit(solution)/shard_map/ppermute | solution.py:25
  121.0 16.7 %collective-permute-start.4 = (bf16[16,2688]{1,0:T(8,128)(2,1)S(1)}, bf16[16,2688]{1,0:T(8,128)(2,1)S(1)}, u32[]{:S(2)}, u32[]{:S(2)}) collective-permute-start(bf16[16,2688]{1,0:T(8,128)(2,1)S(1)} %fusion.14), channel_id=1, source_target_pairs={{0,24},{1,9},{8,16},{9,1},{16,8},{17,25},{24,0},{25,17},{2,26},{3,... | collective-permute-start | bytes 258056 | tf_op jit(solution)/shard_map/ppermute | solution.py:41
  148.5 3.7 %collective-permute-start.6 = (bf16[4,16,2688]{2,1,0:T(8,128)(2,1)S(1)}, bf16[4,16,2688]{2,1,0:T(8,128)(2,1)S(1)}, u32[]{:S(2)}, u32[]{:S(2)}) collective-permute-start(bf16[4,16,2688]{2,1,0:T(8,128)(2,1)S(1)} %all_gather.9), channel_id=1, source_target_pairs={{0,1},{1,0},{2,3},{3,2},{4,5},{5,4},{6,7},{7,6},{8,9},{9,8},{10,11... | collective-permute-start | bytes 1032200 | tf_op jit(solution)/shard_map/ppermute | solution.py:25
  154.3 25.2 %all-to-all-start.2 = ((bf16[32,8,512]{2,1,0:T(8,128)(2,1)}), bf16[32,8,512]{2,1,0:T(8,128)(2,1)S(1)}, u32[]{:S(2)}, u32[]{:S(2)}) async-start(bf16[32,8,512]{2,1,0:T(8,128)(2,1)} %pad_maximum_fusion.4), calls=%async_computation.2 | async-start | bytes 524288 | tf_op jit(solution)/shard_map/all_to_all | solution.py:122

commit v5 on v4

--- a/solution.py
+++ b/solution.py
@@ -1,6 +1,8 @@
 import jax
 import jax.numpy as jnp
 from jax import lax
+from jax.experimental import pallas as pl
+from jax.experimental.pallas import tpu as pltpu
 from jax.sharding import Mesh, PartitionSpec as P
 
 SECTION = ("y", "zl")
@@ -19,6 +21,29 @@
     return lax.dot_general(
         left, right, (((0,), (0,)), ((), ())), preferred_element_type=F32
     )
+
+
+def held(*arrays):
+    count = len(arrays)
+
+    def body(*refs):
+        sources, targets, done = refs[:count], refs[count:-1], refs[-1]
+        copies = [
+            pltpu.make_async_copy(source, target, done.at[i])
+            for i, (source, target) in enumerate(zip(sources, targets))
+        ]
+        for copy in copies:
+            copy.start()
+        for copy in copies:
+            copy.wait()
+
+    return pl.pallas_call(
+        body,
+        out_shape=[pltpu.VMEM(a.shape, a.dtype) for a in arrays],
+        in_specs=[pl.BlockSpec(memory_space=pl.ANY)] * count,
+        out_specs=[pl.BlockSpec(memory_space=pltpu.VMEM)] * count,
+        scratch_shapes=[pltpu.SemaphoreType.DMA((count,))],
+    )(*arrays)
 
 
 def swap_core(block):
@@ -57,9 +82,9 @@
     return jnp.concatenate([hidden, gate_delta, up_delta], axis=1).astype(BF16)
 
 
-def gather_over_x(block):
-    mine = lax.all_gather(block, "x", axis=0, tiled=False)
-    return mine, swap_core(mine)
+def copies_over_x(block):
+    copies = jnp.broadcast_to(block[None], (lax.axis_size("x"),) + block.shape)
+    return lax.all_to_all(copies, "x", 0, 0)
 
 
 def shards(tokens, gate_weight, up_weight, down_weight, out_grad):
@@ -68,8 +93,11 @@
     sections = lax.axis_size(SECTION)
     rows = own * sections
     half = rows // 2
-    both = jnp.concatenate([tokens, out_grad], axis=1)
-    both = jnp.broadcast_to(both[None], (sections, own, 2 * width))
+    gate_weight, up_weight, down_weight = held(gate_weight, up_weight, down_weight)
+    copies = (sections, own, width)
+    both = jnp.concatenate(
+        [jnp.broadcast_to(tokens, copies), jnp.broadcast_to(out_grad, copies)], axis=2
+    )
     both = lax.all_to_all(both, SECTION, 0, 0).reshape(rows, 2 * width)
 
     core = lax.axis_index("core")
@@ -98,10 +126,13 @@
     low = low + low_in
     low_in = swap_far(low, (3, 1))
     top = deltas_of(top + top_in)
-    top_mine, top_theirs = gather_over_x(top)
-    low_in, _ = lax.optimization_barrier((low_in, top_theirs))
+    top_mine = lax.all_gather(top, "x", axis=0, tiled=False)
+    top_theirs = swap_core(top_mine)
+    low_in, _ = lax.optimization_barrier((low_in, top_mine))
     low = deltas_of(low + low_in)
-    low_mine, low_theirs = gather_over_x(low)
+    low, _ = lax.optimization_barrier((low, top_theirs))
+    low_mine = copies_over_x(low)
+    low_theirs = swap_core(low_mine)
     mine = jnp.concatenate([top_mine, low_mine], axis=1)
     theirs = jnp.concatenate([top_theirs, low_theirs], axis=1)
     first = core == 0

time: 181 us -> 168 us (0.928)
  waiting for transfers between devices: 63.2 us -> 50.1 us
    ppermute x4, waiting for transfers between devices: 26.9 us -> 13.7 us  [swap_far(): return lax.ppermute(part.astype(BF16), ('zh', 'core'), pairs)]
    all_gather x2 -> x1, blocking collectives: 20.6 us -> 10.3 us  [shards(): top_mine = lax.all_gather(top, 'x', axis=0, tiled=False)]
    all_to_all x0 -> x1, blocking collectives: none -> 9.21 us  [copies_over_x(): return lax.all_to_all(copies, 'x', 0, 0)]
    ppermute x3, starting transfers between devices: 13.3 us -> 16.2 us  [swap_core(): return lax.ppermute(block, 'core', [(0, 1), (1, 0)])]
    all_to_all x1, starting transfers between devices: 6.44 us -> 3.87 us  [shards(): ends = lax.all_to_all(ends, SECTION, 0, 0)]
  transfers between devices with their start and end apart: 9 -> 9, of which waited for: 7 -> 7; matrix products, arithmetic and copies ran while one was open for 2% -> 3% of each run, Pallas kernels for 0% -> 1%
where the time goes in v5:
time: 168 us; the launch traced here: 167 us
  starting transfers between devices  70.9 us (42%)
  waiting for transfers between devices  50.1 us (30%)
  blocking collectives  34 us (20%)
  matrix products  5.75 us (3%)
  other arithmetic  2.36 us (1%)
  local copies, waits for them, and re-layouts  2.04 us (1%)
    ppermute x4, starting transfers between devices, swap_far(): return lax.ppermute(part.astype(BF16), ('zh', 'core'), pairs)  34.8 us
    all_to_all x1, waiting for transfers between devices, shards(): both = lax.all_to_all(both, SECTION, 0, 0).reshape(rows, 2 * width)  17.3 us
    ppermute x3, starting transfers between devices, swap_core(): return lax.ppermute(block, 'core', [(0, 1), (1, 0)])  16.2 us
    all_to_all x1, starting transfers between devices, shards(): both = lax.all_to_all(both, SECTION, 0, 0).reshape(rows, 2 * width)  16.1 us
    all_to_all x1, waiting for transfers between devices, shards(): ends = lax.all_to_all(ends, SECTION, 0, 0)  15.7 us
    all_to_all x1, blocking collectives, sum_over_x(): return lax.all_to_all(pieces, 'x', 0, 0).astype(F32).sum(0)  14.5 us
    ppermute x4, waiting for transfers between devices, swap_far(): return lax.ppermute(part.astype(BF16), ('zh', 'core'), pairs)  13.7 us
    all_gather x1, blocking collectives, shards(): top_mine = lax.all_gather(top, 'x', axis=0, tiled=False)  10.3 us
  transfers between devices with their start and end apart: 9, of which 7 were waited for; matrix products, arithmetic and copies ran while one was open for 3% of the time, Pallas kernels for 1%

profile of v5, /device:TPU:1, one launch (start us, length us, event | category | flops | bytes accessed | tf_op | source)
XLA Modules:
  0.0 167.3 jit_solution(14460201294445481571)
XLA Ops:
  0.6 0.7 broadcast_in_dim.12
  1.3 0.7 broadcast_in_dim.13
  2.0 0.7 pad_maximum_fusion.4
  2.8 16.1 %all-to-all-start = ((bf16[32,8,512]{2,1,0:T(8,128)(2,1)}), bf16[32,8,512]{2,1,0:T(8,128)(2,1)S(1)}, u32[]{:S(2)}, u32[]{:S(2)}) async-start(bf16[32,8,512]{2,1,0:T(8,128)(2,1)} %pad_maximum_fusion.4), calls=%async_computation | async-start | bytes 524288 | tf_op jit(solution)/shard_map/all_to_all | solution.py:101
  18.9 1.3 shard_map.92
  20.2 17.3 %all-to-all-done = bf16[32,8,512]{2,1,0:T(8,128)(2,1)S(1)} async-done(((bf16[32,8,512]{2,1,0:T(8,128)(2,1)}), bf16[32,8,512]{2,1,0:T(8,128)(2,1)S(1)}, u32[]{:S(2)}, u32[]{:S(2)}) %all-to-all-start) | async-done | bytes 262176 | tf_op jit(solution)/shard_map/all_to_all | solution.py:101
  38.0 0.3 convolution_convert_fusion.3
  38.3 3.8 %collective-permute-start = (bf16[128,2688]{1,0:T(8,128)(2,1)S(1)}, bf16[128,2688]{1,0:T(8,128)(2,1)S(1)}, u32[]{:S(2)}, u32[]{:S(2)}) collective-permute-start(bf16[128,2688]{1,0:T(8,128)(2,1)S(1)} %pad_maximum_fusion.1), channel_id=1, source_target_pairs={{0,1},{1,0},{2,3},{3,2},{4,5},{5,4},{6,7},{7,6},{8,9},{9,8},{10,11... | collective-permute-start | bytes 2064392 | tf_op jit(solution)/shard_map/ppermute | solution.py:50
  42.9 1.0 collective-permute-done
  44.0 14.5 %all_to_all.20 = bf16[4,32,2688]{2,1,0:T(8,128)(2,1)S(1)} all-to-all(bf16[4,32,2688]{2,1,0:T(8,128)(2,1)S(1)} %bitcast.41), channel_id=1, replica_groups=mesh['y'=4,'zl'=8,'zh'=4,'x'=4,'core'=2] {'x'}, dimensions={0} | all-to-all | bytes 1376256 | tf_op jit(solution)/shard_map/all_to_all | solution.py:57
  58.6 15.2 %collective-permute-start.1 = (bf16[16,2688]{1,0:T(8,128)(2,1)S(1)}, bf16[16,2688]{1,0:T(8,128)(2,1)S(1)}, u32[]{:S(2)}, u32[]{:S(2)}) collective-permute-start(bf16[16,2688]{1,0:T(8,128)(2,1)S(1)} %get-tuple-element.21), channel_id=1, source_target_pairs={{0,8},{1,25},{8,0},{9,17},{16,24},{17,9},{24,16},{25,1},{2,10},{3,... | collective-permute-start | bytes 258056 | tf_op jit(solution)/shard_map/ppermute | solution.py:66
  73.8 1.9 %collective-permute-start.3 = (bf16[16,2688]{1,0:T(8,128)(2,1)S(1)}, bf16[16,2688]{1,0:T(8,128)(2,1)S(1)}, u32[]{:S(2)}, u32[]{:S(2)}) collective-permute-start(bf16[16,2688]{1,0:T(8,128)(2,1)S(1)} %get-tuple-element.22), channel_id=1, source_target_pairs={{0,8},{1,25},{8,0},{9,17},{16,24},{17,9},{24,16},{25,1},{2,10},{3,... | collective-permute-start | bytes 258056 | tf_op jit(solution)/shard_map/ppermute | solution.py:66
  75.7 6.8 %collective-permute-done.1 = bf16[16,2688]{1,0:T(8,128)(2,1)S(1)} collective-permute-done((bf16[16,2688]{1,0:T(8,128)(2,1)S(1)}, bf16[16,2688]{1,0:T(8,128)(2,1)S(1)}, u32[]{:S(2)}, u32[]{:S(2)}) %collective-permute-start.1) | collective-permute-done | bytes 86048 | tf_op jit(solution)/shard_map/ppermute | solution.py:66
  82.6 11.1 %collective-permute-start.2 = (bf16[16,2688]{1,0:T(8,128)(2,1)S(1)}, bf16[16,2688]{1,0:T(8,128)(2,1)S(1)}, u32[]{:S(2)}, u32[]{:S(2)}) collective-permute-start(bf16[16,2688]{1,0:T(8,128)(2,1)S(1)} %get-tuple-element.17), channel_id=1, source_target_pairs={{0,24},{1,9},{8,16},{9,1},{16,8},{17,25},{24,0},{25,17},{2,26},{3,... | collective-permute-start | bytes 258056 | tf_op jit(solution)/shard_map/ppermute | solution.py:66
  93.7 6.6 %collective-permute-start.4 = (bf16[16,2688]{1,0:T(8,128)(2,1)S(1)}, bf16[16,2688]{1,0:T(8,128)(2,1)S(1)}, u32[]{:S(2)}, u32[]{:S(2)}) collective-permute-start(bf16[16,2688]{1,0:T(8,128)(2,1)S(1)} %fusion.14), channel_id=1, source_target_pairs={{0,24},{1,9},{8,16},{9,1},{16,8},{17,25},{24,0},{25,17},{2,26},{3,... | collective-permute-start | bytes 258056 | tf_op jit(solution)/shard_map/ppermute | solution.py:66
  100.3 6.9 %collective-permute-done.2 = bf16[16,2688]{1,0:T(8,128)(2,1)S(1)} collective-permute-done((bf16[16,2688]{1,0:T(8,128)(2,1)S(1)}, bf16[16,2688]{1,0:T(8,128)(2,1)S(1)}, u32[]{:S(2)}, u32[]{:S(2)}) %collective-permute-start.2) | collective-permute-done | bytes 86048 | tf_op jit(solution)/shard_map/ppermute | solution.py:66
  107.2 10.3 %all_gather.4 = bf16[4,16,2688]{2,1,0:T(8,128)(2,1)S(1)} all-gather(bf16[1,16,2688]{2,1,0:T(8,128)(2,1)S(1)} %pad_maximum_fusion.6), channel_id=1, replica_groups=mesh['y'=4,'zl'=8,'zh'=4,'x'=4,'core'=2] {'x'}, dimensions={0}, use_global_device_ids=true | all-gather | bytes 430080 | tf_op jit(solution)/shard_map/all_gather | solution.py:129
  117.5 8.8 %collective-permute-start.5 = (bf16[4,16,2688]{2,1,0:T(8,128)(2,1)S(1)}, bf16[4,16,2688]{2,1,0:T(8,128)(2,1)S(1)}, u32[]{:S(2)}, u32[]{:S(2)}) collective-permute-start(bf16[4,16,2688]{2,1,0:T(8,128)(2,1)S(1)} %all_gather.4), channel_id=1, source_target_pairs={{0,1},{1,0},{2,3},{3,2},{4,5},{5,4},{6,7},{7,6},{8,9},{9,8},{10,11... | collective-permute-start | bytes 1032200 | tf_op jit(solution)/shard_map/ppermute | solution.py:50
  126.5 1.1 collective-permute-done.5
  127.6 9.2 %all_to_all.21 = bf16[4,16,2688]{2,1,0:T(8,128)(2,1)S(1)} all-to-all(bf16[4,16,2688]{2,1,0:T(8,128)(2,1)S(1)} %broadcast_in_dim.14), channel_id=1, replica_groups=mesh['y'=4,'zl'=8,'zh'=4,'x'=4,'core'=2] {'x'}, dimensions={0} | all-to-all | bytes 688128 | tf_op jit(solution)/shard_map/all_to_all | solution.py:87
  136.9 3.6 %collective-permute-start.6 = (bf16[4,16,2688]{2,1,0:T(8,128)(2,1)S(1)}, bf16[4,16,2688]{2,1,0:T(8,128)(2,1)S(1)}, u32[]{:S(2)}, u32[]{:S(2)}) collective-permute-start(bf16[4,16,2688]{2,1,0:T(8,128)(2,1)S(1)} %all_to_all.21), channel_id=1, source_target_pairs={{0,1},{1,0},{2,3},{3,2},{4,5},{5,4},{6,7},{7,6},{8,9},{9,8},{10,11... | collective-permute-start | bytes 1032200 | tf_op jit(solution)/shard_map/ppermute | solution.py:50
  140.4 1.3 collective-permute-done.6
  142.1 0.3 fusion.2
  142.4 0.3 fusion.7
  142.7 0.3 fusion.3
  143.1 0.7 pad_maximum_fusion.5
  143.8 3.9 %all-to-all-start.3 = ((bf16[32,8,512]{2,1,0:T(8,128)(2,1)}), bf16[32,8,512]{2,1,0:T(8,128)(2,1)S(1)}, u32[]{:S(2)}, u32[]{:S(2)}) async-start(bf16[32,8,512]{2,1,0:T(8,128)(2,1)} %pad_maximum_fusion.5), calls=%async_computation.3 | async-start | bytes 524288 | tf_op jit(solution)/shard_map/all_to_all | solution.py:153
  147.7 1.1 convolution_convert_fusion
  148.8 1.1 convolution_convert_fusion.1
  149.9 1.1 convolution_convert_fusion.2
  150.9 15.7 %all-to-all-done.3 = bf16[32,8,512]{2,1,0:T(8,128)(2,1)S(1)} async-done(((bf16[32,8,512]{2,1,0:T(8,128)(2,1)}), bf16[32,8,512]{2,1,0:T(8,128)(2,1)S(1)}, u32[]{:S(2)}, u32[]{:S(2)}) %all-to-all-start.3) | async-done | bytes 262176 | tf_op jit(solution)/shard_map/all_to_all | solution.py:153
  166.7 0.6 fusion.33
  (23 shorter events, 2.2 us)
Async XLA Ops:
  2.8 34.7 %all-to-all-start = ((bf16[32,8,512]{2,1,0:T(8,128)(2,1)}), bf16[32,8,512]{2,1,0:T(8,128)(2,1)S(1)}, u32[]{:S(2)}, u32[]{:S(2)}) async-start(bf16[32,8,512]{2,1,0:T(8,128)(2,1)} %pad_maximum_fusion.4), calls=%async_computation | async-start | bytes 524288 | tf_op jit(solution)/shard_map/all_to_all | solution.py:101
  38.3 5.5 %collective-permute-start = (bf16[128,2688]{1,0:T(8,128)(2,1)S(1)}, bf16[128,2688]{1,0:T(8,128)(2,1)S(1)}, u32[]{:S(2)}, u32[]{:S(2)}) collective-permute-start(bf16[128,2688]{1,0:T(8,128)(2,1)S(1)} %pad_maximum_fusion.1), channel_id=1, source_target_pairs={{0,1},{1,0},{2,3},{3,2},{4,5},{5,4},{6,7},{7,6},{8,9},{9,8},{10,11... | collective-permute-start | bytes 2064392 | tf_op jit(solution)/shard_map/ppermute | solution.py:50
  58.6 23.9 %collective-permute-start.1 = (bf16[16,2688]{1,0:T(8,128)(2,1)S(1)}, bf16[16,2688]{1,0:T(8,128)(2,1)S(1)}, u32[]{:S(2)}, u32[]{:S(2)}) collective-permute-start(bf16[16,2688]{1,0:T(8,128)(2,1)S(1)} %get-tuple-element.21), channel_id=1, source_target_pairs={{0,8},{1,25},{8,0},{9,17},{16,24},{17,9},{24,16},{25,1},{2,10},{3,... | collective-permute-start | bytes 258056 | tf_op jit(solution)/shard_map/ppermute | solution.py:66
  73.8 19.8 %collective-permute-start.3 = (bf16[16,2688]{1,0:T(8,128)(2,1)S(1)}, bf16[16,2688]{1,0:T(8,128)(2,1)S(1)}, u32[]{:S(2)}, u32[]{:S(2)}) collective-permute-start(bf16[16,2688]{1,0:T(8,128)(2,1)S(1)} %get-tuple-element.22), channel_id=1, source_target_pairs={{0,8},{1,25},{8,0},{9,17},{16,24},{17,9},{24,16},{25,1},{2,10},{3,... | collective-permute-start | bytes 258056 | tf_op jit(solution)/shard_map/ppermute | solution.py:66
  82.6 24.6 %collective-permute-start.2 = (bf16[16,2688]{1,0:T(8,128)(2,1)S(1)}, bf16[16,2688]{1,0:T(8,128)(2,1)S(1)}, u32[]{:S(2)}, u32[]{:S(2)}) collective-permute-start(bf16[16,2688]{1,0:T(8,128)(2,1)S(1)} %get-tuple-element.17), channel_id=1, source_target_pairs={{0,24},{1,9},{8,16},{9,1},{16,8},{17,25},{24,0},{25,17},{2,26},{3,... | collective-permute-start | bytes 258056 | tf_op jit(solution)/shard_map/ppermute | solution.py:66
  93.7 32.7 %collective-permute-start.4 = (bf16[16,2688]{1,0:T(8,128)(2,1)S(1)}, bf16[16,2688]{1,0:T(8,128)(2,1)S(1)}, u32[]{:S(2)}, u32[]{:S(2)}) collective-permute-start(bf16[16,2688]{1,0:T(8,128)(2,1)S(1)} %fusion.14), channel_id=1, source_target_pairs={{0,24},{1,9},{8,16},{9,1},{16,8},{17,25},{24,0},{25,17},{2,26},{3,... | collective-permute-start | bytes 258056 | tf_op jit(solution)/shard_map/ppermute | solution.py:66
  117.5 10.1 %collective-permute-start.5 = (bf16[4,16,2688]{2,1,0:T(8,128)(2,1)S(1)}, bf16[4,16,2688]{2,1,0:T(8,128)(2,1)S(1)}, u32[]{:S(2)}, u32[]{:S(2)}) collective-permute-start(bf16[4,16,2688]{2,1,0:T(8,128)(2,1)S(1)} %all_gather.4), channel_id=1, source_target_pairs={{0,1},{1,0},{2,3},{3,2},{4,5},{5,4},{6,7},{7,6},{8,9},{9,8},{10,11... | collective-permute-start | bytes 1032200 | tf_op jit(solution)/shard_map/ppermute | solution.py:50
  136.9 4.8 %collective-permute-start.6 = (bf16[4,16,2688]{2,1,0:T(8,128)(2,1)S(1)}, bf16[4,16,2688]{2,1,0:T(8,128)(2,1)S(1)}, u32[]{:S(2)}, u32[]{:S(2)}) collective-permute-start(bf16[4,16,2688]{2,1,0:T(8,128)(2,1)S(1)} %all_to_all.21), channel_id=1, source_target_pairs={{0,1},{1,0},{2,3},{3,2},{4,5},{5,4},{6,7},{7,6},{8,9},{9,8},{10,11... | collective-permute-start | bytes 1032200 | tf_op jit(solution)/shard_map/ppermute | solution.py:50
  143.8 22.9 %all-to-all-start.3 = ((bf16[32,8,512]{2,1,0:T(8,128)(2,1)}), bf16[32,8,512]{2,1,0:T(8,128)(2,1)S(1)}, u32[]{:S(2)}, u32[]{:S(2)}) async-start(bf16[32,8,512]{2,1,0:T(8,128)(2,1)} %pad_maximum_fusion.5), calls=%async_computation.3 | async-start | bytes 524288 | tf_op jit(solution)/shard_map/all_to_all | solution.py:153

commit v6 on v5

--- a/solution.py
+++ b/solution.py
@@ -44,6 +44,21 @@
         out_specs=[pl.BlockSpec(memory_space=pltpu.VMEM)] * count,
         scratch_shapes=[pltpu.SemaphoreType.DMA((count,))],
     )(*arrays)
+
+
+def side_by_side(left, right, count):
+    rows, width = left.shape
+
+    def body(left_ref, right_ref, out_ref):
+        pair = jnp.concatenate([left_ref[...], right_ref[...]], axis=1)
+        out_ref[...] = jnp.broadcast_to(pair[None], (count, rows, 2 * width))
+
+    return pl.pallas_call(
+        body,
+        out_shape=pltpu.VMEM((count, rows, 2 * width), left.dtype),
+        in_specs=[pl.BlockSpec(memory_space=pltpu.VMEM)] * 2,
+        out_specs=pl.BlockSpec(memory_space=pltpu.VMEM),
+    )(left, right)
 
 
 def swap_core(block):
@@ -94,10 +109,7 @@
     rows = own * sections
     half = rows // 2
     gate_weight, up_weight, down_weight = held(gate_weight, up_weight, down_weight)
-    copies = (sections, own, width)
-    both = jnp.concatenate(
-        [jnp.broadcast_to(tokens, copies), jnp.broadcast_to(out_grad, copies)], axis=2
-    )
+    both = side_by_side(tokens, out_grad, sections)
     both = lax.all_to_all(both, SECTION, 0, 0).reshape(rows, 2 * width)
 
     core = lax.axis_index("core")
@@ -125,16 +137,8 @@
     top_in = swap_far(top, (3, 1))
     low = low + low_in
     low_in = swap_far(low, (3, 1))
-    top = deltas_of(top + top_in)
-    top_mine = lax.all_gather(top, "x", axis=0, tiled=False)
-    top_theirs = swap_core(top_mine)
-    low_in, _ = lax.optimization_barrier((low_in, top_mine))
-    low = deltas_of(low + low_in)
-    low, _ = lax.optimization_barrier((low, top_theirs))
-    low_mine = copies_over_x(low)
-    low_theirs = swap_core(low_mine)
-    mine = jnp.concatenate([top_mine, low_mine], axis=1)
-    theirs = jnp.concatenate([top_theirs, low_theirs], axis=1)
+    mine = copies_over_x(deltas_of(jnp.concatenate([top + top_in, low + low_in])))
+    theirs = swap_core(mine)
     first = core == 0
     whole = jnp.stack(
         [jnp.where(first, mine, theirs), jnp.where(first, theirs, mine)]

time: 168 us -> 162 us (0.964)
  blocking collectives: 34 us -> 24.7 us
  waiting for transfers between devices: 50.1 us -> 52.8 us
  starting transfers between devices: 70.9 us -> 72.6 us
    all_gather x1 -> x0, blocking collectives: 10.3 us -> none  [shards(): top_mine = lax.all_gather(top, 'x', axis=0, tiled=False)]
    all_to_all x1, starting transfers between devices: 3.87 us -> 10.8 us  [shards(): ends = lax.all_to_all(ends, SECTION, 0, 0)]
    ppermute x3 -> x2, starting transfers between devices: 16.2 us -> 11 us  [swap_core(): return lax.ppermute(block, 'core', [(0, 1), (1, 0)])]
    ppermute x4, waiting for transfers between devices: 13.7 us -> 17.3 us  [swap_far(): return lax.ppermute(part.astype(BF16), ('zh', 'core'), pairs)]
    ppermute x3 -> x2, waiting for transfers between devices: 3.37 us -> 2.73 us  [swap_core(): return lax.ppermute(block, 'core', [(0, 1), (1, 0)])]
  transfers between devices with their start and end apart: 9 -> 8, of which waited for: 7 -> 7; matrix products, arithmetic and copies ran while one was open for 3% -> 3% of each run, Pallas kernels for 1% -> 1%
where the time goes in v6:
time: 162 us
  starting transfers between devices  72.6 us (45%)
  waiting for transfers between devices  52.8 us (33%)
  blocking collectives  24.7 us (15%)
  matrix products  5.76 us (4%)
  Pallas kernels  2.75 us (2%)
    ppermute x4, starting transfers between devices, swap_far(): return lax.ppermute(part.astype(BF16), ('zh', 'core'), pairs)  34.8 us
    ppermute x4, waiting for transfers between devices, swap_far(): return lax.ppermute(part.astype(BF16), ('zh', 'core'), pairs)  17.3 us
    all_to_all x1, waiting for transfers between devices, shards(): both = lax.all_to_all(both, SECTION, 0, 0).reshape(rows, 2 * width)  17.3 us
    all_to_all x1, starting transfers between devices, shards(): both = lax.all_to_all(both, SECTION, 0, 0).reshape(rows, 2 * width)  16.1 us
    all_to_all x1, waiting for transfers between devices, shards(): ends = lax.all_to_all(ends, SECTION, 0, 0)  15.5 us
    all_to_all x1, blocking collectives, sum_over_x(): return lax.all_to_all(pieces, 'x', 0, 0).astype(F32).sum(0)  14.5 us
    ppermute x2, starting transfers between devices, swap_core(): return lax.ppermute(block, 'core', [(0, 1), (1, 0)])  11 us
    all_to_all x1, starting transfers between devices, shards(): ends = lax.all_to_all(ends, SECTION, 0, 0)  10.8 us
  transfers between devices with their start and end apart: 8, of which 7 were waited for; matrix products, arithmetic and copies ran while one was open for 3% of the time, Pallas kernels for 1%

profile of v6, /device:TPU:1, one launch (start us, length us, event | category | flops | bytes accessed | tf_op | source)
XLA Modules:
  0.0 161.6 jit_solution(1669925117056246213)
XLA Ops:
  0.6 1.4 shard_map.92
  2.1 16.1 %all-to-all-start = ((bf16[32,8,512]{2,1,0:T(8,128)(2,1)}), bf16[32,8,512]{2,1,0:T(8,128)(2,1)S(1)}, u32[]{:S(2)}, u32[]{:S(2)}) async-start(bf16[32,8,512]{2,1,0:T(8,128)(2,1)} %shard_map.92), calls=%async_computation | async-start | bytes 524288 | tf_op jit(solution)/shard_map/all_to_all | solution.py:113
  18.2 1.3 shard_map.93
  19.5 17.3 %all-to-all-done = bf16[32,8,512]{2,1,0:T(8,128)(2,1)S(1)} async-done(((bf16[32,8,512]{2,1,0:T(8,128)(2,1)}), bf16[32,8,512]{2,1,0:T(8,128)(2,1)S(1)}, u32[]{:S(2)}, u32[]{:S(2)}) %all-to-all-start) | async-done | bytes 262176 | tf_op jit(solution)/shard_map/all_to_all | solution.py:113
  37.0 0.2 convolution_convert_fusion.5
  37.3 0.3 convolution_convert_fusion.3
  37.6 3.8 %collective-permute-start = (bf16[128,2688]{1,0:T(8,128)(2,1)S(1)}, bf16[128,2688]{1,0:T(8,128)(2,1)S(1)}, u32[]{:S(2)}, u32[]{:S(2)}) collective-permute-start(bf16[128,2688]{1,0:T(8,128)(2,1)S(1)} %pad_maximum_fusion.1), channel_id=1, source_target_pairs={{0,1},{1,0},{2,3},{3,2},{4,5},{5,4},{6,7},{7,6},{8,9},{9,8},{10,11... | collective-permute-start | bytes 2064392 | tf_op jit(solution)/shard_map/ppermute | solution.py:65
  41.4 0.3 fusion.18
  41.7 0.2 fusion.22
  41.9 0.2 fusion.24
  42.2 1.0 collective-permute-done
  43.3 14.5 %all_to_all.20 = bf16[4,32,2688]{2,1,0:T(8,128)(2,1)S(1)} all-to-all(bf16[4,32,2688]{2,1,0:T(8,128)(2,1)S(1)} %bitcast.35), channel_id=1, replica_groups=mesh['y'=4,'zl'=8,'zh'=4,'x'=4,'core'=2] {'x'}, dimensions={0} | all-to-all | bytes 1376256 | tf_op jit(solution)/shard_map/all_to_all | solution.py:72
  57.9 15.2 %collective-permute-start.1 = (bf16[16,2688]{1,0:T(8,128)(2,1)S(1)}, bf16[16,2688]{1,0:T(8,128)(2,1)S(1)}, u32[]{:S(2)}, u32[]{:S(2)}) collective-permute-start(bf16[16,2688]{1,0:T(8,128)(2,1)S(1)} %get-tuple-element.20), channel_id=1, source_target_pairs={{0,8},{1,25},{8,0},{9,17},{16,24},{17,9},{24,16},{25,1},{2,10},{3,... | collective-permute-start | bytes 258056 | tf_op jit(solution)/shard_map/ppermute | solution.py:81
  73.1 1.9 %collective-permute-start.3 = (bf16[16,2688]{1,0:T(8,128)(2,1)S(1)}, bf16[16,2688]{1,0:T(8,128)(2,1)S(1)}, u32[]{:S(2)}, u32[]{:S(2)}) collective-permute-start(bf16[16,2688]{1,0:T(8,128)(2,1)S(1)} %get-tuple-element.21), channel_id=1, source_target_pairs={{0,8},{1,25},{8,0},{9,17},{16,24},{17,9},{24,16},{25,1},{2,10},{3,... | collective-permute-start | bytes 258056 | tf_op jit(solution)/shard_map/ppermute | solution.py:81
  75.0 6.8 %collective-permute-done.1 = bf16[16,2688]{1,0:T(8,128)(2,1)S(1)} collective-permute-done((bf16[16,2688]{1,0:T(8,128)(2,1)S(1)}, bf16[16,2688]{1,0:T(8,128)(2,1)S(1)}, u32[]{:S(2)}, u32[]{:S(2)}) %collective-permute-start.1) | collective-permute-done | bytes 86048 | tf_op jit(solution)/shard_map/ppermute | solution.py:81
  81.9 11.1 %collective-permute-start.2 = (bf16[16,2688]{1,0:T(8,128)(2,1)S(1)}, bf16[16,2688]{1,0:T(8,128)(2,1)S(1)}, u32[]{:S(2)}, u32[]{:S(2)}) collective-permute-start(bf16[16,2688]{1,0:T(8,128)(2,1)S(1)} %get-tuple-element.13), channel_id=1, source_target_pairs={{0,24},{1,9},{8,16},{9,1},{16,8},{17,25},{24,0},{25,17},{2,26},{3,... | collective-permute-start | bytes 258056 | tf_op jit(solution)/shard_map/ppermute | solution.py:81
  93.0 6.6 %collective-permute-start.4 = (bf16[16,2688]{1,0:T(8,128)(2,1)S(1)}, bf16[16,2688]{1,0:T(8,128)(2,1)S(1)}, u32[]{:S(2)}, u32[]{:S(2)}) collective-permute-start(bf16[16,2688]{1,0:T(8,128)(2,1)S(1)} %fusion.16), channel_id=1, source_target_pairs={{0,24},{1,9},{8,16},{9,1},{16,8},{17,25},{24,0},{25,17},{2,26},{3,... | collective-permute-start | bytes 258056 | tf_op jit(solution)/shard_map/ppermute | solution.py:81
  99.6 7.2 %collective-permute-done.2 = bf16[16,2688]{1,0:T(8,128)(2,1)S(1)} collective-permute-done((bf16[16,2688]{1,0:T(8,128)(2,1)S(1)}, bf16[16,2688]{1,0:T(8,128)(2,1)S(1)}, u32[]{:S(2)}, u32[]{:S(2)}) %collective-permute-start.2) | collective-permute-done | bytes 86048 | tf_op jit(solution)/shard_map/ppermute | solution.py:81
  106.8 3.3 %collective-permute-done.4 = bf16[16,2688]{1,0:T(8,128)(2,1)S(1)} collective-permute-done((bf16[16,2688]{1,0:T(8,128)(2,1)S(1)}, bf16[16,2688]{1,0:T(8,128)(2,1)S(1)}, u32[]{:S(2)}, u32[]{:S(2)}) %collective-permute-start.4) | collective-permute-done | bytes 86048 | tf_op jit(solution)/shard_map/ppermute | solution.py:81
  110.3 10.2 %all_to_all.21 = bf16[4,32,2688]{2,1,0:T(8,128)(2,1)S(1)} all-to-all(bf16[4,32,2688]{2,1,0:T(8,128)(2,1)S(1)} %broadcast_in_dim.2), channel_id=1, replica_groups=mesh['y'=4,'zl'=8,'zh'=4,'x'=4,'core'=2] {'x'}, dimensions={0} | all-to-all | bytes 1376256 | tf_op jit(solution)/shard_map/all_to_all | solution.py:102
  120.5 7.2 %collective-permute-start.5 = (bf16[4,32,2688]{2,1,0:T(8,128)(2,1)S(1)}, bf16[4,32,2688]{2,1,0:T(8,128)(2,1)S(1)}, u32[]{:S(2)}, u32[]{:S(2)}) collective-permute-start(bf16[4,32,2688]{2,1,0:T(8,128)(2,1)S(1)} %all_to_all.21), channel_id=1, source_target_pairs={{0,1},{1,0},{2,3},{3,2},{4,5},{5,4},{6,7},{7,6},{8,9},{9,8},{10,11... | collective-permute-start | bytes 2064392 | tf_op jit(solution)/shard_map/ppermute | solution.py:65
  127.7 1.7 %collective-permute-done.5 = bf16[4,32,2688]{2,1,0:T(8,128)(2,1)S(1)} collective-permute-done((bf16[4,32,2688]{2,1,0:T(8,128)(2,1)S(1)}, bf16[4,32,2688]{2,1,0:T(8,128)(2,1)S(1)}, u32[]{:S(2)}, u32[]{:S(2)}) %collective-permute-start.5) | collective-permute-done | bytes 688160 | tf_op jit(solution)/shard_map/ppermute | solution.py:65
  129.7 0.3 fusion.2
  130.0 0.3 fusion.7
  130.4 0.3 fusion.3
  130.7 0.7 pad_maximum_fusion.2
  131.4 10.8 %all-to-all-start.3 = ((bf16[32,8,512]{2,1,0:T(8,128)(2,1)}), bf16[32,8,512]{2,1,0:T(8,128)(2,1)S(1)}, u32[]{:S(2)}, u32[]{:S(2)}) async-start(bf16[32,8,512]{2,1,0:T(8,128)(2,1)} %pad_maximum_fusion.2), calls=%async_computation.3 | async-start | bytes 524288 | tf_op jit(solution)/shard_map/all_to_all | solution.py:157
  142.2 1.1 convolution_convert_fusion
  143.3 1.1 convolution_convert_fusion.1
  144.4 1.1 convolution_convert_fusion.2
  145.5 15.5 %all-to-all-done.3 = bf16[32,8,512]{2,1,0:T(8,128)(2,1)S(1)} async-done(((bf16[32,8,512]{2,1,0:T(8,128)(2,1)}), bf16[32,8,512]{2,1,0:T(8,128)(2,1)S(1)}, u32[]{:S(2)}, u32[]{:S(2)}) %all-to-all-start.3) | async-done | bytes 262176 | tf_op jit(solution)/shard_map/all_to_all | solution.py:157
  161.0 0.6 fusion.32
  (16 shorter events, 1.1 us)
Async XLA Ops:
  2.1 34.7 %all-to-all-start = ((bf16[32,8,512]{2,1,0:T(8,128)(2,1)}), bf16[32,8,512]{2,1,0:T(8,128)(2,1)S(1)}, u32[]{:S(2)}, u32[]{:S(2)}) async-start(bf16[32,8,512]{2,1,0:T(8,128)(2,1)} %shard_map.92), calls=%async_computation | async-start | bytes 524288 | tf_op jit(solution)/shard_map/all_to_all | solution.py:113
  37.6 5.5 %collective-permute-start = (bf16[128,2688]{1,0:T(8,128)(2,1)S(1)}, bf16[128,2688]{1,0:T(8,128)(2,1)S(1)}, u32[]{:S(2)}, u32[]{:S(2)}) collective-permute-start(bf16[128,2688]{1,0:T(8,128)(2,1)S(1)} %pad_maximum_fusion.1), channel_id=1, source_target_pairs={{0,1},{1,0},{2,3},{3,2},{4,5},{5,4},{6,7},{7,6},{8,9},{9,8},{10,11... | collective-permute-start | bytes 2064392 | tf_op jit(solution)/shard_map/ppermute | solution.py:65
  57.9 23.9 %collective-permute-start.1 = (bf16[16,2688]{1,0:T(8,128)(2,1)S(1)}, bf16[16,2688]{1,0:T(8,128)(2,1)S(1)}, u32[]{:S(2)}, u32[]{:S(2)}) collective-permute-start(bf16[16,2688]{1,0:T(8,128)(2,1)S(1)} %get-tuple-element.20), channel_id=1, source_target_pairs={{0,8},{1,25},{8,0},{9,17},{16,24},{17,9},{24,16},{25,1},{2,10},{3,... | collective-permute-start | bytes 258056 | tf_op jit(solution)/shard_map/ppermute | solution.py:81
  73.1 19.8 %collective-permute-start.3 = (bf16[16,2688]{1,0:T(8,128)(2,1)S(1)}, bf16[16,2688]{1,0:T(8,128)(2,1)S(1)}, u32[]{:S(2)}, u32[]{:S(2)}) collective-permute-start(bf16[16,2688]{1,0:T(8,128)(2,1)S(1)} %get-tuple-element.21), channel_id=1, source_target_pairs={{0,8},{1,25},{8,0},{9,17},{16,24},{17,9},{24,16},{25,1},{2,10},{3,... | collective-permute-start | bytes 258056 | tf_op jit(solution)/shard_map/ppermute | solution.py:81
  81.9 24.9 %collective-permute-start.2 = (bf16[16,2688]{1,0:T(8,128)(2,1)S(1)}, bf16[16,2688]{1,0:T(8,128)(2,1)S(1)}, u32[]{:S(2)}, u32[]{:S(2)}) collective-permute-start(bf16[16,2688]{1,0:T(8,128)(2,1)S(1)} %get-tuple-element.13), channel_id=1, source_target_pairs={{0,24},{1,9},{8,16},{9,1},{16,8},{17,25},{24,0},{25,17},{2,26},{3,... | collective-permute-start | bytes 258056 | tf_op jit(solution)/shard_map/ppermute | solution.py:81
  93.0 17.1 %collective-permute-start.4 = (bf16[16,2688]{1,0:T(8,128)(2,1)S(1)}, bf16[16,2688]{1,0:T(8,128)(2,1)S(1)}, u32[]{:S(2)}, u32[]{:S(2)}) collective-permute-start(bf16[16,2688]{1,0:T(8,128)(2,1)S(1)} %fusion.16), channel_id=1, source_target_pairs={{0,24},{1,9},{8,16},{9,1},{16,8},{17,25},{24,0},{25,17},{2,26},{3,... | collective-permute-start | bytes 258056 | tf_op jit(solution)/shard_map/ppermute | solution.py:81
  120.5 9.0 %collective-permute-start.5 = (bf16[4,32,2688]{2,1,0:T(8,128)(2,1)S(1)}, bf16[4,32,2688]{2,1,0:T(8,128)(2,1)S(1)}, u32[]{:S(2)}, u32[]{:S(2)}) collective-permute-start(bf16[4,32,2688]{2,1,0:T(8,128)(2,1)S(1)} %all_to_all.21), channel_id=1, source_target_pairs={{0,1},{1,0},{2,3},{3,2},{4,5},{5,4},{6,7},{7,6},{8,9},{9,8},{10,11... | collective-permute-start | bytes 2064392 | tf_op jit(solution)/shard_map/ppermute | solution.py:65
  131.4 29.5 %all-to-all-start.3 = ((bf16[32,8,512]{2,1,0:T(8,128)(2,1)}), bf16[32,8,512]{2,1,0:T(8,128)(2,1)S(1)}, u32[]{:S(2)}, u32[]{:S(2)}) async-start(bf16[32,8,512]{2,1,0:T(8,128)(2,1)} %pad_maximum_fusion.2), calls=%async_computation.3 | async-start | bytes 524288 | tf_op jit(solution)/shard_map/all_to_all | solution.py:157

commit v7 on v6

--- a/solution.py
+++ b/solution.py
@@ -109,8 +109,11 @@
     rows = own * sections
     half = rows // 2
     gate_weight, up_weight, down_weight = held(gate_weight, up_weight, down_weight)
-    both = side_by_side(tokens, out_grad, sections)
-    both = lax.all_to_all(both, SECTION, 0, 0).reshape(rows, 2 * width)
+    runs, lines = lax.axis_size("zl"), lax.axis_size("y")
+    both = side_by_side(tokens, out_grad, runs)
+    both = lax.all_to_all(both, "zl", 0, 0)
+    both = jnp.broadcast_to(both[None], (lines,) + both.shape)
+    both = lax.all_to_all(both, "y", 0, 0).reshape(rows, 2 * width)
 
     core = lax.axis_index("core")
 
@@ -153,9 +156,9 @@
         up_delta, up_weight
     )
     ends = jnp.concatenate([forward_part, backward_part], axis=1).astype(BF16)
-    ends = ends.reshape(sections, own, 2 * width)
-    ends = lax.all_to_all(ends, SECTION, 0, 0)
-    ends = ends.astype(F32).sum(0).astype(BF16)
+    ends = ends.reshape(lines, runs, own, 2 * width)
+    ends = lax.all_to_all(ends, "y", 0, 0).astype(F32).sum(0).astype(BF16)
+    ends = lax.all_to_all(ends, "zl", 0, 0).astype(F32).sum(0).astype(BF16)
     all_tokens, all_grads = both[:, :width], both[:, width:]
     gate_grads = contract_first(all_tokens, gate_delta).astype(BF16)
     up_grads = contract_first(all_tokens, up_delta).astype(BF16)

time: 162 us -> 165 us (1.019)
  blocking collectives: 24.7 us -> 46.1 us
  waiting for transfers between devices: 52.8 us -> 34.7 us
  starting transfers between devices: 72.6 us -> 70.8 us
    all_to_all x0 -> x1, blocking collectives: none -> 22.6 us  [shards(): both = lax.all_to_all(both, 'zl', 0, 0)]
    all_to_all x2 -> x3, waiting for transfers between devices: 32.8 us -> 16.8 us  [the longest x1 7.58 us: shards(): ends = lax.all_to_all(ends, 'zl', 0, 0).astype(F32).sum(0).astype(BF16)]
    all_to_all x2 -> x3, starting transfers between devices: 26.9 us -> 21.8 us  [the longest x1 14.2 us: shards(): ends = lax.all_to_all(ends, 'zl', 0, 0).astype(F32).sum(0).astype(BF16)]
    ppermute x2, starting transfers between devices: 11 us -> 13.6 us  [swap_core(): return lax.ppermute(block, 'core', [(0, 1), (1, 0)])]
    ppermute x4, waiting for transfers between devices: 17.3 us -> 15.2 us  [swap_far(): return lax.ppermute(part.astype(BF16), ('zh', 'core'), pairs)]
  transfers between devices with their start and end apart: 8 -> 9, of which waited for: 7 -> 8; matrix products, arithmetic and copies ran while one was open for 3% -> 3% of each run, Pallas kernels for 1% -> 1%
where the time goes in v7:
time: 165 us; the launch traced here: 164 us
  starting transfers between devices  70.8 us (43%)
  blocking collectives  46.1 us (28%)
  waiting for transfers between devices  34.7 us (21%)
  matrix products  5.75 us (3%)
  other arithmetic  2.14 us (1%)
  Pallas kernels  2.03 us (1%)
    ppermute x4, starting transfers between devices, swap_far(): return lax.ppermute(part.astype(BF16), ('zh', 'core'), pairs)  35.4 us
    all_to_all x1, blocking collectives, shards(): both = lax.all_to_all(both, 'zl', 0, 0)  22.6 us
    ppermute x4, waiting for transfers between devices, swap_far(): return lax.ppermute(part.astype(BF16), ('zh', 'core'), pairs)  15.2 us
    all_to_all x1, starting transfers between devices, shards(): ends = lax.all_to_all(ends, 'zl', 0, 0).astype(F32).sum(0).astype(BF16)  14.2 us
    ppermute x2, starting transfers between devices, swap_core(): return lax.ppermute(block, 'core', [(0, 1), (1, 0)])  13.6 us
    all_to_all x1, blocking collectives, sum_over_x(): return lax.all_to_all(pieces, 'x', 0, 0).astype(F32).sum(0)  13.2 us
    all_to_all x1, blocking collectives, copies_over_x(): return lax.all_to_all(copies, 'x', 0, 0)  10.2 us
    all_to_all x1, waiting for transfers between devices, shards(): ends = lax.all_to_all(ends, 'zl', 0, 0).astype(F32).sum(0).astype(BF16)  7.58 us
  transfers between devices with their start and end apart: 9, of which 8 were waited for; matrix products, arithmetic and copies ran while one was open for 3% of the time, Pallas kernels for 1%

profile of v7, /device:TPU:1, one launch (start us, length us, event | category | flops | bytes accessed | tf_op | source)
XLA Modules:
  0.0 163.7 jit_solution(4594708944676562170)
XLA Ops:
  0.6 0.7 shard_map.92
  1.3 22.6 %all_to_all.30 = bf16[8,8,512]{2,1,0:T(8,128)(2,1)S(1)} all-to-all(bf16[8,8,512]{2,1,0:T(8,128)(2,1)S(1)} %shard_map.92), channel_id=1, replica_groups=mesh['y'=4,'zl'=8,'zh'=4,'x'=4,'core'=2] {'zl'}, dimensions={0} | all-to-all | bytes 131072 | tf_op jit(solution)/shard_map/all_to_all | solution.py:114
  24.0 0.7 broadcast_in_dim.4
  24.7 4.2 %all-to-all-start.1 = ((bf16[4,8,8,512]{3,2,1,0:T(8,128)(2,1)}), bf16[4,8,8,512]{3,2,1,0:T(8,128)(2,1)S(1)}, u32[]{:S(2)}, u32[]{:S(2)}) async-start(bf16[4,8,8,512]{3,2,1,0:T(8,128)(2,1)} %broadcast_in_dim.4), calls=%async_computation.1 | async-start | bytes 524288 | tf_op jit(solution)/shard_map/all_to_all | solution.py:116
  28.9 1.3 shard_map.93
  30.2 4.2 %all-to-all-done.1 = bf16[4,8,8,512]{3,2,1,0:T(8,128)(2,1)S(1)} async-done(((bf16[4,8,8,512]{3,2,1,0:T(8,128)(2,1)}), bf16[4,8,8,512]{3,2,1,0:T(8,128)(2,1)S(1)}, u32[]{:S(2)}, u32[]{:S(2)}) %all-to-all-start.1) | async-done | bytes 262176 | tf_op jit(solution)/shard_map/all_to_all | solution.py:116
  35.2 7.1 %collective-permute-start = (bf16[128,2688]{1,0:T(8,128)(2,1)S(1)}, bf16[128,2688]{1,0:T(8,128)(2,1)S(1)}, u32[]{:S(2)}, u32[]{:S(2)}) collective-permute-start(bf16[128,2688]{1,0:T(8,128)(2,1)S(1)} %pad_maximum_fusion.1), channel_id=1, source_target_pairs={{0,1},{1,0},{2,3},{3,2},{4,5},{5,4},{6,7},{7,6},{8,9},{9,8},{10,11... | collective-permute-start | bytes 2064392 | tf_op jit(solution)/shard_map/ppermute | solution.py:65
  43.1 1.0 collective-permute-done
  44.2 13.2 %all_to_all.31 = bf16[4,32,2688]{2,1,0:T(8,128)(2,1)S(1)} all-to-all(bf16[4,32,2688]{2,1,0:T(8,128)(2,1)S(1)} %bitcast.33), channel_id=1, replica_groups=mesh['y'=4,'zl'=8,'zh'=4,'x'=4,'core'=2] {'x'}, dimensions={0} | all-to-all | bytes 1376256 | tf_op jit(solution)/shard_map/all_to_all | solution.py:72
  57.6 14.8 %collective-permute-start.1 = (bf16[16,2688]{1,0:T(8,128)(2,1)S(1)}, bf16[16,2688]{1,0:T(8,128)(2,1)S(1)}, u32[]{:S(2)}, u32[]{:S(2)}) collective-permute-start(bf16[16,2688]{1,0:T(8,128)(2,1)S(1)} %get-tuple-element.20), channel_id=1, source_target_pairs={{0,8},{1,25},{8,0},{9,17},{16,24},{17,9},{24,16},{25,1},{2,10},{3,... | collective-permute-start | bytes 258056 | tf_op jit(solution)/shard_map/ppermute | solution.py:81
  72.4 1.9 %collective-permute-start.3 = (bf16[16,2688]{1,0:T(8,128)(2,1)S(1)}, bf16[16,2688]{1,0:T(8,128)(2,1)S(1)}, u32[]{:S(2)}, u32[]{:S(2)}) collective-permute-start(bf16[16,2688]{1,0:T(8,128)(2,1)S(1)} %get-tuple-element.21), channel_id=1, source_target_pairs={{0,8},{1,25},{8,0},{9,17},{16,24},{17,9},{24,16},{25,1},{2,10},{3,... | collective-permute-start | bytes 258056 | tf_op jit(solution)/shard_map/ppermute | solution.py:81
  74.3 7.7 %collective-permute-done.1 = bf16[16,2688]{1,0:T(8,128)(2,1)S(1)} collective-permute-done((bf16[16,2688]{1,0:T(8,128)(2,1)S(1)}, bf16[16,2688]{1,0:T(8,128)(2,1)S(1)}, u32[]{:S(2)}, u32[]{:S(2)}) %collective-permute-start.1) | collective-permute-done | bytes 86048 | tf_op jit(solution)/shard_map/ppermute | solution.py:81
  82.0 11.0 %collective-permute-start.2 = (bf16[16,2688]{1,0:T(8,128)(2,1)S(1)}, bf16[16,2688]{1,0:T(8,128)(2,1)S(1)}, u32[]{:S(2)}, u32[]{:S(2)}) collective-permute-start(bf16[16,2688]{1,0:T(8,128)(2,1)S(1)} %get-tuple-element.13), channel_id=1, source_target_pairs={{0,24},{1,9},{8,16},{9,1},{16,8},{17,25},{24,0},{25,17},{2,26},{3,... | collective-permute-start | bytes 258056 | tf_op jit(solution)/shard_map/ppermute | solution.py:81
  93.0 7.7 %collective-permute-start.4 = (bf16[16,2688]{1,0:T(8,128)(2,1)S(1)}, bf16[16,2688]{1,0:T(8,128)(2,1)S(1)}, u32[]{:S(2)}, u32[]{:S(2)}) collective-permute-start(bf16[16,2688]{1,0:T(8,128)(2,1)S(1)} %fusion.14), channel_id=1, source_target_pairs={{0,24},{1,9},{8,16},{9,1},{16,8},{17,25},{24,0},{25,17},{2,26},{3,... | collective-permute-start | bytes 258056 | tf_op jit(solution)/shard_map/ppermute | solution.py:81
  100.8 3.6 %collective-permute-done.2 = bf16[16,2688]{1,0:T(8,128)(2,1)S(1)} collective-permute-done((bf16[16,2688]{1,0:T(8,128)(2,1)S(1)}, bf16[16,2688]{1,0:T(8,128)(2,1)S(1)}, u32[]{:S(2)}, u32[]{:S(2)}) %collective-permute-start.2) | collective-permute-done | bytes 86048 | tf_op jit(solution)/shard_map/ppermute | solution.py:81
  104.3 3.9 %collective-permute-done.4 = bf16[16,2688]{1,0:T(8,128)(2,1)S(1)} collective-permute-done((bf16[16,2688]{1,0:T(8,128)(2,1)S(1)}, bf16[16,2688]{1,0:T(8,128)(2,1)S(1)}, u32[]{:S(2)}, u32[]{:S(2)}) %collective-permute-start.4) | collective-permute-done | bytes 86048 | tf_op jit(solution)/shard_map/ppermute | solution.py:81
  108.5 10.2 %all_to_all.32 = bf16[4,32,2688]{2,1,0:T(8,128)(2,1)S(1)} all-to-all(bf16[4,32,2688]{2,1,0:T(8,128)(2,1)S(1)} %broadcast_in_dim.5), channel_id=1, replica_groups=mesh['y'=4,'zl'=8,'zh'=4,'x'=4,'core'=2] {'x'}, dimensions={0} | all-to-all | bytes 1376256 | tf_op jit(solution)/shard_map/all_to_all | solution.py:102
  118.7 6.5 %collective-permute-start.5 = (bf16[4,32,2688]{2,1,0:T(8,128)(2,1)S(1)}, bf16[4,32,2688]{2,1,0:T(8,128)(2,1)S(1)}, u32[]{:S(2)}, u32[]{:S(2)}) collective-permute-start(bf16[4,32,2688]{2,1,0:T(8,128)(2,1)S(1)} %all_to_all.32), channel_id=1, source_target_pairs={{0,1},{1,0},{2,3},{3,2},{4,5},{5,4},{6,7},{7,6},{8,9},{9,8},{10,11... | collective-permute-start | bytes 2064392 | tf_op jit(solution)/shard_map/ppermute | solution.py:65
  125.2 1.7 %collective-permute-done.5 = bf16[4,32,2688]{2,1,0:T(8,128)(2,1)S(1)} collective-permute-done((bf16[4,32,2688]{2,1,0:T(8,128)(2,1)S(1)}, bf16[4,32,2688]{2,1,0:T(8,128)(2,1)S(1)}, u32[]{:S(2)}, u32[]{:S(2)}) %collective-permute-start.5) | collective-permute-done | bytes 688160 | tf_op jit(solution)/shard_map/ppermute | solution.py:65
  127.2 0.3 convolution_convert_fusion.6
  127.5 0.3 fusion.5
  127.9 0.3 fusion.1
  128.2 0.7 pad_maximum_fusion.2
  128.9 3.4 %all-to-all-start.4 = ((bf16[4,8,8,512]{3,2,1,0:T(8,128)(2,1)}), bf16[4,8,8,512]{3,2,1,0:T(8,128)(2,1)S(1)}, u32[]{:S(2)}, u32[]{:S(2)}) async-start(bf16[4,8,8,512]{3,2,1,0:T(8,128)(2,1)} %pad_maximum_fusion.2), calls=%async_computation.4 | async-start | bytes 524288 | tf_op jit(solution)/shard_map/all_to_all | solution.py:160
  132.3 1.1 convolution_convert_fusion
  133.4 5.0 %all-to-all-done.4 = bf16[4,8,8,512]{3,2,1,0:T(8,128)(2,1)S(1)} async-done(((bf16[4,8,8,512]{3,2,1,0:T(8,128)(2,1)}), bf16[4,8,8,512]{3,2,1,0:T(8,128)(2,1)S(1)}, u32[]{:S(2)}, u32[]{:S(2)}) %all-to-all-start.4) | async-done | bytes 262176 | tf_op jit(solution)/shard_map/all_to_all | solution.py:160
  138.4 0.7 reduce_sum.34
  139.1 14.2 %all-to-all-start.5 = ((bf16[8,8,512]{2,1,0:T(8,128)(2,1)}), bf16[8,8,512]{2,1,0:T(8,128)(2,1)S(1)}, u32[]{:S(2)}, u32[]{:S(2)}) async-start(bf16[8,8,512]{2,1,0:T(8,128)(2,1)} %reduce_sum.34), calls=%async_computation.5 | async-start | bytes 131072 | tf_op jit(solution)/shard_map/all_to_all | solution.py:161
  153.3 1.1 convolution_convert_fusion.1
  154.4 1.1 convolution_convert_fusion.2
  155.5 7.6 %all-to-all-done.5 = bf16[8,8,512]{2,1,0:T(8,128)(2,1)S(1)} async-done(((bf16[8,8,512]{2,1,0:T(8,128)(2,1)}), bf16[8,8,512]{2,1,0:T(8,128)(2,1)S(1)}, u32[]{:S(2)}, u32[]{:S(2)}) %all-to-all-start.5) | async-done | bytes 65568 | tf_op jit(solution)/shard_map/all_to_all | solution.py:161
  163.1 0.6 fusion.30
  (21 shorter events, 2.3 us)
Async XLA Ops:
  24.7 9.7 %all-to-all-start.1 = ((bf16[4,8,8,512]{3,2,1,0:T(8,128)(2,1)}), bf16[4,8,8,512]{3,2,1,0:T(8,128)(2,1)S(1)}, u32[]{:S(2)}, u32[]{:S(2)}) async-start(bf16[4,8,8,512]{3,2,1,0:T(8,128)(2,1)} %broadcast_in_dim.4), calls=%async_computation.1 | async-start | bytes 524288 | tf_op jit(solution)/shard_map/all_to_all | solution.py:116
  35.2 8.8 %collective-permute-start = (bf16[128,2688]{1,0:T(8,128)(2,1)S(1)}, bf16[128,2688]{1,0:T(8,128)(2,1)S(1)}, u32[]{:S(2)}, u32[]{:S(2)}) collective-permute-start(bf16[128,2688]{1,0:T(8,128)(2,1)S(1)} %pad_maximum_fusion.1), channel_id=1, source_target_pairs={{0,1},{1,0},{2,3},{3,2},{4,5},{5,4},{6,7},{7,6},{8,9},{9,8},{10,11... | collective-permute-start | bytes 2064392 | tf_op jit(solution)/shard_map/ppermute | solution.py:65
  57.6 24.5 %collective-permute-start.1 = (bf16[16,2688]{1,0:T(8,128)(2,1)S(1)}, bf16[16,2688]{1,0:T(8,128)(2,1)S(1)}, u32[]{:S(2)}, u32[]{:S(2)}) collective-permute-start(bf16[16,2688]{1,0:T(8,128)(2,1)S(1)} %get-tuple-element.20), channel_id=1, source_target_pairs={{0,8},{1,25},{8,0},{9,17},{16,24},{17,9},{24,16},{25,1},{2,10},{3,... | collective-permute-start | bytes 258056 | tf_op jit(solution)/shard_map/ppermute | solution.py:81
  72.4 20.6 %collective-permute-start.3 = (bf16[16,2688]{1,0:T(8,128)(2,1)S(1)}, bf16[16,2688]{1,0:T(8,128)(2,1)S(1)}, u32[]{:S(2)}, u32[]{:S(2)}) collective-permute-start(bf16[16,2688]{1,0:T(8,128)(2,1)S(1)} %get-tuple-element.21), channel_id=1, source_target_pairs={{0,8},{1,25},{8,0},{9,17},{16,24},{17,9},{24,16},{25,1},{2,10},{3,... | collective-permute-start | bytes 258056 | tf_op jit(solution)/shard_map/ppermute | solution.py:81
  82.0 22.3 %collective-permute-start.2 = (bf16[16,2688]{1,0:T(8,128)(2,1)S(1)}, bf16[16,2688]{1,0:T(8,128)(2,1)S(1)}, u32[]{:S(2)}, u32[]{:S(2)}) collective-permute-start(bf16[16,2688]{1,0:T(8,128)(2,1)S(1)} %get-tuple-element.13), channel_id=1, source_target_pairs={{0,24},{1,9},{8,16},{9,1},{16,8},{17,25},{24,0},{25,17},{2,26},{3,... | collective-permute-start | bytes 258056 | tf_op jit(solution)/shard_map/ppermute | solution.py:81
  93.0 15.2 %collective-permute-start.4 = (bf16[16,2688]{1,0:T(8,128)(2,1)S(1)}, bf16[16,2688]{1,0:T(8,128)(2,1)S(1)}, u32[]{:S(2)}, u32[]{:S(2)}) collective-permute-start(bf16[16,2688]{1,0:T(8,128)(2,1)S(1)} %fusion.14), channel_id=1, source_target_pairs={{0,24},{1,9},{8,16},{9,1},{16,8},{17,25},{24,0},{25,17},{2,26},{3,... | collective-permute-start | bytes 258056 | tf_op jit(solution)/shard_map/ppermute | solution.py:81
  118.7 8.3 %collective-permute-start.5 = (bf16[4,32,2688]{2,1,0:T(8,128)(2,1)S(1)}, bf16[4,32,2688]{2,1,0:T(8,128)(2,1)S(1)}, u32[]{:S(2)}, u32[]{:S(2)}) collective-permute-start(bf16[4,32,2688]{2,1,0:T(8,128)(2,1)S(1)} %all_to_all.32), channel_id=1, source_target_pairs={{0,1},{1,0},{2,3},{3,2},{4,5},{5,4},{6,7},{7,6},{8,9},{9,8},{10,11... | collective-permute-start | bytes 2064392 | tf_op jit(solution)/shard_map/ppermute | solution.py:65
  128.9 9.5 %all-to-all-start.4 = ((bf16[4,8,8,512]{3,2,1,0:T(8,128)(2,1)}), bf16[4,8,8,512]{3,2,1,0:T(8,128)(2,1)S(1)}, u32[]{:S(2)}, u32[]{:S(2)}) async-start(bf16[4,8,8,512]{3,2,1,0:T(8,128)(2,1)} %pad_maximum_fusion.2), calls=%async_computation.4 | async-start | bytes 524288 | tf_op jit(solution)/shard_map/all_to_all | solution.py:160
  139.1 24.0 %all-to-all-start.5 = ((bf16[8,8,512]{2,1,0:T(8,128)(2,1)}), bf16[8,8,512]{2,1,0:T(8,128)(2,1)S(1)}, u32[]{:S(2)}, u32[]{:S(2)}) async-start(bf16[8,8,512]{2,1,0:T(8,128)(2,1)} %reduce_sum.34), calls=%async_computation.5 | async-start | bytes 131072 | tf_op jit(solution)/shard_map/all_to_all | solution.py:161

commit v8 on v7

--- a/solution.py
+++ b/solution.py
@@ -156,9 +156,8 @@
         up_delta, up_weight
     )
     ends = jnp.concatenate([forward_part, backward_part], axis=1).astype(BF16)
-    ends = ends.reshape(lines, runs, own, 2 * width)
-    ends = lax.all_to_all(ends, "y", 0, 0).astype(F32).sum(0).astype(BF16)
-    ends = lax.all_to_all(ends, "zl", 0, 0).astype(F32).sum(0).astype(BF16)
+    ends = ends.reshape(sections, own, 2 * width)
+    ends = lax.all_to_all(ends, SECTION, 0, 0).astype(F32).sum(0).astype(BF16)
     all_tokens, all_grads = both[:, :width], both[:, width:]
     gate_grads = contract_first(all_tokens, gate_delta).astype(BF16)
     up_grads = contract_first(all_tokens, up_delta).astype(BF16)

time: 165 us -> 164 us (level)
  waiting for transfers between devices: 34.7 us -> 37.6 us
  starting transfers between devices: 70.8 us -> 68.5 us
    all_to_all x2 -> x1, waiting for transfers between devices: 12.6 us -> 15.5 us  [shards(): ends = lax.all_to_all(ends, SECTION, 0, 0).astype(F32).sum(0).astype(BF16)]
    all_to_all x2 -> x1, starting transfers between devices: 17.6 us -> 15.3 us  [shards(): ends = lax.all_to_all(ends, SECTION, 0, 0).astype(F32).sum(0).astype(BF16)]
  transfers between devices with their start and end apart: 9 -> 8, of which waited for: 8 -> 7; matrix products, arithmetic and copies ran while one was open for 3% -> 3% of each run, Pallas kernels for 1% -> 1%
where the time goes in v8:
time: 164 us
  starting transfers between devices  68.5 us (42%)
  blocking collectives  46.1 us (28%)
  waiting for transfers between devices  37.6 us (23%)
  matrix products  5.75 us (4%)
  Pallas kernels  2.03 us (1%)
    ppermute x4, starting transfers between devices, swap_far(): return lax.ppermute(part.astype(BF16), ('zh', 'core'), pairs)  35.4 us
    all_to_all x1, blocking collectives, shards(): both = lax.all_to_all(both, 'zl', 0, 0)  22.6 us
    all_to_all x1, waiting for transfers between devices, shards(): ends = lax.all_to_all(ends, SECTION, 0, 0).astype(F32).sum(0).astype(BF16)  15.5 us
    all_to_all x1, starting transfers between devices, shards(): ends = lax.all_to_all(ends, SECTION, 0, 0).astype(F32).sum(0).astype(BF16)  15.3 us
    ppermute x4, waiting for transfers between devices, swap_far(): return lax.ppermute(part.astype(BF16), ('zh', 'core'), pairs)  15.2 us
    ppermute x2, starting transfers between devices, swap_core(): return lax.ppermute(block, 'core', [(0, 1), (1, 0)])  13.6 us
    all_to_all x1, blocking collectives, sum_over_x(): return lax.all_to_all(pieces, 'x', 0, 0).astype(F32).sum(0)  13.2 us
    all_to_all x1, blocking collectives, copies_over_x(): return lax.all_to_all(copies, 'x', 0, 0)  10.2 us
  transfers between devices with their start and end apart: 8, of which 7 were waited for; matrix products, arithmetic and copies ran while one was open for 3% of the time, Pallas kernels for 1%

profile of v8, /device:TPU:1, one launch (start us, length us, event | category | flops | bytes accessed | tf_op | source)
XLA Modules:
  0.0 163.7 jit_solution(190103809671913869)
XLA Ops:
  0.6 0.7 shard_map.92
  1.3 22.6 %all_to_all.25 = bf16[8,8,512]{2,1,0:T(8,128)(2,1)S(1)} all-to-all(bf16[8,8,512]{2,1,0:T(8,128)(2,1)S(1)} %shard_map.92), channel_id=1, replica_groups=mesh['y'=4,'zl'=8,'zh'=4,'x'=4,'core'=2] {'zl'}, dimensions={0} | all-to-all | bytes 131072 | tf_op jit(solution)/shard_map/all_to_all | solution.py:114
  24.0 0.7 broadcast_in_dim.4
  24.7 4.2 %all-to-all-start.1 = ((bf16[4,8,8,512]{3,2,1,0:T(8,128)(2,1)}), bf16[4,8,8,512]{3,2,1,0:T(8,128)(2,1)S(1)}, u32[]{:S(2)}, u32[]{:S(2)}) async-start(bf16[4,8,8,512]{3,2,1,0:T(8,128)(2,1)} %broadcast_in_dim.4), calls=%async_computation.1 | async-start | bytes 524288 | tf_op jit(solution)/shard_map/all_to_all | solution.py:116
  28.9 1.3 shard_map.93
  30.2 4.2 %all-to-all-done.1 = bf16[4,8,8,512]{3,2,1,0:T(8,128)(2,1)S(1)} async-done(((bf16[4,8,8,512]{3,2,1,0:T(8,128)(2,1)}), bf16[4,8,8,512]{3,2,1,0:T(8,128)(2,1)S(1)}, u32[]{:S(2)}, u32[]{:S(2)}) %all-to-all-start.1) | async-done | bytes 262176 | tf_op jit(solution)/shard_map/all_to_all | solution.py:116
  34.9 0.3 convolution_convert_fusion.3
  35.2 7.1 %collective-permute-start = (bf16[128,2688]{1,0:T(8,128)(2,1)S(1)}, bf16[128,2688]{1,0:T(8,128)(2,1)S(1)}, u32[]{:S(2)}, u32[]{:S(2)}) collective-permute-start(bf16[128,2688]{1,0:T(8,128)(2,1)S(1)} %pad_maximum_fusion.1), channel_id=1, source_target_pairs={{0,1},{1,0},{2,3},{3,2},{4,5},{5,4},{6,7},{7,6},{8,9},{9,8},{10,11... | collective-permute-start | bytes 2064392 | tf_op jit(solution)/shard_map/ppermute | solution.py:65
  42.3 0.3 fusion.18
  42.6 0.2 fusion.22
  43.1 1.0 collective-permute-done
  44.2 13.2 %all_to_all.26 = bf16[4,32,2688]{2,1,0:T(8,128)(2,1)S(1)} all-to-all(bf16[4,32,2688]{2,1,0:T(8,128)(2,1)S(1)} %bitcast.35), channel_id=1, replica_groups=mesh['y'=4,'zl'=8,'zh'=4,'x'=4,'core'=2] {'x'}, dimensions={0} | all-to-all | bytes 1376256 | tf_op jit(solution)/shard_map/all_to_all | solution.py:72
  57.6 14.8 %collective-permute-start.1 = (bf16[16,2688]{1,0:T(8,128)(2,1)S(1)}, bf16[16,2688]{1,0:T(8,128)(2,1)S(1)}, u32[]{:S(2)}, u32[]{:S(2)}) collective-permute-start(bf16[16,2688]{1,0:T(8,128)(2,1)S(1)} %get-tuple-element.20), channel_id=1, source_target_pairs={{0,8},{1,25},{8,0},{9,17},{16,24},{17,9},{24,16},{25,1},{2,10},{3,... | collective-permute-start | bytes 258056 | tf_op jit(solution)/shard_map/ppermute | solution.py:81
  72.4 1.9 %collective-permute-start.3 = (bf16[16,2688]{1,0:T(8,128)(2,1)S(1)}, bf16[16,2688]{1,0:T(8,128)(2,1)S(1)}, u32[]{:S(2)}, u32[]{:S(2)}) collective-permute-start(bf16[16,2688]{1,0:T(8,128)(2,1)S(1)} %get-tuple-element.21), channel_id=1, source_target_pairs={{0,8},{1,25},{8,0},{9,17},{16,24},{17,9},{24,16},{25,1},{2,10},{3,... | collective-permute-start | bytes 258056 | tf_op jit(solution)/shard_map/ppermute | solution.py:81
  74.3 7.7 %collective-permute-done.1 = bf16[16,2688]{1,0:T(8,128)(2,1)S(1)} collective-permute-done((bf16[16,2688]{1,0:T(8,128)(2,1)S(1)}, bf16[16,2688]{1,0:T(8,128)(2,1)S(1)}, u32[]{:S(2)}, u32[]{:S(2)}) %collective-permute-start.1) | collective-permute-done | bytes 86048 | tf_op jit(solution)/shard_map/ppermute | solution.py:81
  82.0 11.0 %collective-permute-start.2 = (bf16[16,2688]{1,0:T(8,128)(2,1)S(1)}, bf16[16,2688]{1,0:T(8,128)(2,1)S(1)}, u32[]{:S(2)}, u32[]{:S(2)}) collective-permute-start(bf16[16,2688]{1,0:T(8,128)(2,1)S(1)} %get-tuple-element.13), channel_id=1, source_target_pairs={{0,24},{1,9},{8,16},{9,1},{16,8},{17,25},{24,0},{25,17},{2,26},{3,... | collective-permute-start | bytes 258056 | tf_op jit(solution)/shard_map/ppermute | solution.py:81
  93.0 7.7 %collective-permute-start.4 = (bf16[16,2688]{1,0:T(8,128)(2,1)S(1)}, bf16[16,2688]{1,0:T(8,128)(2,1)S(1)}, u32[]{:S(2)}, u32[]{:S(2)}) collective-permute-start(bf16[16,2688]{1,0:T(8,128)(2,1)S(1)} %fusion.16), channel_id=1, source_target_pairs={{0,24},{1,9},{8,16},{9,1},{16,8},{17,25},{24,0},{25,17},{2,26},{3,... | collective-permute-start | bytes 258056 | tf_op jit(solution)/shard_map/ppermute | solution.py:81
  100.8 3.6 %collective-permute-done.2 = bf16[16,2688]{1,0:T(8,128)(2,1)S(1)} collective-permute-done((bf16[16,2688]{1,0:T(8,128)(2,1)S(1)}, bf16[16,2688]{1,0:T(8,128)(2,1)S(1)}, u32[]{:S(2)}, u32[]{:S(2)}) %collective-permute-start.2) | collective-permute-done | bytes 86048 | tf_op jit(solution)/shard_map/ppermute | solution.py:81
  104.3 3.9 %collective-permute-done.4 = bf16[16,2688]{1,0:T(8,128)(2,1)S(1)} collective-permute-done((bf16[16,2688]{1,0:T(8,128)(2,1)S(1)}, bf16[16,2688]{1,0:T(8,128)(2,1)S(1)}, u32[]{:S(2)}, u32[]{:S(2)}) %collective-permute-start.4) | collective-permute-done | bytes 86048 | tf_op jit(solution)/shard_map/ppermute | solution.py:81
  108.5 10.2 %all_to_all.27 = bf16[4,32,2688]{2,1,0:T(8,128)(2,1)S(1)} all-to-all(bf16[4,32,2688]{2,1,0:T(8,128)(2,1)S(1)} %broadcast_in_dim.5), channel_id=1, replica_groups=mesh['y'=4,'zl'=8,'zh'=4,'x'=4,'core'=2] {'x'}, dimensions={0} | all-to-all | bytes 1376256 | tf_op jit(solution)/shard_map/all_to_all | solution.py:102
  118.7 6.5 %collective-permute-start.5 = (bf16[4,32,2688]{2,1,0:T(8,128)(2,1)S(1)}, bf16[4,32,2688]{2,1,0:T(8,128)(2,1)S(1)}, u32[]{:S(2)}, u32[]{:S(2)}) collective-permute-start(bf16[4,32,2688]{2,1,0:T(8,128)(2,1)S(1)} %all_to_all.27), channel_id=1, source_target_pairs={{0,1},{1,0},{2,3},{3,2},{4,5},{5,4},{6,7},{7,6},{8,9},{9,8},{10,11... | collective-permute-start | bytes 2064392 | tf_op jit(solution)/shard_map/ppermute | solution.py:65
  125.2 1.7 %collective-permute-done.5 = bf16[4,32,2688]{2,1,0:T(8,128)(2,1)S(1)} collective-permute-done((bf16[4,32,2688]{2,1,0:T(8,128)(2,1)S(1)}, bf16[4,32,2688]{2,1,0:T(8,128)(2,1)S(1)}, u32[]{:S(2)}, u32[]{:S(2)}) %collective-permute-start.5) | collective-permute-done | bytes 688160 | tf_op jit(solution)/shard_map/ppermute | solution.py:65
  127.2 0.3 fusion.2
  127.5 0.3 fusion.7
  127.9 0.3 fusion.3
  128.2 0.7 pad_maximum_fusion.2
  128.9 15.3 %all-to-all-start.4 = ((bf16[32,8,512]{2,1,0:T(8,128)(2,1)}), bf16[32,8,512]{2,1,0:T(8,128)(2,1)S(1)}, u32[]{:S(2)}, u32[]{:S(2)}) async-start(bf16[32,8,512]{2,1,0:T(8,128)(2,1)} %pad_maximum_fusion.2), calls=%async_computation.4 | async-start | bytes 524288 | tf_op jit(solution)/shard_map/all_to_all | solution.py:160
  144.2 1.1 convolution_convert_fusion
  145.4 1.1 convolution_convert_fusion.1
  146.4 1.1 convolution_convert_fusion.2
  147.5 15.5 %all-to-all-done.4 = bf16[32,8,512]{2,1,0:T(8,128)(2,1)S(1)} async-done(((bf16[32,8,512]{2,1,0:T(8,128)(2,1)}), bf16[32,8,512]{2,1,0:T(8,128)(2,1)S(1)}, u32[]{:S(2)}, u32[]{:S(2)}) %all-to-all-start.4) | async-done | bytes 262176 | tf_op jit(solution)/shard_map/all_to_all | solution.py:160
  163.1 0.6 fusion.32
  (18 shorter events, 1.6 us)
Async XLA Ops:
  24.7 9.7 %all-to-all-start.1 = ((bf16[4,8,8,512]{3,2,1,0:T(8,128)(2,1)}), bf16[4,8,8,512]{3,2,1,0:T(8,128)(2,1)S(1)}, u32[]{:S(2)}, u32[]{:S(2)}) async-start(bf16[4,8,8,512]{3,2,1,0:T(8,128)(2,1)} %broadcast_in_dim.4), calls=%async_computation.1 | async-start | bytes 524288 | tf_op jit(solution)/shard_map/all_to_all | solution.py:116
  35.2 8.8 %collective-permute-start = (bf16[128,2688]{1,0:T(8,128)(2,1)S(1)}, bf16[128,2688]{1,0:T(8,128)(2,1)S(1)}, u32[]{:S(2)}, u32[]{:S(2)}) collective-permute-start(bf16[128,2688]{1,0:T(8,128)(2,1)S(1)} %pad_maximum_fusion.1), channel_id=1, source_target_pairs={{0,1},{1,0},{2,3},{3,2},{4,5},{5,4},{6,7},{7,6},{8,9},{9,8},{10,11... | collective-permute-start | bytes 2064392 | tf_op jit(solution)/shard_map/ppermute | solution.py:65
  57.6 24.5 %collective-permute-start.1 = (bf16[16,2688]{1,0:T(8,128)(2,1)S(1)}, bf16[16,2688]{1,0:T(8,128)(2,1)S(1)}, u32[]{:S(2)}, u32[]{:S(2)}) collective-permute-start(bf16[16,2688]{1,0:T(8,128)(2,1)S(1)} %get-tuple-element.20), channel_id=1, source_target_pairs={{0,8},{1,25},{8,0},{9,17},{16,24},{17,9},{24,16},{25,1},{2,10},{3,... | collective-permute-start | bytes 258056 | tf_op jit(solution)/shard_map/ppermute | solution.py:81
  72.4 20.6 %collective-permute-start.3 = (bf16[16,2688]{1,0:T(8,128)(2,1)S(1)}, bf16[16,2688]{1,0:T(8,128)(2,1)S(1)}, u32[]{:S(2)}, u32[]{:S(2)}) collective-permute-start(bf16[16,2688]{1,0:T(8,128)(2,1)S(1)} %get-tuple-element.21), channel_id=1, source_target_pairs={{0,8},{1,25},{8,0},{9,17},{16,24},{17,9},{24,16},{25,1},{2,10},{3,... | collective-permute-start | bytes 258056 | tf_op jit(solution)/shard_map/ppermute | solution.py:81
  82.0 22.3 %collective-permute-start.2 = (bf16[16,2688]{1,0:T(8,128)(2,1)S(1)}, bf16[16,2688]{1,0:T(8,128)(2,1)S(1)}, u32[]{:S(2)}, u32[]{:S(2)}) collective-permute-start(bf16[16,2688]{1,0:T(8,128)(2,1)S(1)} %get-tuple-element.13), channel_id=1, source_target_pairs={{0,24},{1,9},{8,16},{9,1},{16,8},{17,25},{24,0},{25,17},{2,26},{3,... | collective-permute-start | bytes 258056 | tf_op jit(solution)/shard_map/ppermute | solution.py:81
  93.0 15.2 %collective-permute-start.4 = (bf16[16,2688]{1,0:T(8,128)(2,1)S(1)}, bf16[16,2688]{1,0:T(8,128)(2,1)S(1)}, u32[]{:S(2)}, u32[]{:S(2)}) collective-permute-start(bf16[16,2688]{1,0:T(8,128)(2,1)S(1)} %fusion.16), channel_id=1, source_target_pairs={{0,24},{1,9},{8,16},{9,1},{16,8},{17,25},{24,0},{25,17},{2,26},{3,... | collective-permute-start | bytes 258056 | tf_op jit(solution)/shard_map/ppermute | solution.py:81
  118.7 8.3 %collective-permute-start.5 = (bf16[4,32,2688]{2,1,0:T(8,128)(2,1)S(1)}, bf16[4,32,2688]{2,1,0:T(8,128)(2,1)S(1)}, u32[]{:S(2)}, u32[]{:S(2)}) collective-permute-start(bf16[4,32,2688]{2,1,0:T(8,128)(2,1)S(1)} %all_to_all.27), channel_id=1, source_target_pairs={{0,1},{1,0},{2,3},{3,2},{4,5},{5,4},{6,7},{7,6},{8,9},{9,8},{10,11... | collective-permute-start | bytes 2064392 | tf_op jit(solution)/shard_map/ppermute | solution.py:65
  128.9 34.1 %all-to-all-start.4 = ((bf16[32,8,512]{2,1,0:T(8,128)(2,1)}), bf16[32,8,512]{2,1,0:T(8,128)(2,1)S(1)}, u32[]{:S(2)}, u32[]{:S(2)}) async-start(bf16[32,8,512]{2,1,0:T(8,128)(2,1)} %pad_maximum_fusion.2), calls=%async_computation.4 | async-start | bytes 524288 | tf_op jit(solution)/shard_map/all_to_all | solution.py:160

commit v9 on v8

--- a/solution.py
+++ b/solution.py
@@ -134,12 +134,12 @@
 
     piece = part.shape[0] // 2
     top, low = part[:piece], part[piece:]
-    top_in, low_in = swap_far(top, (1, 3)), swap_far(low, (1, 3))
+    top_in, low_in = swap_far(top, (1, 3)), swap_far(low, (3, 1))
     top = top + top_in
     low_in, _ = lax.optimization_barrier((low_in, top))
     top_in = swap_far(top, (3, 1))
     low = low + low_in
-    low_in = swap_far(low, (3, 1))
+    low_in = swap_far(low, (1, 3))
     mine = copies_over_x(deltas_of(jnp.concatenate([top + top_in, low + low_in])))
     theirs = swap_core(mine)
     first = core == 0

time: 164 us -> 160 us (0.976)
  waiting for transfers between devices: 37.6 us -> 35.6 us
  starting transfers between devices: 68.5 us -> 66.7 us
    all_to_all x1, starting transfers between devices: 15.3 us -> 3.87 us  [shards(): ends = lax.all_to_all(ends, SECTION, 0, 0).astype(F32).sum(0).astype(BF16)]
    ppermute x4, starting transfers between devices: 35.4 us -> 44.5 us  [swap_far(): return lax.ppermute(part.astype(BF16), ('zh', 'core'), pairs)]
    ppermute x4, waiting for transfers between devices: 15.2 us -> 12.9 us  [swap_far(): return lax.ppermute(part.astype(BF16), ('zh', 'core'), pairs)]
  transfers between devices with their start and end apart: 8 -> 8, of which waited for: 7 -> 6; matrix products, arithmetic and copies ran while one was open for 3% -> 3% of each run, Pallas kernels for 1% -> 1%
where the time goes in v9:
time: 160 us
  starting transfers between devices  66.7 us (42%)
  blocking collectives  46 us (29%)
  waiting for transfers between devices  35.6 us (22%)
  matrix products  5.75 us (4%)
  Pallas kernels  2.03 us (1%)
    ppermute x4, starting transfers between devices, swap_far(): return lax.ppermute(part.astype(BF16), ('zh', 'core'), pairs)  44.5 us
    all_to_all x1, blocking collectives, shards(): both = lax.all_to_all(both, 'zl', 0, 0)  22.6 us
    all_to_all x1, waiting for transfers between devices, shards(): ends = lax.all_to_all(ends, SECTION, 0, 0).astype(F32).sum(0).astype(BF16)  15.8 us
    ppermute x2, starting transfers between devices, swap_core(): return lax.ppermute(block, 'core', [(0, 1), (1, 0)])  14.2 us
    all_to_all x1, blocking collectives, sum_over_x(): return lax.all_to_all(pieces, 'x', 0, 0).astype(F32).sum(0)  13.2 us
    ppermute x4, waiting for transfers between devices, swap_far(): return lax.ppermute(part.astype(BF16), ('zh', 'core'), pairs)  12.9 us
    all_to_all x1, blocking collectives, copies_over_x(): return lax.all_to_all(copies, 'x', 0, 0)  10.2 us
    all_to_all x1, waiting for transfers between devices, shards(): both = lax.all_to_all(both, 'y', 0, 0).reshape(rows, 2 * width)  4.2 us
  transfers between devices with their start and end apart: 8, of which 6 were waited for; matrix products, arithmetic and copies ran while one was open for 3% of the time, Pallas kernels for 1%

profile of v9, /device:TPU:1, one launch (start us, length us, event | category | flops | bytes accessed | tf_op | source)
XLA Modules:
  0.0 159.9 jit_solution(318148741321272377)
XLA Ops:
  0.6 0.7 shard_map.92
  1.3 22.6 %all_to_all.25 = bf16[8,8,512]{2,1,0:T(8,128)(2,1)S(1)} all-to-all(bf16[8,8,512]{2,1,0:T(8,128)(2,1)S(1)} %shard_map.92), channel_id=1, replica_groups=mesh['y'=4,'zl'=8,'zh'=4,'x'=4,'core'=2] {'zl'}, dimensions={0} | all-to-all | bytes 131072 | tf_op jit(solution)/shard_map/all_to_all | solution.py:114
  24.0 0.7 broadcast_in_dim.4
  24.7 4.2 %all-to-all-start.1 = ((bf16[4,8,8,512]{3,2,1,0:T(8,128)(2,1)}), bf16[4,8,8,512]{3,2,1,0:T(8,128)(2,1)S(1)}, u32[]{:S(2)}, u32[]{:S(2)}) async-start(bf16[4,8,8,512]{3,2,1,0:T(8,128)(2,1)} %broadcast_in_dim.4), calls=%async_computation.1 | async-start | bytes 524288 | tf_op jit(solution)/shard_map/all_to_all | solution.py:116
  28.9 1.3 shard_map.93
  30.2 4.2 %all-to-all-done.1 = bf16[4,8,8,512]{3,2,1,0:T(8,128)(2,1)S(1)} async-done(((bf16[4,8,8,512]{3,2,1,0:T(8,128)(2,1)}), bf16[4,8,8,512]{3,2,1,0:T(8,128)(2,1)S(1)}, u32[]{:S(2)}, u32[]{:S(2)}) %all-to-all-start.1) | async-done | bytes 262176 | tf_op jit(solution)/shard_map/all_to_all | solution.py:116
  34.9 0.3 convolution_convert_fusion.3
  35.2 7.1 %collective-permute-start = (bf16[128,2688]{1,0:T(8,128)(2,1)S(1)}, bf16[128,2688]{1,0:T(8,128)(2,1)S(1)}, u32[]{:S(2)}, u32[]{:S(2)}) collective-permute-start(bf16[128,2688]{1,0:T(8,128)(2,1)S(1)} %pad_maximum_fusion.1), channel_id=1, source_target_pairs={{0,1},{1,0},{2,3},{3,2},{4,5},{5,4},{6,7},{7,6},{8,9},{9,8},{10,11... | collective-permute-start | bytes 2064392 | tf_op jit(solution)/shard_map/ppermute | solution.py:65
  42.3 0.3 fusion.18
  42.6 0.2 fusion.22
  42.8 0.2 fusion.24
  43.1 1.0 collective-permute-done
  44.2 13.2 %all_to_all.26 = bf16[4,32,2688]{2,1,0:T(8,128)(2,1)S(1)} all-to-all(bf16[4,32,2688]{2,1,0:T(8,128)(2,1)S(1)} %bitcast.35), channel_id=1, replica_groups=mesh['y'=4,'zl'=8,'zh'=4,'x'=4,'core'=2] {'x'}, dimensions={0} | all-to-all | bytes 1376256 | tf_op jit(solution)/shard_map/all_to_all | solution.py:72
  57.6 14.8 %collective-permute-start.1 = (bf16[16,2688]{1,0:T(8,128)(2,1)S(1)}, bf16[16,2688]{1,0:T(8,128)(2,1)S(1)}, u32[]{:S(2)}, u32[]{:S(2)}) collective-permute-start(bf16[16,2688]{1,0:T(8,128)(2,1)S(1)} %get-tuple-element.20), channel_id=1, source_target_pairs={{0,8},{1,25},{8,0},{9,17},{16,24},{17,9},{24,16},{25,1},{2,10},{3,... | collective-permute-start | bytes 258056 | tf_op jit(solution)/shard_map/ppermute | solution.py:81
  72.4 8.2 %collective-permute-start.3 = (bf16[16,2688]{1,0:T(8,128)(2,1)S(1)}, bf16[16,2688]{1,0:T(8,128)(2,1)S(1)}, u32[]{:S(2)}, u32[]{:S(2)}) collective-permute-start(bf16[16,2688]{1,0:T(8,128)(2,1)S(1)} %get-tuple-element.21), channel_id=1, source_target_pairs={{0,24},{1,9},{8,16},{9,1},{16,8},{17,25},{24,0},{25,17},{2,26},{3,... | collective-permute-start | bytes 258056 | tf_op jit(solution)/shard_map/ppermute | solution.py:81
  80.6 19.6 %collective-permute-start.2 = (bf16[16,2688]{1,0:T(8,128)(2,1)S(1)}, bf16[16,2688]{1,0:T(8,128)(2,1)S(1)}, u32[]{:S(2)}, u32[]{:S(2)}) collective-permute-start(bf16[16,2688]{1,0:T(8,128)(2,1)S(1)} %get-tuple-element.13), channel_id=1, source_target_pairs={{0,24},{1,9},{8,16},{9,1},{16,8},{17,25},{24,0},{25,17},{2,26},{3,... | collective-permute-start | bytes 258056 | tf_op jit(solution)/shard_map/ppermute | solution.py:81
  100.2 1.9 %collective-permute-start.4 = (bf16[16,2688]{1,0:T(8,128)(2,1)S(1)}, bf16[16,2688]{1,0:T(8,128)(2,1)S(1)}, u32[]{:S(2)}, u32[]{:S(2)}) collective-permute-start(bf16[16,2688]{1,0:T(8,128)(2,1)S(1)} %fusion.16), channel_id=1, source_target_pairs={{0,8},{1,25},{8,0},{9,17},{16,24},{17,9},{24,16},{25,1},{2,10},{3,... | collective-permute-start | bytes 258056 | tf_op jit(solution)/shard_map/ppermute | solution.py:81
  102.1 3.3 %collective-permute-done.2 = bf16[16,2688]{1,0:T(8,128)(2,1)S(1)} collective-permute-done((bf16[16,2688]{1,0:T(8,128)(2,1)S(1)}, bf16[16,2688]{1,0:T(8,128)(2,1)S(1)}, u32[]{:S(2)}, u32[]{:S(2)}) %collective-permute-start.2) | collective-permute-done | bytes 86048 | tf_op jit(solution)/shard_map/ppermute | solution.py:81
  105.5 9.6 %collective-permute-done.4 = bf16[16,2688]{1,0:T(8,128)(2,1)S(1)} collective-permute-done((bf16[16,2688]{1,0:T(8,128)(2,1)S(1)}, bf16[16,2688]{1,0:T(8,128)(2,1)S(1)}, u32[]{:S(2)}, u32[]{:S(2)}) %collective-permute-start.4) | collective-permute-done | bytes 86048 | tf_op jit(solution)/shard_map/ppermute | solution.py:81
  115.2 10.2 %all_to_all.27 = bf16[4,32,2688]{2,1,0:T(8,128)(2,1)S(1)} all-to-all(bf16[4,32,2688]{2,1,0:T(8,128)(2,1)S(1)} %broadcast_in_dim.5), channel_id=1, replica_groups=mesh['y'=4,'zl'=8,'zh'=4,'x'=4,'core'=2] {'x'}, dimensions={0} | all-to-all | bytes 1376256 | tf_op jit(solution)/shard_map/all_to_all | solution.py:102
  125.4 7.1 %collective-permute-start.5 = (bf16[4,32,2688]{2,1,0:T(8,128)(2,1)S(1)}, bf16[4,32,2688]{2,1,0:T(8,128)(2,1)S(1)}, u32[]{:S(2)}, u32[]{:S(2)}) collective-permute-start(bf16[4,32,2688]{2,1,0:T(8,128)(2,1)S(1)} %all_to_all.27), channel_id=1, source_target_pairs={{0,1},{1,0},{2,3},{3,2},{4,5},{5,4},{6,7},{7,6},{8,9},{9,8},{10,11... | collective-permute-start | bytes 2064392 | tf_op jit(solution)/shard_map/ppermute | solution.py:65
  132.6 1.7 %collective-permute-done.5 = bf16[4,32,2688]{2,1,0:T(8,128)(2,1)S(1)} collective-permute-done((bf16[4,32,2688]{2,1,0:T(8,128)(2,1)S(1)}, bf16[4,32,2688]{2,1,0:T(8,128)(2,1)S(1)}, u32[]{:S(2)}, u32[]{:S(2)}) %collective-permute-start.5) | collective-permute-done | bytes 688160 | tf_op jit(solution)/shard_map/ppermute | solution.py:65
  134.6 0.3 fusion.2
  134.9 0.3 fusion.7
  135.2 0.3 fusion.3
  135.6 0.7 pad_maximum_fusion.2
  136.3 3.9 %all-to-all-start.4 = ((bf16[32,8,512]{2,1,0:T(8,128)(2,1)}), bf16[32,8,512]{2,1,0:T(8,128)(2,1)S(1)}, u32[]{:S(2)}, u32[]{:S(2)}) async-start(bf16[32,8,512]{2,1,0:T(8,128)(2,1)} %pad_maximum_fusion.2), calls=%async_computation.4 | async-start | bytes 524288 | tf_op jit(solution)/shard_map/all_to_all | solution.py:160
  140.2 1.1 convolution_convert_fusion
  141.3 1.1 convolution_convert_fusion.1
  142.4 1.1 convolution_convert_fusion.2
  143.5 15.8 %all-to-all-done.4 = bf16[32,8,512]{2,1,0:T(8,128)(2,1)S(1)} async-done(((bf16[32,8,512]{2,1,0:T(8,128)(2,1)}), bf16[32,8,512]{2,1,0:T(8,128)(2,1)S(1)}, u32[]{:S(2)}, u32[]{:S(2)}) %all-to-all-start.4) | async-done | bytes 262176 | tf_op jit(solution)/shard_map/all_to_all | solution.py:160
  159.3 0.6 fusion.32
  (18 shorter events, 1.3 us)
Async XLA Ops:
  24.7 9.7 %all-to-all-start.1 = ((bf16[4,8,8,512]{3,2,1,0:T(8,128)(2,1)}), bf16[4,8,8,512]{3,2,1,0:T(8,128)(2,1)S(1)}, u32[]{:S(2)}, u32[]{:S(2)}) async-start(bf16[4,8,8,512]{3,2,1,0:T(8,128)(2,1)} %broadcast_in_dim.4), calls=%async_computation.1 | async-start | bytes 524288 | tf_op jit(solution)/shard_map/all_to_all | solution.py:116
  35.2 8.8 %collective-permute-start = (bf16[128,2688]{1,0:T(8,128)(2,1)S(1)}, bf16[128,2688]{1,0:T(8,128)(2,1)S(1)}, u32[]{:S(2)}, u32[]{:S(2)}) collective-permute-start(bf16[128,2688]{1,0:T(8,128)(2,1)S(1)} %pad_maximum_fusion.1), channel_id=1, source_target_pairs={{0,1},{1,0},{2,3},{3,2},{4,5},{5,4},{6,7},{7,6},{8,9},{9,8},{10,11... | collective-permute-start | bytes 2064392 | tf_op jit(solution)/shard_map/ppermute | solution.py:65
  57.6 23.0 %collective-permute-start.1 = (bf16[16,2688]{1,0:T(8,128)(2,1)S(1)}, bf16[16,2688]{1,0:T(8,128)(2,1)S(1)}, u32[]{:S(2)}, u32[]{:S(2)}) collective-permute-start(bf16[16,2688]{1,0:T(8,128)(2,1)S(1)} %get-tuple-element.20), channel_id=1, source_target_pairs={{0,8},{1,25},{8,0},{9,17},{16,24},{17,9},{24,16},{25,1},{2,10},{3,... | collective-permute-start | bytes 258056 | tf_op jit(solution)/shard_map/ppermute | solution.py:81
  72.4 27.8 %collective-permute-start.3 = (bf16[16,2688]{1,0:T(8,128)(2,1)S(1)}, bf16[16,2688]{1,0:T(8,128)(2,1)S(1)}, u32[]{:S(2)}, u32[]{:S(2)}) collective-permute-start(bf16[16,2688]{1,0:T(8,128)(2,1)S(1)} %get-tuple-element.21), channel_id=1, source_target_pairs={{0,24},{1,9},{8,16},{9,1},{16,8},{17,25},{24,0},{25,17},{2,26},{3,... | collective-permute-start | bytes 258056 | tf_op jit(solution)/shard_map/ppermute | solution.py:81
  80.6 24.9 %collective-permute-start.2 = (bf16[16,2688]{1,0:T(8,128)(2,1)S(1)}, bf16[16,2688]{1,0:T(8,128)(2,1)S(1)}, u32[]{:S(2)}, u32[]{:S(2)}) collective-permute-start(bf16[16,2688]{1,0:T(8,128)(2,1)S(1)} %get-tuple-element.13), channel_id=1, source_target_pairs={{0,24},{1,9},{8,16},{9,1},{16,8},{17,25},{24,0},{25,17},{2,26},{3,... | collective-permute-start | bytes 258056 | tf_op jit(solution)/shard_map/ppermute | solution.py:81
  100.2 14.8 %collective-permute-start.4 = (bf16[16,2688]{1,0:T(8,128)(2,1)S(1)}, bf16[16,2688]{1,0:T(8,128)(2,1)S(1)}, u32[]{:S(2)}, u32[]{:S(2)}) collective-permute-start(bf16[16,2688]{1,0:T(8,128)(2,1)S(1)} %fusion.16), channel_id=1, source_target_pairs={{0,8},{1,25},{8,0},{9,17},{16,24},{17,9},{24,16},{25,1},{2,10},{3,... | collective-permute-start | bytes 258056 | tf_op jit(solution)/shard_map/ppermute | solution.py:81
  125.4 8.9 %collective-permute-start.5 = (bf16[4,32,2688]{2,1,0:T(8,128)(2,1)S(1)}, bf16[4,32,2688]{2,1,0:T(8,128)(2,1)S(1)}, u32[]{:S(2)}, u32[]{:S(2)}) collective-permute-start(bf16[4,32,2688]{2,1,0:T(8,128)(2,1)S(1)} %all_to_all.27), channel_id=1, source_target_pairs={{0,1},{1,0},{2,3},{3,2},{4,5},{5,4},{6,7},{7,6},{8,9},{9,8},{10,11... | collective-permute-start | bytes 2064392 | tf_op jit(solution)/shard_map/ppermute | solution.py:65
  136.3 22.9 %all-to-all-start.4 = ((bf16[32,8,512]{2,1,0:T(8,128)(2,1)}), bf16[32,8,512]{2,1,0:T(8,128)(2,1)S(1)}, u32[]{:S(2)}, u32[]{:S(2)}) async-start(bf16[32,8,512]{2,1,0:T(8,128)(2,1)} %pad_maximum_fusion.2), calls=%async_computation.4 | async-start | bytes 524288 | tf_op jit(solution)/shard_map/all_to_all | solution.py:160

commit v10 on v9

--- a/solution.py
+++ b/solution.py
@@ -141,21 +141,34 @@
     low = low + low_in
     low_in = swap_far(low, (1, 3))
     mine = copies_over_x(deltas_of(jnp.concatenate([top + top_in, low + low_in])))
+    mine = mine.reshape(half, 3 * units)
     theirs = swap_core(mine)
-    first = core == 0
-    whole = jnp.stack(
-        [jnp.where(first, mine, theirs), jnp.where(first, theirs, mine)]
-    ).reshape(rows, 3 * units)
+
+    def ends_of(some):
+        forward_part = jnp.dot(
+            some[:, :units], down_weight, preferred_element_type=F32
+        )
+        backward_part = contract_last(
+            some[:, units : 2 * units], gate_weight
+        ) + contract_last(some[:, 2 * units :], up_weight)
+        return jnp.concatenate([forward_part, backward_part], axis=1).astype(BF16)
+
+    def in_order(own_rows, other_rows):
+        first = core == 0
+        return jnp.stack(
+            [
+                jnp.where(first, own_rows, other_rows),
+                jnp.where(first, other_rows, own_rows),
+            ]
+        )
+
+    ends = in_order(ends_of(mine), ends_of(theirs))
+    whole = in_order(mine, theirs).reshape(rows, 3 * units)
     hidden, gate_delta, up_delta = (
         whole[:, :units],
         whole[:, units : 2 * units],
         whole[:, 2 * units :],
     )
-    forward_part = jnp.dot(hidden, down_weight, preferred_element_type=F32)
-    backward_part = contract_last(gate_delta, gate_weight) + contract_last(
-        up_delta, up_weight
-    )
-    ends = jnp.concatenate([forward_part, backward_part], axis=1).astype(BF16)
     ends = ends.reshape(sections, own, 2 * width)
     ends = lax.all_to_all(ends, SECTION, 0, 0).astype(F32).sum(0).astype(BF16)
     all_tokens, all_grads = both[:, :width], both[:, width:]

time: 160 us -> 162 us (1.012)
  starting transfers between devices: 66.7 us -> 58.4 us
  waiting for transfers between devices: 35.6 us -> 40.7 us
  blocking collectives: 46 us -> 49.7 us
    ppermute x4, waiting for transfers between devices: 12.9 us -> 19.2 us  [swap_far(): return lax.ppermute(part.astype(BF16), ('zh', 'core'), pairs)]
    ppermute x2, starting transfers between devices: 14.2 us -> 9.68 us  [swap_core(): return lax.ppermute(block, 'core', [(0, 1), (1, 0)])]
    ppermute x4, starting transfers between devices: 44.5 us -> 40.6 us  [swap_far(): return lax.ppermute(part.astype(BF16), ('zh', 'core'), pairs)]
    all_to_all x1, blocking collectives: 10.2 us -> 13.9 us  [copies_over_x(): return lax.all_to_all(copies, 'x', 0, 0)]
  transfers between devices with their start and end apart: 8 -> 8, of which waited for: 6 -> 7; matrix products, arithmetic and copies ran while one was open for 3% -> 3% of each run, Pallas kernels for 1% -> 1%
where the time goes in v10:
time: 162 us; the launch traced here: 161 us
  starting transfers between devices  58.4 us (36%)
  blocking collectives  49.7 us (31%)
  waiting for transfers between devices  40.7 us (25%)
  matrix products  6.45 us (4%)
  Pallas kernels  2.03 us (1%)
  other arithmetic  1.62 us (1%)
    ppermute x4, starting transfers between devices, swap_far(): return lax.ppermute(part.astype(BF16), ('zh', 'core'), pairs)  40.6 us
    all_to_all x1, blocking collectives, shards(): both = lax.all_to_all(both, 'zl', 0, 0)  22.6 us
    ppermute x4, waiting for transfers between devices, swap_far(): return lax.ppermute(part.astype(BF16), ('zh', 'core'), pairs)  19.2 us
    all_to_all x1, waiting for transfers between devices, shards(): ends = lax.all_to_all(ends, SECTION, 0, 0).astype(F32).sum(0).astype(BF16)  15.4 us
    all_to_all x1, blocking collectives, copies_over_x(): return lax.all_to_all(copies, 'x', 0, 0)  13.9 us
    all_to_all x1, blocking collectives, sum_over_x(): return lax.all_to_all(pieces, 'x', 0, 0).astype(F32).sum(0)  13.2 us
    ppermute x2, starting transfers between devices, swap_core(): return lax.ppermute(block, 'core', [(0, 1), (1, 0)])  9.68 us
    all_to_all x1, waiting for transfers between devices, shards(): both = lax.all_to_all(both, 'y', 0, 0).reshape(rows, 2 * width)  4.2 us
  transfers between devices with their start and end apart: 8, of which 7 were waited for; matrix products, arithmetic and copies ran while one was open for 3% of the time, Pallas kernels for 1%

profile of v10, /device:TPU:1, one launch (start us, length us, event | category | flops | bytes accessed | tf_op | source)
XLA Modules:
  0.0 161.1 jit_solution(5344810397051760803)
XLA Ops:
  0.6 0.7 shard_map.92
  1.3 22.6 %all_to_all.25 = bf16[8,8,512]{2,1,0:T(8,128)(2,1)S(1)} all-to-all(bf16[8,8,512]{2,1,0:T(8,128)(2,1)S(1)} %shard_map.92), channel_id=1, replica_groups=mesh['y'=4,'zl'=8,'zh'=4,'x'=4,'core'=2] {'zl'}, dimensions={0} | all-to-all | bytes 131072 | tf_op jit(solution)/shard_map/all_to_all | solution.py:114
  24.0 0.7 broadcast_in_dim.4
  24.7 4.2 %all-to-all-start.1 = ((bf16[4,8,8,512]{3,2,1,0:T(8,128)(2,1)}), bf16[4,8,8,512]{3,2,1,0:T(8,128)(2,1)S(1)}, u32[]{:S(2)}, u32[]{:S(2)}) async-start(bf16[4,8,8,512]{3,2,1,0:T(8,128)(2,1)} %broadcast_in_dim.4), calls=%async_computation.1 | async-start | bytes 524288 | tf_op jit(solution)/shard_map/all_to_all | solution.py:116
  28.9 1.3 shard_map.93
  30.2 4.2 %all-to-all-done.1 = bf16[4,8,8,512]{3,2,1,0:T(8,128)(2,1)S(1)} async-done(((bf16[4,8,8,512]{3,2,1,0:T(8,128)(2,1)}), bf16[4,8,8,512]{3,2,1,0:T(8,128)(2,1)S(1)}, u32[]{:S(2)}, u32[]{:S(2)}) %all-to-all-start.1) | async-done | bytes 262176 | tf_op jit(solution)/shard_map/all_to_all | solution.py:116
  34.9 0.3 convolution_convert_fusion.3
  35.2 7.1 %collective-permute-start = (bf16[128,2688]{1,0:T(8,128)(2,1)S(1)}, bf16[128,2688]{1,0:T(8,128)(2,1)S(1)}, u32[]{:S(2)}, u32[]{:S(2)}) collective-permute-start(bf16[128,2688]{1,0:T(8,128)(2,1)S(1)} %pad_maximum_fusion.1), channel_id=1, source_target_pairs={{0,1},{1,0},{2,3},{3,2},{4,5},{5,4},{6,7},{7,6},{8,9},{9,8},{10,11... | collective-permute-start | bytes 2064392 | tf_op jit(solution)/shard_map/ppermute | solution.py:65
  42.3 0.3 fusion.25
  43.1 1.0 collective-permute-done
  44.2 13.2 %all_to_all.26 = bf16[4,32,2688]{2,1,0:T(8,128)(2,1)S(1)} all-to-all(bf16[4,32,2688]{2,1,0:T(8,128)(2,1)S(1)} %bitcast.47), channel_id=1, replica_groups=mesh['y'=4,'zl'=8,'zh'=4,'x'=4,'core'=2] {'x'}, dimensions={0} | all-to-all | bytes 1376256 | tf_op jit(solution)/shard_map/all_to_all | solution.py:72
  57.5 14.8 %collective-permute-start.1 = (bf16[16,2688]{1,0:T(8,128)(2,1)S(1)}, bf16[16,2688]{1,0:T(8,128)(2,1)S(1)}, u32[]{:S(2)}, u32[]{:S(2)}) collective-permute-start(bf16[16,2688]{1,0:T(8,128)(2,1)S(1)} %get-tuple-element.20), channel_id=1, source_target_pairs={{0,8},{1,25},{8,0},{9,17},{16,24},{17,9},{24,16},{25,1},{2,10},{3,... | collective-permute-start | bytes 258056 | tf_op jit(solution)/shard_map/ppermute | solution.py:81
  72.4 8.2 %collective-permute-start.3 = (bf16[16,2688]{1,0:T(8,128)(2,1)S(1)}, bf16[16,2688]{1,0:T(8,128)(2,1)S(1)}, u32[]{:S(2)}, u32[]{:S(2)}) collective-permute-start(bf16[16,2688]{1,0:T(8,128)(2,1)S(1)} %get-tuple-element.21), channel_id=1, source_target_pairs={{0,24},{1,9},{8,16},{9,1},{16,8},{17,25},{24,0},{25,17},{2,26},{3,... | collective-permute-start | bytes 258056 | tf_op jit(solution)/shard_map/ppermute | solution.py:81
  80.6 11.8 %collective-permute-done.3 = bf16[16,2688]{1,0:T(8,128)(2,1)S(1)} collective-permute-done((bf16[16,2688]{1,0:T(8,128)(2,1)S(1)}, bf16[16,2688]{1,0:T(8,128)(2,1)S(1)}, u32[]{:S(2)}, u32[]{:S(2)}) %collective-permute-start.3) | collective-permute-done | bytes 86048 | tf_op jit(solution)/shard_map/ppermute | solution.py:81
  92.4 5.0 %collective-permute-start.4 = (bf16[16,2688]{1,0:T(8,128)(2,1)S(1)}, bf16[16,2688]{1,0:T(8,128)(2,1)S(1)}, u32[]{:S(2)}, u32[]{:S(2)}) collective-permute-start(bf16[16,2688]{1,0:T(8,128)(2,1)S(1)} %fusion.23), channel_id=1, source_target_pairs={{0,8},{1,25},{8,0},{9,17},{16,24},{17,9},{24,16},{25,1},{2,10},{3,... | collective-permute-start | bytes 258056 | tf_op jit(solution)/shard_map/ppermute | solution.py:81
  97.4 12.6 %collective-permute-start.2 = (bf16[16,2688]{1,0:T(8,128)(2,1)S(1)}, bf16[16,2688]{1,0:T(8,128)(2,1)S(1)}, u32[]{:S(2)}, u32[]{:S(2)}) collective-permute-start(bf16[16,2688]{1,0:T(8,128)(2,1)S(1)} %get-tuple-element.13), channel_id=1, source_target_pairs={{0,24},{1,9},{8,16},{9,1},{16,8},{17,25},{24,0},{25,17},{2,26},{3,... | collective-permute-start | bytes 258056 | tf_op jit(solution)/shard_map/ppermute | solution.py:81
  110.0 5.4 %collective-permute-done.4 = bf16[16,2688]{1,0:T(8,128)(2,1)S(1)} collective-permute-done((bf16[16,2688]{1,0:T(8,128)(2,1)S(1)}, bf16[16,2688]{1,0:T(8,128)(2,1)S(1)}, u32[]{:S(2)}, u32[]{:S(2)}) %collective-permute-start.4) | collective-permute-done | bytes 86048 | tf_op jit(solution)/shard_map/ppermute | solution.py:81
  115.5 2.0 %collective-permute-done.2 = bf16[16,2688]{1,0:T(8,128)(2,1)S(1)} collective-permute-done((bf16[16,2688]{1,0:T(8,128)(2,1)S(1)}, bf16[16,2688]{1,0:T(8,128)(2,1)S(1)}, u32[]{:S(2)}, u32[]{:S(2)}) %collective-permute-start.2) | collective-permute-done | bytes 86048 | tf_op jit(solution)/shard_map/ppermute | solution.py:81
  117.7 13.9 %all_to_all.27 = bf16[4,32,2688]{2,1,0:T(8,128)(2,1)S(1)} all-to-all(bf16[4,32,2688]{2,1,0:T(8,128)(2,1)S(1)} %broadcast_in_dim.5), channel_id=1, replica_groups=mesh['y'=4,'zl'=8,'zh'=4,'x'=4,'core'=2] {'x'}, dimensions={0} | all-to-all | bytes 1376256 | tf_op jit(solution)/shard_map/all_to_all | solution.py:102
  131.5 2.6 %collective-permute-start.5 = (bf16[128,2688]{1,0:T(8,128)(2,1)S(1)}, bf16[128,2688]{1,0:T(8,128)(2,1)S(1)}, u32[]{:S(2)}, u32[]{:S(2)}) collective-permute-start(bf16[128,2688]{1,0:T(8,128)(2,1)S(1)} %bitcast.31), channel_id=1, source_target_pairs={{0,1},{1,0},{2,3},{3,2},{4,5},{5,4},{6,7},{7,6},{8,9},{9,8},{10,11... | collective-permute-start | bytes 2064392 | tf_op jit(solution)/shard_map/ppermute | solution.py:65
  134.4 0.3 fusion.15
  134.7 0.3 fusion.6
  135.0 0.9 collective-permute-done.5
  136.1 0.3 fusion.10
  136.4 0.3 fusion.5
  136.8 0.7 pad_maximum_fusion.2
  137.5 3.9 %all-to-all-start.4 = ((bf16[32,8,512]{2,1,0:T(8,128)(2,1)}), bf16[32,8,512]{2,1,0:T(8,128)(2,1)S(1)}, u32[]{:S(2)}, u32[]{:S(2)}) async-start(bf16[32,8,512]{2,1,0:T(8,128)(2,1)} %bitcast.7), calls=%async_computation.4 | async-start | bytes 524288 | tf_op jit(solution)/shard_map/all_to_all | solution.py:173
  141.7 1.1 convolution_convert_fusion
  142.9 1.1 convolution_convert_fusion.1
  144.0 1.1 convolution_convert_fusion.2
  145.1 15.4 %all-to-all-done.4 = bf16[32,8,512]{2,1,0:T(8,128)(2,1)S(1)} async-done(((bf16[32,8,512]{2,1,0:T(8,128)(2,1)}), bf16[32,8,512]{2,1,0:T(8,128)(2,1)S(1)}, u32[]{:S(2)}, u32[]{:S(2)}) %all-to-all-start.4) | async-done | bytes 262176 | tf_op jit(solution)/shard_map/all_to_all | solution.py:173
  160.5 0.6 fusion.39
  (22 shorter events, 2.3 us)
Async XLA Ops:
  24.7 9.7 %all-to-all-start.1 = ((bf16[4,8,8,512]{3,2,1,0:T(8,128)(2,1)}), bf16[4,8,8,512]{3,2,1,0:T(8,128)(2,1)S(1)}, u32[]{:S(2)}, u32[]{:S(2)}) async-start(bf16[4,8,8,512]{3,2,1,0:T(8,128)(2,1)} %broadcast_in_dim.4), calls=%async_computation.1 | async-start | bytes 524288 | tf_op jit(solution)/shard_map/all_to_all | solution.py:116
  35.2 8.8 %collective-permute-start = (bf16[128,2688]{1,0:T(8,128)(2,1)S(1)}, bf16[128,2688]{1,0:T(8,128)(2,1)S(1)}, u32[]{:S(2)}, u32[]{:S(2)}) collective-permute-start(bf16[128,2688]{1,0:T(8,128)(2,1)S(1)} %pad_maximum_fusion.1), channel_id=1, source_target_pairs={{0,1},{1,0},{2,3},{3,2},{4,5},{5,4},{6,7},{7,6},{8,9},{9,8},{10,11... | collective-permute-start | bytes 2064392 | tf_op jit(solution)/shard_map/ppermute | solution.py:65
  57.5 23.0 %collective-permute-start.1 = (bf16[16,2688]{1,0:T(8,128)(2,1)S(1)}, bf16[16,2688]{1,0:T(8,128)(2,1)S(1)}, u32[]{:S(2)}, u32[]{:S(2)}) collective-permute-start(bf16[16,2688]{1,0:T(8,128)(2,1)S(1)} %get-tuple-element.20), channel_id=1, source_target_pairs={{0,8},{1,25},{8,0},{9,17},{16,24},{17,9},{24,16},{25,1},{2,10},{3,... | collective-permute-start | bytes 258056 | tf_op jit(solution)/shard_map/ppermute | solution.py:81
  72.4 20.0 %collective-permute-start.3 = (bf16[16,2688]{1,0:T(8,128)(2,1)S(1)}, bf16[16,2688]{1,0:T(8,128)(2,1)S(1)}, u32[]{:S(2)}, u32[]{:S(2)}) collective-permute-start(bf16[16,2688]{1,0:T(8,128)(2,1)S(1)} %get-tuple-element.21), channel_id=1, source_target_pairs={{0,24},{1,9},{8,16},{9,1},{16,8},{17,25},{24,0},{25,17},{2,26},{3,... | collective-permute-start | bytes 258056 | tf_op jit(solution)/shard_map/ppermute | solution.py:81
  92.4 23.1 %collective-permute-start.4 = (bf16[16,2688]{1,0:T(8,128)(2,1)S(1)}, bf16[16,2688]{1,0:T(8,128)(2,1)S(1)}, u32[]{:S(2)}, u32[]{:S(2)}) collective-permute-start(bf16[16,2688]{1,0:T(8,128)(2,1)S(1)} %fusion.23), channel_id=1, source_target_pairs={{0,8},{1,25},{8,0},{9,17},{16,24},{17,9},{24,16},{25,1},{2,10},{3,... | collective-permute-start | bytes 258056 | tf_op jit(solution)/shard_map/ppermute | solution.py:81
  97.4 20.1 %collective-permute-start.2 = (bf16[16,2688]{1,0:T(8,128)(2,1)S(1)}, bf16[16,2688]{1,0:T(8,128)(2,1)S(1)}, u32[]{:S(2)}, u32[]{:S(2)}) collective-permute-start(bf16[16,2688]{1,0:T(8,128)(2,1)S(1)} %get-tuple-element.13), channel_id=1, source_target_pairs={{0,24},{1,9},{8,16},{9,1},{16,8},{17,25},{24,0},{25,17},{2,26},{3,... | collective-permute-start | bytes 258056 | tf_op jit(solution)/shard_map/ppermute | solution.py:81
  131.5 4.4 %collective-permute-start.5 = (bf16[128,2688]{1,0:T(8,128)(2,1)S(1)}, bf16[128,2688]{1,0:T(8,128)(2,1)S(1)}, u32[]{:S(2)}, u32[]{:S(2)}) collective-permute-start(bf16[128,2688]{1,0:T(8,128)(2,1)S(1)} %bitcast.31), channel_id=1, source_target_pairs={{0,1},{1,0},{2,3},{3,2},{4,5},{5,4},{6,7},{7,6},{8,9},{9,8},{10,11... | collective-permute-start | bytes 2064392 | tf_op jit(solution)/shard_map/ppermute | solution.py:65
  137.5 22.9 %all-to-all-start.4 = ((bf16[32,8,512]{2,1,0:T(8,128)(2,1)}), bf16[32,8,512]{2,1,0:T(8,128)(2,1)S(1)}, u32[]{:S(2)}, u32[]{:S(2)}) async-start(bf16[32,8,512]{2,1,0:T(8,128)(2,1)} %bitcast.7), calls=%async_computation.4 | async-start | bytes 524288 | tf_op jit(solution)/shard_map/all_to_all | solution.py:173

commit v11 on v10

--- a/solution.py
+++ b/solution.py
@@ -136,8 +136,9 @@
     top, low = part[:piece], part[piece:]
     top_in, low_in = swap_far(top, (1, 3)), swap_far(low, (3, 1))
     top = top + top_in
-    low_in, _ = lax.optimization_barrier((low_in, top))
-    top_in = swap_far(top, (3, 1))
+    sent = top.astype(BF16)
+    low_in, _ = lax.optimization_barrier((low_in, sent))
+    top_in = swap_far(sent, (3, 1))
     low = low + low_in
     low_in = swap_far(low, (1, 3))
     mine = copies_over_x(deltas_of(jnp.concatenate([top + top_in, low + low_in])))

time: 162 us -> 160 us (0.988)
  starting transfers between devices: 58.4 us -> 66.6 us
  waiting for transfers between devices: 40.7 us -> 34.5 us
  blocking collectives: 49.7 us -> 46 us
    ppermute x4, waiting for transfers between devices: 19.2 us -> 13 us  [swap_far(): return lax.ppermute(part.astype(BF16), ('zh', 'core'), pairs)]
    ppermute x2, starting transfers between devices: 9.68 us -> 14.1 us  [swap_core(): return lax.ppermute(block, 'core', [(0, 1), (1, 0)])]
    ppermute x4, starting transfers between devices: 40.6 us -> 44.5 us  [swap_far(): return lax.ppermute(part.astype(BF16), ('zh', 'core'), pairs)]
    all_to_all x1, blocking collectives: 13.9 us -> 10.2 us  [copies_over_x(): return lax.all_to_all(copies, 'x', 0, 0)]
  transfers between devices with their start and end apart: 8 -> 8, of which waited for: 7 -> 6; matrix products, arithmetic and copies ran while one was open for 3% -> 3% of each run, Pallas kernels for 1% -> 1%
where the time goes in v11:
time: 160 us
  starting transfers between devices  66.6 us (42%)
  blocking collectives  46 us (29%)
  waiting for transfers between devices  34.5 us (22%)
  matrix products  6.45 us (4%)
  Pallas kernels  2.03 us (1%)
  other arithmetic  1.62 us (1%)
    ppermute x4, starting transfers between devices, swap_far(): return lax.ppermute(part.astype(BF16), ('zh', 'core'), pairs)  44.5 us
    all_to_all x1, blocking collectives, shards(): both = lax.all_to_all(both, 'zl', 0, 0)  22.6 us
    all_to_all x1, waiting for transfers between devices, shards(): ends = lax.all_to_all(ends, SECTION, 0, 0).astype(F32).sum(0).astype(BF16)  15.4 us
    ppermute x2, starting transfers between devices, swap_core(): return lax.ppermute(block, 'core', [(0, 1), (1, 0)])  14.1 us
    all_to_all x1, blocking collectives, sum_over_x(): return lax.all_to_all(pieces, 'x', 0, 0).astype(F32).sum(0)  13.2 us
    ppermute x4, waiting for transfers between devices, swap_far(): return lax.ppermute(part.astype(BF16), ('zh', 'core'), pairs)  13 us
    all_to_all x1, blocking collectives, copies_over_x(): return lax.all_to_all(copies, 'x', 0, 0)  10.2 us
    all_to_all x1, waiting for transfers between devices, shards(): both = lax.all_to_all(both, 'y', 0, 0).reshape(rows, 2 * width)  4.2 us
  transfers between devices with their start and end apart: 8, of which 6 were waited for; matrix products, arithmetic and copies ran while one was open for 3% of the time, Pallas kernels for 1%

profile of v11, /device:TPU:1, one launch (start us, length us, event | category | flops | bytes accessed | tf_op | source)
XLA Modules:
  0.0 159.5 jit_solution(8232859048226463311)
XLA Ops:
  0.6 0.7 shard_map.92
  1.3 22.6 %all_to_all.25 = bf16[8,8,512]{2,1,0:T(8,128)(2,1)S(1)} all-to-all(bf16[8,8,512]{2,1,0:T(8,128)(2,1)S(1)} %shard_map.92), channel_id=1, replica_groups=mesh['y'=4,'zl'=8,'zh'=4,'x'=4,'core'=2] {'zl'}, dimensions={0} | all-to-all | bytes 131072 | tf_op jit(solution)/shard_map/all_to_all | solution.py:114
  24.0 0.7 broadcast_in_dim.4
  24.7 4.2 %all-to-all-start.1 = ((bf16[4,8,8,512]{3,2,1,0:T(8,128)(2,1)}), bf16[4,8,8,512]{3,2,1,0:T(8,128)(2,1)S(1)}, u32[]{:S(2)}, u32[]{:S(2)}) async-start(bf16[4,8,8,512]{3,2,1,0:T(8,128)(2,1)} %broadcast_in_dim.4), calls=%async_computation.1 | async-start | bytes 524288 | tf_op jit(solution)/shard_map/all_to_all | solution.py:116
  28.9 1.3 shard_map.93
  30.2 4.2 %all-to-all-done.1 = bf16[4,8,8,512]{3,2,1,0:T(8,128)(2,1)S(1)} async-done(((bf16[4,8,8,512]{3,2,1,0:T(8,128)(2,1)}), bf16[4,8,8,512]{3,2,1,0:T(8,128)(2,1)S(1)}, u32[]{:S(2)}, u32[]{:S(2)}) %all-to-all-start.1) | async-done | bytes 262176 | tf_op jit(solution)/shard_map/all_to_all | solution.py:116
  34.9 0.3 convolution_convert_fusion.3
  35.2 7.1 %collective-permute-start = (bf16[128,2688]{1,0:T(8,128)(2,1)S(1)}, bf16[128,2688]{1,0:T(8,128)(2,1)S(1)}, u32[]{:S(2)}, u32[]{:S(2)}) collective-permute-start(bf16[128,2688]{1,0:T(8,128)(2,1)S(1)} %pad_maximum_fusion.1), channel_id=1, source_target_pairs={{0,1},{1,0},{2,3},{3,2},{4,5},{5,4},{6,7},{7,6},{8,9},{9,8},{10,11... | collective-permute-start | bytes 2064392 | tf_op jit(solution)/shard_map/ppermute | solution.py:65
  42.3 0.3 fusion.26
  42.6 0.2 fusion.32
  43.1 1.0 collective-permute-done
  44.2 13.2 %all_to_all.26 = bf16[4,32,2688]{2,1,0:T(8,128)(2,1)S(1)} all-to-all(bf16[4,32,2688]{2,1,0:T(8,128)(2,1)S(1)} %bitcast.47), channel_id=1, replica_groups=mesh['y'=4,'zl'=8,'zh'=4,'x'=4,'core'=2] {'x'}, dimensions={0} | all-to-all | bytes 1376256 | tf_op jit(solution)/shard_map/all_to_all | solution.py:72
  57.5 14.8 %collective-permute-start.1 = (bf16[16,2688]{1,0:T(8,128)(2,1)S(1)}, bf16[16,2688]{1,0:T(8,128)(2,1)S(1)}, u32[]{:S(2)}, u32[]{:S(2)}) collective-permute-start(bf16[16,2688]{1,0:T(8,128)(2,1)S(1)} %get-tuple-element.20), channel_id=1, source_target_pairs={{0,8},{1,25},{8,0},{9,17},{16,24},{17,9},{24,16},{25,1},{2,10},{3,... | collective-permute-start | bytes 258056 | tf_op jit(solution)/shard_map/ppermute | solution.py:81
  72.4 8.2 %collective-permute-start.3 = (bf16[16,2688]{1,0:T(8,128)(2,1)S(1)}, bf16[16,2688]{1,0:T(8,128)(2,1)S(1)}, u32[]{:S(2)}, u32[]{:S(2)}) collective-permute-start(bf16[16,2688]{1,0:T(8,128)(2,1)S(1)} %get-tuple-element.21), channel_id=1, source_target_pairs={{0,24},{1,9},{8,16},{9,1},{16,8},{17,25},{24,0},{25,17},{2,26},{3,... | collective-permute-start | bytes 258056 | tf_op jit(solution)/shard_map/ppermute | solution.py:81
  80.6 19.6 %collective-permute-start.2 = (bf16[16,2688]{1,0:T(8,128)(2,1)S(1)}, bf16[16,2688]{1,0:T(8,128)(2,1)S(1)}, u32[]{:S(2)}, u32[]{:S(2)}) collective-permute-start(bf16[16,2688]{1,0:T(8,128)(2,1)S(1)} %fusion.23), channel_id=1, source_target_pairs={{0,24},{1,9},{8,16},{9,1},{16,8},{17,25},{24,0},{25,17},{2,26},{3,... | collective-permute-start | bytes 258056 | tf_op jit(solution)/shard_map/ppermute | solution.py:81
  100.2 1.9 %collective-permute-start.4 = (bf16[16,2688]{1,0:T(8,128)(2,1)S(1)}, bf16[16,2688]{1,0:T(8,128)(2,1)S(1)}, u32[]{:S(2)}, u32[]{:S(2)}) collective-permute-start(bf16[16,2688]{1,0:T(8,128)(2,1)S(1)} %fusion.24), channel_id=1, source_target_pairs={{0,8},{1,25},{8,0},{9,17},{16,24},{17,9},{24,16},{25,1},{2,10},{3,... | collective-permute-start | bytes 258056 | tf_op jit(solution)/shard_map/ppermute | solution.py:81
  102.1 3.3 %collective-permute-done.2 = bf16[16,2688]{1,0:T(8,128)(2,1)S(1)} collective-permute-done((bf16[16,2688]{1,0:T(8,128)(2,1)S(1)}, bf16[16,2688]{1,0:T(8,128)(2,1)S(1)}, u32[]{:S(2)}, u32[]{:S(2)}) %collective-permute-start.2) | collective-permute-done | bytes 86048 | tf_op jit(solution)/shard_map/ppermute | solution.py:81
  105.4 9.7 %collective-permute-done.4 = bf16[16,2688]{1,0:T(8,128)(2,1)S(1)} collective-permute-done((bf16[16,2688]{1,0:T(8,128)(2,1)S(1)}, bf16[16,2688]{1,0:T(8,128)(2,1)S(1)}, u32[]{:S(2)}, u32[]{:S(2)}) %collective-permute-start.4) | collective-permute-done | bytes 86048 | tf_op jit(solution)/shard_map/ppermute | solution.py:81
  115.3 10.2 %all_to_all.27 = bf16[4,32,2688]{2,1,0:T(8,128)(2,1)S(1)} all-to-all(bf16[4,32,2688]{2,1,0:T(8,128)(2,1)S(1)} %broadcast_in_dim.5), channel_id=1, replica_groups=mesh['y'=4,'zl'=8,'zh'=4,'x'=4,'core'=2] {'x'}, dimensions={0} | all-to-all | bytes 1376256 | tf_op jit(solution)/shard_map/all_to_all | solution.py:102
  125.5 7.0 %collective-permute-start.5 = (bf16[128,2688]{1,0:T(8,128)(2,1)S(1)}, bf16[128,2688]{1,0:T(8,128)(2,1)S(1)}, u32[]{:S(2)}, u32[]{:S(2)}) collective-permute-start(bf16[128,2688]{1,0:T(8,128)(2,1)S(1)} %bitcast.31), channel_id=1, source_target_pairs={{0,1},{1,0},{2,3},{3,2},{4,5},{5,4},{6,7},{7,6},{8,9},{9,8},{10,11... | collective-permute-start | bytes 2064392 | tf_op jit(solution)/shard_map/ppermute | solution.py:65
  132.8 0.3 fusion.15
  133.1 0.3 fusion.6
  133.4 0.9 collective-permute-done.5
  134.5 0.3 fusion.10
  134.9 0.3 fusion.5
  135.2 0.7 pad_maximum_fusion.2
  135.9 3.9 %all-to-all-start.4 = ((bf16[32,8,512]{2,1,0:T(8,128)(2,1)}), bf16[32,8,512]{2,1,0:T(8,128)(2,1)S(1)}, u32[]{:S(2)}, u32[]{:S(2)}) async-start(bf16[32,8,512]{2,1,0:T(8,128)(2,1)} %bitcast.7), calls=%async_computation.4 | async-start | bytes 524288 | tf_op jit(solution)/shard_map/all_to_all | solution.py:174
  140.1 1.1 convolution_convert_fusion
  141.3 1.1 convolution_convert_fusion.1
  142.4 1.1 convolution_convert_fusion.2
  143.5 15.4 %all-to-all-done.4 = bf16[32,8,512]{2,1,0:T(8,128)(2,1)S(1)} async-done(((bf16[32,8,512]{2,1,0:T(8,128)(2,1)}), bf16[32,8,512]{2,1,0:T(8,128)(2,1)S(1)}, u32[]{:S(2)}, u32[]{:S(2)}) %all-to-all-start.4) | async-done | bytes 262176 | tf_op jit(solution)/shard_map/all_to_all | solution.py:174
  158.9 0.6 fusion.39
  (21 shorter events, 2.1 us)
Async XLA Ops:
  24.7 9.7 %all-to-all-start.1 = ((bf16[4,8,8,512]{3,2,1,0:T(8,128)(2,1)}), bf16[4,8,8,512]{3,2,1,0:T(8,128)(2,1)S(1)}, u32[]{:S(2)}, u32[]{:S(2)}) async-start(bf16[4,8,8,512]{3,2,1,0:T(8,128)(2,1)} %broadcast_in_dim.4), calls=%async_computation.1 | async-start | bytes 524288 | tf_op jit(solution)/shard_map/all_to_all | solution.py:116
  35.2 8.8 %collective-permute-start = (bf16[128,2688]{1,0:T(8,128)(2,1)S(1)}, bf16[128,2688]{1,0:T(8,128)(2,1)S(1)}, u32[]{:S(2)}, u32[]{:S(2)}) collective-permute-start(bf16[128,2688]{1,0:T(8,128)(2,1)S(1)} %pad_maximum_fusion.1), channel_id=1, source_target_pairs={{0,1},{1,0},{2,3},{3,2},{4,5},{5,4},{6,7},{7,6},{8,9},{9,8},{10,11... | collective-permute-start | bytes 2064392 | tf_op jit(solution)/shard_map/ppermute | solution.py:65
  57.5 23.0 %collective-permute-start.1 = (bf16[16,2688]{1,0:T(8,128)(2,1)S(1)}, bf16[16,2688]{1,0:T(8,128)(2,1)S(1)}, u32[]{:S(2)}, u32[]{:S(2)}) collective-permute-start(bf16[16,2688]{1,0:T(8,128)(2,1)S(1)} %get-tuple-element.20), channel_id=1, source_target_pairs={{0,8},{1,25},{8,0},{9,17},{16,24},{17,9},{24,16},{25,1},{2,10},{3,... | collective-permute-start | bytes 258056 | tf_op jit(solution)/shard_map/ppermute | solution.py:81
  72.4 27.8 %collective-permute-start.3 = (bf16[16,2688]{1,0:T(8,128)(2,1)S(1)}, bf16[16,2688]{1,0:T(8,128)(2,1)S(1)}, u32[]{:S(2)}, u32[]{:S(2)}) collective-permute-start(bf16[16,2688]{1,0:T(8,128)(2,1)S(1)} %get-tuple-element.21), channel_id=1, source_target_pairs={{0,24},{1,9},{8,16},{9,1},{16,8},{17,25},{24,0},{25,17},{2,26},{3,... | collective-permute-start | bytes 258056 | tf_op jit(solution)/shard_map/ppermute | solution.py:81
  80.6 24.9 %collective-permute-start.2 = (bf16[16,2688]{1,0:T(8,128)(2,1)S(1)}, bf16[16,2688]{1,0:T(8,128)(2,1)S(1)}, u32[]{:S(2)}, u32[]{:S(2)}) collective-permute-start(bf16[16,2688]{1,0:T(8,128)(2,1)S(1)} %fusion.23), channel_id=1, source_target_pairs={{0,24},{1,9},{8,16},{9,1},{16,8},{17,25},{24,0},{25,17},{2,26},{3,... | collective-permute-start | bytes 258056 | tf_op jit(solution)/shard_map/ppermute | solution.py:81
  100.2 14.9 %collective-permute-start.4 = (bf16[16,2688]{1,0:T(8,128)(2,1)S(1)}, bf16[16,2688]{1,0:T(8,128)(2,1)S(1)}, u32[]{:S(2)}, u32[]{:S(2)}) collective-permute-start(bf16[16,2688]{1,0:T(8,128)(2,1)S(1)} %fusion.24), channel_id=1, source_target_pairs={{0,8},{1,25},{8,0},{9,17},{16,24},{17,9},{24,16},{25,1},{2,10},{3,... | collective-permute-start | bytes 258056 | tf_op jit(solution)/shard_map/ppermute | solution.py:81
  125.5 8.8 %collective-permute-start.5 = (bf16[128,2688]{1,0:T(8,128)(2,1)S(1)}, bf16[128,2688]{1,0:T(8,128)(2,1)S(1)}, u32[]{:S(2)}, u32[]{:S(2)}) collective-permute-start(bf16[128,2688]{1,0:T(8,128)(2,1)S(1)} %bitcast.31), channel_id=1, source_target_pairs={{0,1},{1,0},{2,3},{3,2},{4,5},{5,4},{6,7},{7,6},{8,9},{9,8},{10,11... | collective-permute-start | bytes 2064392 | tf_op jit(solution)/shard_map/ppermute | solution.py:65
  135.9 22.9 %all-to-all-start.4 = ((bf16[32,8,512]{2,1,0:T(8,128)(2,1)}), bf16[32,8,512]{2,1,0:T(8,128)(2,1)S(1)}, u32[]{:S(2)}, u32[]{:S(2)}) async-start(bf16[32,8,512]{2,1,0:T(8,128)(2,1)} %bitcast.7), calls=%async_computation.4 | async-start | bytes 524288 | tf_op jit(solution)/shard_map/all_to_all | solution.py:174

commit v12 on v11

--- a/solution.py
+++ b/solution.py
@@ -109,11 +109,8 @@
     rows = own * sections
     half = rows // 2
     gate_weight, up_weight, down_weight = held(gate_weight, up_weight, down_weight)
-    runs, lines = lax.axis_size("zl"), lax.axis_size("y")
-    both = side_by_side(tokens, out_grad, runs)
-    both = lax.all_to_all(both, "zl", 0, 0)
-    both = jnp.broadcast_to(both[None], (lines,) + both.shape)
-    both = lax.all_to_all(both, "y", 0, 0).reshape(rows, 2 * width)
+    both = side_by_side(tokens, out_grad, sections)
+    both = lax.all_to_all(both, SECTION, 0, 0).reshape(rows, 2 * width)
 
     core = lax.axis_index("core")
 

time: 160 us -> 159 us (level)
  blocking collectives: 46 us -> 24.7 us
  waiting for transfers between devices: 34.5 us -> 46.5 us
  starting transfers between devices: 66.6 us -> 75.2 us
    all_to_all x1 -> x0, blocking collectives: 22.6 us -> none  [shards(): both = lax.all_to_all(both, 'zl', 0, 0)]
    all_to_all x1, waiting for transfers between devices: 4.2 us -> 17.3 us  [shards(): both = lax.all_to_all(both, SECTION, 0, 0).reshape(rows, 2 * width)]
    all_to_all x1, starting transfers between devices: 4.18 us -> 16.1 us  [shards(): both = lax.all_to_all(both, SECTION, 0, 0).reshape(rows, 2 * width)]
    ppermute x2, starting transfers between devices: 14.1 us -> 10.5 us  [swap_core(): return lax.ppermute(block, 'core', [(0, 1), (1, 0)])]
where the time goes in v12:
time: 159 us
  starting transfers between devices  75.2 us (47%)
  waiting for transfers between devices  46.5 us (29%)
  blocking collectives  24.7 us (16%)
  matrix products  6.45 us (4%)
  Pallas kernels  2.75 us (2%)
  other arithmetic  1.62 us (1%)
    ppermute x4, starting transfers between devices, swap_far(): return lax.ppermute(part.astype(BF16), ('zh', 'core'), pairs)  44 us
    all_to_all x1, waiting for transfers between devices, shards(): both = lax.all_to_all(both, SECTION, 0, 0).reshape(rows, 2 * width)  17.3 us
    all_to_all x1, starting transfers between devices, shards(): both = lax.all_to_all(both, SECTION, 0, 0).reshape(rows, 2 * width)  16.1 us
    all_to_all x1, waiting for transfers between devices, shards(): ends = lax.all_to_all(ends, SECTION, 0, 0).astype(F32).sum(0).astype(BF16)  15.1 us
    all_to_all x1, blocking collectives, sum_over_x(): return lax.all_to_all(pieces, 'x', 0, 0).astype(F32).sum(0)  14.5 us
    ppermute x4, waiting for transfers between devices, swap_far(): return lax.ppermute(part.astype(BF16), ('zh', 'core'), pairs)  12.2 us
    ppermute x2, starting transfers between devices, swap_core(): return lax.ppermute(block, 'core', [(0, 1), (1, 0)])  10.5 us
    all_to_all x1, blocking collectives, copies_over_x(): return lax.all_to_all(copies, 'x', 0, 0)  10.2 us
  transfers between devices with their start and end apart: 8, of which 6 were waited for; matrix products, arithmetic and copies ran while one was open for 3% of the time, Pallas kernels for 1%

profile of v12, /device:TPU:1, one launch (start us, length us, event | category | flops | bytes accessed | tf_op | source)
XLA Modules:
  0.0 158.7 jit_solution(10108332751835115929)
XLA Ops:
  0.6 1.4 shard_map.92
  2.1 16.1 %all-to-all-start = ((bf16[32,8,512]{2,1,0:T(8,128)(2,1)}), bf16[32,8,512]{2,1,0:T(8,128)(2,1)S(1)}, u32[]{:S(2)}, u32[]{:S(2)}) async-start(bf16[32,8,512]{2,1,0:T(8,128)(2,1)} %shard_map.92), calls=%async_computation | async-start | bytes 524288 | tf_op jit(solution)/shard_map/all_to_all | solution.py:113
  18.2 1.3 shard_map.93
  19.5 17.3 %all-to-all-done = bf16[32,8,512]{2,1,0:T(8,128)(2,1)S(1)} async-done(((bf16[32,8,512]{2,1,0:T(8,128)(2,1)}), bf16[32,8,512]{2,1,0:T(8,128)(2,1)S(1)}, u32[]{:S(2)}, u32[]{:S(2)}) %all-to-all-start) | async-done | bytes 262176 | tf_op jit(solution)/shard_map/all_to_all | solution.py:113
  37.3 0.3 convolution_convert_fusion.3
  37.6 3.8 %collective-permute-start = (bf16[128,2688]{1,0:T(8,128)(2,1)S(1)}, bf16[128,2688]{1,0:T(8,128)(2,1)S(1)}, u32[]{:S(2)}, u32[]{:S(2)}) collective-permute-start(bf16[128,2688]{1,0:T(8,128)(2,1)S(1)} %pad_maximum_fusion.1), channel_id=1, source_target_pairs={{0,1},{1,0},{2,3},{3,2},{4,5},{5,4},{6,7},{7,6},{8,9},{9,8},{10,11... | collective-permute-start | bytes 2064392 | tf_op jit(solution)/shard_map/ppermute | solution.py:65
  41.4 0.3 fusion.26
  41.7 0.2 fusion.32
  42.2 1.0 collective-permute-done
  43.3 14.5 %all_to_all.20 = bf16[4,32,2688]{2,1,0:T(8,128)(2,1)S(1)} all-to-all(bf16[4,32,2688]{2,1,0:T(8,128)(2,1)S(1)} %bitcast.47), channel_id=1, replica_groups=mesh['y'=4,'zl'=8,'zh'=4,'x'=4,'core'=2] {'x'}, dimensions={0} | all-to-all | bytes 1376256 | tf_op jit(solution)/shard_map/all_to_all | solution.py:72
  57.9 15.2 %collective-permute-start.1 = (bf16[16,2688]{1,0:T(8,128)(2,1)S(1)}, bf16[16,2688]{1,0:T(8,128)(2,1)S(1)}, u32[]{:S(2)}, u32[]{:S(2)}) collective-permute-start(bf16[16,2688]{1,0:T(8,128)(2,1)S(1)} %get-tuple-element.20), channel_id=1, source_target_pairs={{0,8},{1,25},{8,0},{9,17},{16,24},{17,9},{24,16},{25,1},{2,10},{3,... | collective-permute-start | bytes 258056 | tf_op jit(solution)/shard_map/ppermute | solution.py:81
  73.1 8.2 %collective-permute-start.3 = (bf16[16,2688]{1,0:T(8,128)(2,1)S(1)}, bf16[16,2688]{1,0:T(8,128)(2,1)S(1)}, u32[]{:S(2)}, u32[]{:S(2)}) collective-permute-start(bf16[16,2688]{1,0:T(8,128)(2,1)S(1)} %get-tuple-element.21), channel_id=1, source_target_pairs={{0,24},{1,9},{8,16},{9,1},{16,8},{17,25},{24,0},{25,17},{2,26},{3,... | collective-permute-start | bytes 258056 | tf_op jit(solution)/shard_map/ppermute | solution.py:81
  81.3 18.7 %collective-permute-start.2 = (bf16[16,2688]{1,0:T(8,128)(2,1)S(1)}, bf16[16,2688]{1,0:T(8,128)(2,1)S(1)}, u32[]{:S(2)}, u32[]{:S(2)}) collective-permute-start(bf16[16,2688]{1,0:T(8,128)(2,1)S(1)} %fusion.23), channel_id=1, source_target_pairs={{0,24},{1,9},{8,16},{9,1},{16,8},{17,25},{24,0},{25,17},{2,26},{3,... | collective-permute-start | bytes 258056 | tf_op jit(solution)/shard_map/ppermute | solution.py:81
  100.0 1.9 %collective-permute-start.4 = (bf16[16,2688]{1,0:T(8,128)(2,1)S(1)}, bf16[16,2688]{1,0:T(8,128)(2,1)S(1)}, u32[]{:S(2)}, u32[]{:S(2)}) collective-permute-start(bf16[16,2688]{1,0:T(8,128)(2,1)S(1)} %fusion.24), channel_id=1, source_target_pairs={{0,8},{1,25},{8,0},{9,17},{16,24},{17,9},{24,16},{25,1},{2,10},{3,... | collective-permute-start | bytes 258056 | tf_op jit(solution)/shard_map/ppermute | solution.py:81
  102.0 4.3 %collective-permute-done.2 = bf16[16,2688]{1,0:T(8,128)(2,1)S(1)} collective-permute-done((bf16[16,2688]{1,0:T(8,128)(2,1)S(1)}, bf16[16,2688]{1,0:T(8,128)(2,1)S(1)}, u32[]{:S(2)}, u32[]{:S(2)}) %collective-permute-start.2) | collective-permute-done | bytes 86048 | tf_op jit(solution)/shard_map/ppermute | solution.py:81
  106.3 7.8 %collective-permute-done.4 = bf16[16,2688]{1,0:T(8,128)(2,1)S(1)} collective-permute-done((bf16[16,2688]{1,0:T(8,128)(2,1)S(1)}, bf16[16,2688]{1,0:T(8,128)(2,1)S(1)}, u32[]{:S(2)}, u32[]{:S(2)}) %collective-permute-start.4) | collective-permute-done | bytes 86048 | tf_op jit(solution)/shard_map/ppermute | solution.py:81
  114.3 10.2 %all_to_all.21 = bf16[4,32,2688]{2,1,0:T(8,128)(2,1)S(1)} all-to-all(bf16[4,32,2688]{2,1,0:T(8,128)(2,1)S(1)} %broadcast_in_dim.2), channel_id=1, replica_groups=mesh['y'=4,'zl'=8,'zh'=4,'x'=4,'core'=2] {'x'}, dimensions={0} | all-to-all | bytes 1376256 | tf_op jit(solution)/shard_map/all_to_all | solution.py:102
  124.5 6.8 %collective-permute-start.5 = (bf16[128,2688]{1,0:T(8,128)(2,1)S(1)}, bf16[128,2688]{1,0:T(8,128)(2,1)S(1)}, u32[]{:S(2)}, u32[]{:S(2)}) collective-permute-start(bf16[128,2688]{1,0:T(8,128)(2,1)S(1)} %bitcast.31), channel_id=1, source_target_pairs={{0,1},{1,0},{2,3},{3,2},{4,5},{5,4},{6,7},{7,6},{8,9},{9,8},{10,11... | collective-permute-start | bytes 2064392 | tf_op jit(solution)/shard_map/ppermute | solution.py:65
  131.3 0.2 fusion.3
  131.5 0.3 fusion.15
  131.8 0.3 fusion.6
  132.1 0.9 collective-permute-done.5
  133.1 0.2 fusion.4
  133.3 0.3 fusion.10
  133.6 0.3 fusion.5
  134.0 0.7 pad_maximum_fusion.2
  134.7 4.6 %all-to-all-start.3 = ((bf16[32,8,512]{2,1,0:T(8,128)(2,1)}), bf16[32,8,512]{2,1,0:T(8,128)(2,1)S(1)}, u32[]{:S(2)}, u32[]{:S(2)}) async-start(bf16[32,8,512]{2,1,0:T(8,128)(2,1)} %bitcast.7), calls=%async_computation.3 | async-start | bytes 524288 | tf_op jit(solution)/shard_map/all_to_all | solution.py:171
  139.6 1.1 convolution_convert_fusion
  140.7 1.1 convolution_convert_fusion.1
  141.8 1.1 convolution_convert_fusion.2
  142.9 15.1 %all-to-all-done.3 = bf16[32,8,512]{2,1,0:T(8,128)(2,1)S(1)} async-done(((bf16[32,8,512]{2,1,0:T(8,128)(2,1)}), bf16[32,8,512]{2,1,0:T(8,128)(2,1)S(1)}, u32[]{:S(2)}, u32[]{:S(2)}) %all-to-all-start.3) | async-done | bytes 262176 | tf_op jit(solution)/shard_map/all_to_all | solution.py:171
  158.1 0.6 fusion.39
  (19 shorter events, 1.6 us)
Async XLA Ops:
  2.1 34.7 %all-to-all-start = ((bf16[32,8,512]{2,1,0:T(8,128)(2,1)}), bf16[32,8,512]{2,1,0:T(8,128)(2,1)S(1)}, u32[]{:S(2)}, u32[]{:S(2)}) async-start(bf16[32,8,512]{2,1,0:T(8,128)(2,1)} %shard_map.92), calls=%async_computation | async-start | bytes 524288 | tf_op jit(solution)/shard_map/all_to_all | solution.py:113
  37.6 5.5 %collective-permute-start = (bf16[128,2688]{1,0:T(8,128)(2,1)S(1)}, bf16[128,2688]{1,0:T(8,128)(2,1)S(1)}, u32[]{:S(2)}, u32[]{:S(2)}) collective-permute-start(bf16[128,2688]{1,0:T(8,128)(2,1)S(1)} %pad_maximum_fusion.1), channel_id=1, source_target_pairs={{0,1},{1,0},{2,3},{3,2},{4,5},{5,4},{6,7},{7,6},{8,9},{9,8},{10,11... | collective-permute-start | bytes 2064392 | tf_op jit(solution)/shard_map/ppermute | solution.py:65
  57.9 23.4 %collective-permute-start.1 = (bf16[16,2688]{1,0:T(8,128)(2,1)S(1)}, bf16[16,2688]{1,0:T(8,128)(2,1)S(1)}, u32[]{:S(2)}, u32[]{:S(2)}) collective-permute-start(bf16[16,2688]{1,0:T(8,128)(2,1)S(1)} %get-tuple-element.20), channel_id=1, source_target_pairs={{0,8},{1,25},{8,0},{9,17},{16,24},{17,9},{24,16},{25,1},{2,10},{3,... | collective-permute-start | bytes 258056 | tf_op jit(solution)/shard_map/ppermute | solution.py:81
  73.1 26.9 %collective-permute-start.3 = (bf16[16,2688]{1,0:T(8,128)(2,1)S(1)}, bf16[16,2688]{1,0:T(8,128)(2,1)S(1)}, u32[]{:S(2)}, u32[]{:S(2)}) collective-permute-start(bf16[16,2688]{1,0:T(8,128)(2,1)S(1)} %get-tuple-element.21), channel_id=1, source_target_pairs={{0,24},{1,9},{8,16},{9,1},{16,8},{17,25},{24,0},{25,17},{2,26},{3,... | collective-permute-start | bytes 258056 | tf_op jit(solution)/shard_map/ppermute | solution.py:81
  81.3 25.0 %collective-permute-start.2 = (bf16[16,2688]{1,0:T(8,128)(2,1)S(1)}, bf16[16,2688]{1,0:T(8,128)(2,1)S(1)}, u32[]{:S(2)}, u32[]{:S(2)}) collective-permute-start(bf16[16,2688]{1,0:T(8,128)(2,1)S(1)} %fusion.23), channel_id=1, source_target_pairs={{0,24},{1,9},{8,16},{9,1},{16,8},{17,25},{24,0},{25,17},{2,26},{3,... | collective-permute-start | bytes 258056 | tf_op jit(solution)/shard_map/ppermute | solution.py:81
  100.0 14.1 %collective-permute-start.4 = (bf16[16,2688]{1,0:T(8,128)(2,1)S(1)}, bf16[16,2688]{1,0:T(8,128)(2,1)S(1)}, u32[]{:S(2)}, u32[]{:S(2)}) collective-permute-start(bf16[16,2688]{1,0:T(8,128)(2,1)S(1)} %fusion.24), channel_id=1, source_target_pairs={{0,8},{1,25},{8,0},{9,17},{16,24},{17,9},{24,16},{25,1},{2,10},{3,... | collective-permute-start | bytes 258056 | tf_op jit(solution)/shard_map/ppermute | solution.py:81
  124.5 8.5 %collective-permute-start.5 = (bf16[128,2688]{1,0:T(8,128)(2,1)S(1)}, bf16[128,2688]{1,0:T(8,128)(2,1)S(1)}, u32[]{:S(2)}, u32[]{:S(2)}) collective-permute-start(bf16[128,2688]{1,0:T(8,128)(2,1)S(1)} %bitcast.31), channel_id=1, source_target_pairs={{0,1},{1,0},{2,3},{3,2},{4,5},{5,4},{6,7},{7,6},{8,9},{9,8},{10,11... | collective-permute-start | bytes 2064392 | tf_op jit(solution)/shard_map/ppermute | solution.py:65
  134.7 23.4 %all-to-all-start.3 = ((bf16[32,8,512]{2,1,0:T(8,128)(2,1)}), bf16[32,8,512]{2,1,0:T(8,128)(2,1)S(1)}, u32[]{:S(2)}, u32[]{:S(2)}) async-start(bf16[32,8,512]{2,1,0:T(8,128)(2,1)} %bitcast.7), calls=%async_computation.3 | async-start | bytes 524288 | tf_op jit(solution)/shard_map/all_to_all | solution.py:171

commit v13 on v12

--- a/solution.py
+++ b/solution.py
@@ -97,11 +97,6 @@
     return jnp.concatenate([hidden, gate_delta, up_delta], axis=1).astype(BF16)
 
 
-def copies_over_x(block):
-    copies = jnp.broadcast_to(block[None], (lax.axis_size("x"),) + block.shape)
-    return lax.all_to_all(copies, "x", 0, 0)
-
-
 def shards(tokens, gate_weight, up_weight, down_weight, out_grad):
     own, width = tokens.shape
     units = gate_weight.shape[1]
@@ -138,7 +133,8 @@
     top_in = swap_far(sent, (3, 1))
     low = low + low_in
     low_in = swap_far(low, (1, 3))
-    mine = copies_over_x(deltas_of(jnp.concatenate([top + top_in, low + low_in])))
+    mine = deltas_of(jnp.concatenate([top + top_in, low + low_in]))
+    mine = lax.all_gather(mine, "x", axis=0, tiled=True)
     mine = mine.reshape(half, 3 * units)
     theirs = swap_core(mine)
 

time: 159 us -> 161 us (1.013)
  starting transfers between devices: 75.2 us -> 76.9 us
    all_gather x0 -> x1, blocking collectives: none -> 10.3 us  [shards(): mine = lax.all_gather(mine, 'x', axis=0, tiled=True)]
    all_to_all x1 -> x0, blocking collectives: 10.2 us -> none  [copies_over_x(): return lax.all_to_all(copies, 'x', 0, 0)]
    ppermute x2, starting transfers between devices: 10.5 us -> 12.3 us  [swap_core(): return lax.ppermute(block, 'core', [(0, 1), (1, 0)])]
where the time goes in v13:
time: 161 us; the launch traced here: 160 us
  starting transfers between devices  76.9 us (48%)
  waiting for transfers between devices  46.5 us (29%)
  blocking collectives  24.8 us (15%)
  matrix products  6.45 us (4%)
  Pallas kernels  2.75 us (2%)
    ppermute x4, starting transfers between devices, swap_far(): return lax.ppermute(part.astype(BF16), ('zh', 'core'), pairs)  44 us
    all_to_all x1, waiting for transfers between devices, shards(): both = lax.all_to_all(both, SECTION, 0, 0).reshape(rows, 2 * width)  17.3 us
    all_to_all x1, starting transfers between devices, shards(): both = lax.all_to_all(both, SECTION, 0, 0).reshape(rows, 2 * width)  16.1 us
    all_to_all x1, waiting for transfers between devices, shards(): ends = lax.all_to_all(ends, SECTION, 0, 0).astype(F32).sum(0).astype(BF16)  15.2 us
    all_to_all x1, blocking collectives, sum_over_x(): return lax.all_to_all(pieces, 'x', 0, 0).astype(F32).sum(0)  14.5 us
    ppermute x2, starting transfers between devices, swap_core(): return lax.ppermute(block, 'core', [(0, 1), (1, 0)])  12.3 us
    ppermute x4, waiting for transfers between devices, swap_far(): return lax.ppermute(part.astype(BF16), ('zh', 'core'), pairs)  12.2 us
    all_gather x1, blocking collectives, shards(): mine = lax.all_gather(mine, 'x', axis=0, tiled=True)  10.3 us
  transfers between devices with their start and end apart: 8, of which 6 were waited for; matrix products, arithmetic and copies ran while one was open for 3% of the time, Pallas kernels for 1%

profile of v13, /device:TPU:1, one launch (start us, length us, event | category | flops | bytes accessed | tf_op | source)
XLA Modules:
  0.0 160.5 jit_solution(2328753197815591694)
XLA Ops:
  0.6 1.4 shard_map.92
  2.1 16.1 %all-to-all-start = ((bf16[32,8,512]{2,1,0:T(8,128)(2,1)}), bf16[32,8,512]{2,1,0:T(8,128)(2,1)S(1)}, u32[]{:S(2)}, u32[]{:S(2)}) async-start(bf16[32,8,512]{2,1,0:T(8,128)(2,1)} %shard_map.92), calls=%async_computation | async-start | bytes 524288 | tf_op jit(solution)/shard_map/all_to_all | solution.py:108
  18.2 1.3 shard_map.93
  19.5 17.3 %all-to-all-done = bf16[32,8,512]{2,1,0:T(8,128)(2,1)S(1)} async-done(((bf16[32,8,512]{2,1,0:T(8,128)(2,1)}), bf16[32,8,512]{2,1,0:T(8,128)(2,1)S(1)}, u32[]{:S(2)}, u32[]{:S(2)}) %all-to-all-start) | async-done | bytes 262176 | tf_op jit(solution)/shard_map/all_to_all | solution.py:108
  37.3 0.3 convolution_convert_fusion.3
  37.6 3.8 %collective-permute-start = (bf16[128,2688]{1,0:T(8,128)(2,1)S(1)}, bf16[128,2688]{1,0:T(8,128)(2,1)S(1)}, u32[]{:S(2)}, u32[]{:S(2)}) collective-permute-start(bf16[128,2688]{1,0:T(8,128)(2,1)S(1)} %pad_maximum_fusion.1), channel_id=1, source_target_pairs={{0,1},{1,0},{2,3},{3,2},{4,5},{5,4},{6,7},{7,6},{8,9},{9,8},{10,11... | collective-permute-start | bytes 2064392 | tf_op jit(solution)/shard_map/ppermute | solution.py:65
  41.4 0.3 fusion.26
  41.7 0.2 fusion.32
  42.2 1.0 collective-permute-done
  43.3 14.5 %all_to_all.15 = bf16[4,32,2688]{2,1,0:T(8,128)(2,1)S(1)} all-to-all(bf16[4,32,2688]{2,1,0:T(8,128)(2,1)S(1)} %bitcast.40), channel_id=1, replica_groups=mesh['y'=4,'zl'=8,'zh'=4,'x'=4,'core'=2] {'x'}, dimensions={0} | all-to-all | bytes 1376256 | tf_op jit(solution)/shard_map/all_to_all | solution.py:72
  57.9 15.2 %collective-permute-start.1 = (bf16[16,2688]{1,0:T(8,128)(2,1)S(1)}, bf16[16,2688]{1,0:T(8,128)(2,1)S(1)}, u32[]{:S(2)}, u32[]{:S(2)}) collective-permute-start(bf16[16,2688]{1,0:T(8,128)(2,1)S(1)} %get-tuple-element.20), channel_id=1, source_target_pairs={{0,8},{1,25},{8,0},{9,17},{16,24},{17,9},{24,16},{25,1},{2,10},{3,... | collective-permute-start | bytes 258056 | tf_op jit(solution)/shard_map/ppermute | solution.py:81
  73.1 8.2 %collective-permute-start.3 = (bf16[16,2688]{1,0:T(8,128)(2,1)S(1)}, bf16[16,2688]{1,0:T(8,128)(2,1)S(1)}, u32[]{:S(2)}, u32[]{:S(2)}) collective-permute-start(bf16[16,2688]{1,0:T(8,128)(2,1)S(1)} %get-tuple-element.21), channel_id=1, source_target_pairs={{0,24},{1,9},{8,16},{9,1},{16,8},{17,25},{24,0},{25,17},{2,26},{3,... | collective-permute-start | bytes 258056 | tf_op jit(solution)/shard_map/ppermute | solution.py:81
  81.3 18.7 %collective-permute-start.2 = (bf16[16,2688]{1,0:T(8,128)(2,1)S(1)}, bf16[16,2688]{1,0:T(8,128)(2,1)S(1)}, u32[]{:S(2)}, u32[]{:S(2)}) collective-permute-start(bf16[16,2688]{1,0:T(8,128)(2,1)S(1)} %fusion.23), channel_id=1, source_target_pairs={{0,24},{1,9},{8,16},{9,1},{16,8},{17,25},{24,0},{25,17},{2,26},{3,... | collective-permute-start | bytes 258056 | tf_op jit(solution)/shard_map/ppermute | solution.py:81
  100.0 1.9 %collective-permute-start.4 = (bf16[16,2688]{1,0:T(8,128)(2,1)S(1)}, bf16[16,2688]{1,0:T(8,128)(2,1)S(1)}, u32[]{:S(2)}, u32[]{:S(2)}) collective-permute-start(bf16[16,2688]{1,0:T(8,128)(2,1)S(1)} %fusion.24), channel_id=1, source_target_pairs={{0,8},{1,25},{8,0},{9,17},{16,24},{17,9},{24,16},{25,1},{2,10},{3,... | collective-permute-start | bytes 258056 | tf_op jit(solution)/shard_map/ppermute | solution.py:81
  102.0 4.3 %collective-permute-done.2 = bf16[16,2688]{1,0:T(8,128)(2,1)S(1)} collective-permute-done((bf16[16,2688]{1,0:T(8,128)(2,1)S(1)}, bf16[16,2688]{1,0:T(8,128)(2,1)S(1)}, u32[]{:S(2)}, u32[]{:S(2)}) %collective-permute-start.2) | collective-permute-done | bytes 86048 | tf_op jit(solution)/shard_map/ppermute | solution.py:81
  106.3 7.8 %collective-permute-done.4 = bf16[16,2688]{1,0:T(8,128)(2,1)S(1)} collective-permute-done((bf16[16,2688]{1,0:T(8,128)(2,1)S(1)}, bf16[16,2688]{1,0:T(8,128)(2,1)S(1)}, u32[]{:S(2)}, u32[]{:S(2)}) %collective-permute-start.4) | collective-permute-done | bytes 86048 | tf_op jit(solution)/shard_map/ppermute | solution.py:81
  114.3 10.3 %all_gather.3 = bf16[128,2688]{1,0:T(8,128)(2,1)S(1)} all-gather(bf16[32,2688]{1,0:T(8,128)(2,1)S(1)} %pad_maximum_fusion.3), channel_id=1, replica_groups=mesh['y'=4,'zl'=8,'zh'=4,'x'=4,'core'=2] {'x'}, dimensions={0}, use_global_device_ids=true | all-gather | bytes 860160 | tf_op jit(solution)/shard_map/all_gather | solution.py:137
  124.6 8.5 %collective-permute-start.5 = (bf16[128,2688]{1,0:T(8,128)(2,1)S(1)}, bf16[128,2688]{1,0:T(8,128)(2,1)S(1)}, u32[]{:S(2)}, u32[]{:S(2)}) collective-permute-start(bf16[128,2688]{1,0:T(8,128)(2,1)S(1)} %all_gather.3), channel_id=1, source_target_pairs={{0,1},{1,0},{2,3},{3,2},{4,5},{5,4},{6,7},{7,6},{8,9},{9,8},{10,11... | collective-permute-start | bytes 2064392 | tf_op jit(solution)/shard_map/ppermute | solution.py:65
  133.1 0.2 fusion.3
  133.3 0.3 fusion.15
  133.7 0.3 fusion.6
  133.9 0.9 collective-permute-done.5
  134.9 0.2 fusion.4
  135.1 0.3 fusion.10
  135.4 0.3 fusion.5
  135.8 0.7 pad_maximum_fusion.2
  136.5 4.6 %all-to-all-start.2 = ((bf16[32,8,512]{2,1,0:T(8,128)(2,1)}), bf16[32,8,512]{2,1,0:T(8,128)(2,1)S(1)}, u32[]{:S(2)}, u32[]{:S(2)}) async-start(bf16[32,8,512]{2,1,0:T(8,128)(2,1)} %bitcast.6), calls=%async_computation.2 | async-start | bytes 524288 | tf_op jit(solution)/shard_map/all_to_all | solution.py:167
  141.3 1.1 convolution_convert_fusion
  142.4 1.1 convolution_convert_fusion.1
  143.5 1.1 convolution_convert_fusion.2
  144.6 15.2 %all-to-all-done.2 = bf16[32,8,512]{2,1,0:T(8,128)(2,1)S(1)} async-done(((bf16[32,8,512]{2,1,0:T(8,128)(2,1)}), bf16[32,8,512]{2,1,0:T(8,128)(2,1)S(1)}, u32[]{:S(2)}, u32[]{:S(2)}) %all-to-all-start.2) | async-done | bytes 262176 | tf_op jit(solution)/shard_map/all_to_all | solution.py:167
  159.9 0.6 fusion.39
  (18 shorter events, 1.6 us)
Async XLA Ops:
  2.1 34.7 %all-to-all-start = ((bf16[32,8,512]{2,1,0:T(8,128)(2,1)}), bf16[32,8,512]{2,1,0:T(8,128)(2,1)S(1)}, u32[]{:S(2)}, u32[]{:S(2)}) async-start(bf16[32,8,512]{2,1,0:T(8,128)(2,1)} %shard_map.92), calls=%async_computation | async-start | bytes 524288 | tf_op jit(solution)/shard_map/all_to_all | solution.py:108
  37.6 5.5 %collective-permute-start = (bf16[128,2688]{1,0:T(8,128)(2,1)S(1)}, bf16[128,2688]{1,0:T(8,128)(2,1)S(1)}, u32[]{:S(2)}, u32[]{:S(2)}) collective-permute-start(bf16[128,2688]{1,0:T(8,128)(2,1)S(1)} %pad_maximum_fusion.1), channel_id=1, source_target_pairs={{0,1},{1,0},{2,3},{3,2},{4,5},{5,4},{6,7},{7,6},{8,9},{9,8},{10,11... | collective-permute-start | bytes 2064392 | tf_op jit(solution)/shard_map/ppermute | solution.py:65
  57.9 23.4 %collective-permute-start.1 = (bf16[16,2688]{1,0:T(8,128)(2,1)S(1)}, bf16[16,2688]{1,0:T(8,128)(2,1)S(1)}, u32[]{:S(2)}, u32[]{:S(2)}) collective-permute-start(bf16[16,2688]{1,0:T(8,128)(2,1)S(1)} %get-tuple-element.20), channel_id=1, source_target_pairs={{0,8},{1,25},{8,0},{9,17},{16,24},{17,9},{24,16},{25,1},{2,10},{3,... | collective-permute-start | bytes 258056 | tf_op jit(solution)/shard_map/ppermute | solution.py:81
  73.1 26.9 %collective-permute-start.3 = (bf16[16,2688]{1,0:T(8,128)(2,1)S(1)}, bf16[16,2688]{1,0:T(8,128)(2,1)S(1)}, u32[]{:S(2)}, u32[]{:S(2)}) collective-permute-start(bf16[16,2688]{1,0:T(8,128)(2,1)S(1)} %get-tuple-element.21), channel_id=1, source_target_pairs={{0,24},{1,9},{8,16},{9,1},{16,8},{17,25},{24,0},{25,17},{2,26},{3,... | collective-permute-start | bytes 258056 | tf_op jit(solution)/shard_map/ppermute | solution.py:81
  81.3 25.0 %collective-permute-start.2 = (bf16[16,2688]{1,0:T(8,128)(2,1)S(1)}, bf16[16,2688]{1,0:T(8,128)(2,1)S(1)}, u32[]{:S(2)}, u32[]{:S(2)}) collective-permute-start(bf16[16,2688]{1,0:T(8,128)(2,1)S(1)} %fusion.23), channel_id=1, source_target_pairs={{0,24},{1,9},{8,16},{9,1},{16,8},{17,25},{24,0},{25,17},{2,26},{3,... | collective-permute-start | bytes 258056 | tf_op jit(solution)/shard_map/ppermute | solution.py:81
  100.0 14.1 %collective-permute-start.4 = (bf16[16,2688]{1,0:T(8,128)(2,1)S(1)}, bf16[16,2688]{1,0:T(8,128)(2,1)S(1)}, u32[]{:S(2)}, u32[]{:S(2)}) collective-permute-start(bf16[16,2688]{1,0:T(8,128)(2,1)S(1)} %fusion.24), channel_id=1, source_target_pairs={{0,8},{1,25},{8,0},{9,17},{16,24},{17,9},{24,16},{25,1},{2,10},{3,... | collective-permute-start | bytes 258056 | tf_op jit(solution)/shard_map/ppermute | solution.py:81
  124.6 10.3 %collective-permute-start.5 = (bf16[128,2688]{1,0:T(8,128)(2,1)S(1)}, bf16[128,2688]{1,0:T(8,128)(2,1)S(1)}, u32[]{:S(2)}, u32[]{:S(2)}) collective-permute-start(bf16[128,2688]{1,0:T(8,128)(2,1)S(1)} %all_gather.3), channel_id=1, source_target_pairs={{0,1},{1,0},{2,3},{3,2},{4,5},{5,4},{6,7},{7,6},{8,9},{9,8},{10,11... | collective-permute-start | bytes 2064392 | tf_op jit(solution)/shard_map/ppermute | solution.py:65
  136.5 23.3 %all-to-all-start.2 = ((bf16[32,8,512]{2,1,0:T(8,128)(2,1)}), bf16[32,8,512]{2,1,0:T(8,128)(2,1)S(1)}, u32[]{:S(2)}, u32[]{:S(2)}) async-start(bf16[32,8,512]{2,1,0:T(8,128)(2,1)} %bitcast.6), calls=%async_computation.2 | async-start | bytes 524288 | tf_op jit(solution)/shard_map/all_to_all | solution.py:167
